TPU v7x, 256 devices: a whole 4x4x8 slice. The times are simulated.
256 devices in a mesh: section: 4 (over y_hi, core), vocab: 32 (over x, z), hid: 2 (over y_lo).
Axes of the slice: x: 4, y: 4 (y_hi: 2, y_lo: 2; y = y_hi * 2 + y_lo), z: 8, core: 2. Of those that a mesh axis runs over, the one named last changes fastest.
Arguments:
- tokens: bfloat16 [1024, 7168], P(('section', 'vocab'), 'hid'), may hold values from -40 to 40, as said below
- gain: bfloat16 [7168], P('hid'), may hold values from 0.5 to 1.5
- head: bfloat16 [163840, 7168], P(('section', 'vocab'), 'hid'), may hold values from -1 to 1, as said below
Outputs:
- log_probs: float32 [1024, 163840], P('hid', ('section', 'vocab'))
Inputs may be any that keep to these rules, and one draw needn't show every extreme that they name: `tokens`: hidden rows differ in scale from token to token. Rows of the head differ in scale.
All inputs are finite; a program needn't handle non-finite values.
Results may differ from a plain program's by a relative error of at most 0.00067.
Values may be sent and summed in bfloat16 or wider, within the bound.
No kernel may reach another device: no remote copies, remote signals or barrier semaphores. Data moves between devices by JAX's collectives and lax.ppermute only.
A program may use at most 64 MiB of HBM per device.

v0:
```python
import jax
import jax.numpy as jnp
from jax import lax
from jax.sharding import PartitionSpec as P

D = 7168


epsilon = 1e-06


def local(tokens, gain, head):
    scaled = (tokens.astype(jnp.float32) * gain.astype(jnp.float32)).astype(jnp.bfloat16)
    squares = jnp.sum(jnp.square(tokens.astype(jnp.float32)), axis=1)
    all_squares = lax.all_gather(squares, ("section", "vocab"), axis=0, tiled=True)
    partial_logits = lax.dot_general(
        lax.all_gather(scaled, ("section", "vocab"), axis=0, tiled=True),
        head,
        (((1,), (1,)), ((), ())),
        preferred_element_type=jnp.float32,
    )
    summed_logits, summed_squares = lax.psum((partial_logits, all_squares), "hid")
    count = partial_logits.shape[0] // lax.axis_size("hid")
    begin = lax.axis_index("hid") * count
    own_logits = lax.dynamic_slice_in_dim(summed_logits, begin, count, 0)
    own_squares = lax.dynamic_slice_in_dim(summed_squares, begin, count, 0)
    inv_rms = lax.rsqrt(own_squares / D + epsilon)
    logits = own_logits * inv_rms[:, None]
    top = lax.pmax(jnp.max(logits, axis=1), ("section", "vocab"))
    total = lax.psum(jnp.sum(jnp.exp(logits - top[:, None]), axis=1), ("section", "vocab"))
    return logits - top[:, None] - jnp.log(total)[:, None]


def solution(mesh):
    return jax.shard_map(
        local,
        mesh=mesh,
        in_specs=(P(("section", "vocab"), "hid"), P("hid"), P(("section", "vocab"), "hid")),
        out_specs=P("hid", ("section", "vocab")),
        check_vma=False,
    )
```

profile of v0, /device:TPU:8, one launch (start us, length us, event | category | flops | bytes accessed | tf_op | source)
XLA Modules:
  0.0 1157.1 jit_solution(3293950355630215478)
XLA Ops:
  6.5 0.0 all-gather.2.cloned.1.call-start
  6.5 0.7 convert_element_type.11
  7.2 1.6 fusion.2
  8.8 0.0 all-gather.2.cloned.1.call-update
  8.8 0.0 all-reduce.3.cloned.1.call-start
  8.9 130.5 %all-gather.2.cloned.1.call-done = bf16[1024,3584]{1,0:T(8,128)(2,1)} async-done(((bf16[8,3584]{1,0:T(8,128)(2,1)}), bf16[1024,3584]{1,0:T(8,128)(2,1)}) %all-gather.2.cloned.1.call-update) | async-done | bytes 7340048 | tf_op jit(solution)/shard_map/all_gather | solution.py:17
  139.3 16.1 %fusion.3 = f32[1024,1280]{1,0:T(8,128)} fusion(bf16[1024,3584]{1,0:T(8,128)(2,1)} %all-gather.2.cloned.1.call-done, bf16[1280,3584]{1,0:T(8,128)(2,1)} %param.5), kind=kOutput, calls=%fused_computation.9 | convolution fusion | flops 9395240960 | bytes 21757952 | tf_op jit(solution)/shard_map/dot_general | solution.py:16
  155.4 0.0 copy-start
  155.4 0.0 all-reduce.3.cloned.1.call-update
  155.4 0.6 copy-done
  156.1 0.6 dynamic-slice
  157.3 0.2 dynamic-update-slice
  157.6 330.0 %all-reduce = f32[1024]{0:T(1024)S(1)} all-reduce(f32[1024]{0:T(1024)S(1)} %dynamic-update-slice), channel_id=1, replica_groups=mesh['section'=4,'vocab'=32,'hid'=2] {'section','vocab'}, use_global_device_ids=true, to_apply=%add | all-reduce | flops 1024 | bytes 8192
  487.5 4.9 psum.22
  492.5 0.1 add_rsqrt_fusion
  492.6 0.0 all-reduce.3.cloned.1.call-done
  492.6 2.1 fusion
  494.6 323.7 %pmax.7 = f32[512]{0:T(512)S(1)} all-reduce(f32[512]{0:T(512)S(1)} %fusion), channel_id=1, replica_groups=mesh['section'=4,'vocab'=32,'hid'=2] {'section','vocab'}, use_global_device_ids=true, to_apply=%region_4.0 | all-reduce | flops 512 | bytes 4096 | tf_op jit(solution)/shard_map/pmax | solution.py:29
  818.4 2.3 exponential_reduce_fusion
  820.7 326.0 %psum.23 = f32[512]{0:T(512)S(1)} all-reduce(f32[512]{0:T(512)S(1)} %exponential_reduce_fusion), channel_id=1, replica_groups=mesh['section'=4,'vocab'=32,'hid'=2] {'section','vocab'}, use_global_device_ids=true, to_apply=%region_6.0 | all-reduce | flops 512 | bytes 4096 | tf_op jit(solution)/shard_map/psum | solution.py:30
  1146.7 3.6 subtract_subtract_fusion
  (2 shorter events, 0.0 us)
Async XLA Ops:
  6.5 132.8 %all-gather.2.cloned.1.call-start = ((), (), s32[]{:S(2)}) async-start(), calls=%async_computation | async-start | bytes 7397376 | tf_op jit(solution)/shard_map/all_gather | solution.py:17
  8.8 483.7 %all-reduce.3.cloned.1.call-start = ((), (), s32[]{:S(2)}) async-start(), calls=%async_computation.1 | async-start | bytes 10485760 | tf_op jit(solution)/shard_map/psum | solution.py:22
  155.4 0.7 copy-start
Sparse Core Ops, SparseCore 0:
  11.1 128.1 all-gather.1
  155.5 138.8 all-reduce.2
where the time goes:
time: 1160 us
  blocking collectives  985 us (85%)
  waiting for transfers between devices  130 us (11%)
  matrix products  16.1 us (1%)
  between operations  14.1 us (1%)
    unnamed x1, blocking collectives  330 us
    psum x1, blocking collectives, local(): lax.psum(jnp.sum(jnp.exp(logits - top[:, None]), axis=1), ('section', 'vo...  326 us
    pmax x1, blocking collectives, local(): top = lax.pmax(jnp.max(logits, axis=1), ('section', 'vocab'))  324 us
    all_gather x1, waiting for transfers between devices, local(): lax.all_gather(scaled, ('section', 'vocab'), axis=0, tiled=True)  130 us
  transfers between devices with their start and end apart: 2, of which 1 were waited for; matrix products, arithmetic and copies ran while one was open for 0% of the time, Pallas kernels for 0%

commit v1 on v0

v1 whole, which is shorter than its diff:
```python
import itertools

import jax
import jax.numpy as jnp
from jax import lax
from jax.sharding import Mesh
from jax.sharding import PartitionSpec as P

D = 7168
epsilon = 1e-06
AXES = ("yh", "core", "x", "z", "h")
NY, NC, NX, NZ, NH = SIZES = (2, 2, 4, 8, 2)
SCALE = 0.125


def send(value, target):
    pairs = []
    for i, at in enumerate(itertools.product(*[range(n) for n in SIZES])):
        j = 0
        for a, n in zip(target(*at), SIZES):
            j = j * n + a % n
        pairs.append((i, j))
    return lax.ppermute(value, AXES, pairs)


def to_core(value):
    return send(value, lambda y, c, x, z, h: (y, c + 1, x, z, h))


def to_hid(value):
    return send(value, lambda y, c, x, z, h: (y, c, x, z, h + 1))


def along_z(value):
    return send(value, lambda y, c, x, z, h: (y, c, x, z + (1 if c == 0 else -1), h))


def split3(value):
    parts = []
    for _ in range(3):
        part = lax.reduce_precision(value, 8, 7)
        parts.append(part.astype(jnp.bfloat16))
        value = value - part
    return parts


def local(tokens, gain, head):
    yh, core, x, z, h = (lax.axis_index(a) for a in AXES)
    width = tokens.shape[1]
    f32 = tokens.astype(jnp.float32)
    scaled = (f32 * gain.astype(jnp.float32)).astype(jnp.bfloat16)
    squares = jnp.sum(jnp.square(f32), axis=1)
    pieces = jnp.stack(split3(squares), axis=1)
    own = jnp.concatenate([scaled, jnp.pad(pieces, ((0, 0), (0, 125)))], axis=1)
    other = send(own, lambda y, c, x, z, h: (y + 1, c, x, z, h))
    both = jnp.where(yh == h, jnp.concatenate([other, own]), jnp.concatenate([own, other]))
    column = lax.all_to_all(jnp.broadcast_to(both[None], (NX,) + both.shape), "x", 0, 0, tiled=True)
    swapped = to_core(column)
    cols = both.shape[1]

    def halves(first, second):
        return jnp.where(core == 0, first, second)

    plane = jnp.stack([halves(column, swapped), halves(swapped, column)])
    plane = plane.reshape(NC, NX, 2, 8, cols).transpose(2, 0, 1, 3, 4).reshape(128, cols)

    keep = jnp.zeros((NC, NX, NZ, 8, 1280), jnp.float32)
    keep_squares = jnp.zeros((NC, NX, NZ, 8), jnp.float32)
    got = jnp.zeros((NC, NX, NZ, 8, 1280), jnp.float16)
    aside = jnp.zeros((2, NC, NX, NZ, 8), jnp.float32)

    def squares_of(rows):
        return jnp.sum(rows[:, width : width + 3].astype(jnp.float32), axis=1)

    def product(rows):
        return lax.dot_general(rows[:, :width], head, (((1,), (1,)), ((), ())), preferred_element_type=jnp.float32)

    def put(into, value, at, lead=()):
        value = value.reshape(lead + (NC, NX, 1, 8) + value.shape[1 + len(lead) :])
        zero = jnp.int32(0)
        begin = [zero] * into.ndim
        begin[len(lead) + 2] = at
        return lax.dynamic_update_slice(into, value, begin)

    def work(chunk_s, chunk_k, places, state):
        keep, keep_squares, got, aside = state
        n = chunk_s.shape[0]
        partial = product(jnp.concatenate([chunk_s, chunk_k]))
        outward, stay = partial[:n], partial[n:]
        centre = jnp.mean(outward, axis=1)
        moved = to_hid(((outward - centre[:, None]) * SCALE).astype(jnp.float16))
        extra = jnp.stack([squares_of(chunk_s), centre])
        stay_squares = squares_of(chunk_k)
        for i, at in enumerate(places):
            part = slice(64 * i, 64 * i + 64)
            keep = put(keep, stay[part], at)
            keep_squares = put(keep_squares, stay_squares[part], at)
            got = put(got, moved[part], at)
            aside = put(aside, extra[:, part], at, (2,))
        return keep, keep_squares, got, aside

    state = (keep, keep_squares, got, aside)
    state = work(plane[:64], plane[64:], [z], state)
    block = plane
    for step in range(1, 4):
        block = along_z(block)
        second = to_core(block)
        away = jnp.where(core == 0, -step, step)
        places = [(z + away) % NZ, (z - away) % NZ]
        state = work(
            jnp.concatenate([block[:64], second[:64]]), jnp.concatenate([block[64:], second[64:]]), places, state
        )
    half = along_z(lax.dynamic_slice_in_dim(block, core * 64, 64))
    rest = to_core(half)
    keep, keep_squares, got, aside = work(halves(half, rest), halves(rest, half), [(z + 4) % NZ], state)

    aside = to_hid(aside)
    inv_rms = lax.rsqrt((keep_squares + aside[0]).reshape(512) / D + epsilon)
    raw = keep.reshape(512, 1280) + (got.reshape(512, 1280).astype(jnp.float32) / SCALE + aside[1].reshape(512, 1))
    logits = raw * inv_rms[:, None]
    top = jnp.max(logits, axis=1)
    total = jnp.sum(jnp.exp(logits - top[:, None]), axis=1)

    def merge(tops, totals):
        best = jnp.max(tops, axis=0)
        return best, jnp.sum(totals * jnp.exp(tops - best), axis=0)

    for axis in (0, 1):
        pair = jnp.stack([top, total])
        back = send(pair, lambda y, c, x, z, h: (y + 1 - axis, c + axis, x, z, h))
        top, total = merge(jnp.stack([top, back[0]]), jnp.stack([total, back[1]]))
    pair = jnp.stack([top, total])
    every = lax.all_to_all(jnp.broadcast_to(pair[None], (NX * NZ, 2, 512)), ("x", "z"), 0, 0, tiled=True)
    top, total = merge(every[:, 0], every[:, 1])
    return logits - top[:, None] - jnp.log(total)[:, None]


def solution(mesh):
    fine = Mesh(mesh.devices.reshape(SIZES), AXES)
    rows = ("yh", "core", "x", "z")
    return jax.shard_map(
        local,
        mesh=fine,
        in_specs=(P(rows, "h"), P("h"), P(rows, "h")),
        out_specs=P("h", rows),
        check_vma=False,
    )
```

time: 1160 us -> 165 us (0.14)
  blocking collectives: 985 us -> 11.9 us
  waiting for transfers between devices: 130 us -> 47.2 us
  local copies, waits for them, and re-layouts: 1.49 us -> 39.1 us
  starting transfers between devices: 0.04 us -> 18.6 us
  between operations: 14.1 us -> 0.49 us
  matrix products: 16.1 us -> 28.2 us
    psum x2 -> x0, blocking collectives: 331 us -> none  [the longest x1 326 us: local(): lax.psum(jnp.sum(jnp.exp(logits - top[:, None]), axis=1), ('section', 'vo...]
    unnamed x1 -> x0, blocking collectives: 330 us -> none
    pmax x1 -> x0, blocking collectives: 324 us -> none  [local(): top = lax.pmax(jnp.max(logits, axis=1), ('section', 'vocab'))]
    all_gather x1 -> x0, waiting for transfers between devices: 130 us -> none  [local(): lax.all_gather(scaled, ('section', 'vocab'), axis=0, tiled=True)]
    ppermute x0 -> x18, waiting for transfers between devices: none -> 36.8 us  [send(): return lax.ppermute(value, AXES, pairs)]
    dynamic_update_slice x0 -> x32, local copies, waits for them, and re-layouts: none -> 19.2 us  [put(): return lax.dynamic_update_slice(into, value, begin)]
    dot_general x1 -> x5, matrix products: 16.1 us -> 28.2 us  [product(): lax.dot_general(rows[:, :width], head, (((1,), (1,)), ((), ())), preferre...]
    all_to_all x0 -> x1, blocking collectives: none -> 11.9 us  [local(): lax.all_to_all(jnp.broadcast_to(both[None], (NX,) + both.shape), 'x', 0,...]
  transfers between devices with their start and end apart: 2 -> 19, of which waited for: 1 -> 12; matrix products, arithmetic and copies ran while one was open for 0% -> 34% of each run, Pallas kernels for 0% -> 0%
where the time goes in v1:
time: 165 us; the launch traced here: 164 us
  waiting for transfers between devices  47.2 us (29%)
  local copies, waits for them, and re-layouts  39.1 us (24%)
  matrix products  28.2 us (17%)
  starting transfers between devices  18.6 us (11%)
  other arithmetic  18.5 us (11%)
  blocking collectives  11.9 us (7%)
    ppermute x18, waiting for transfers between devices, send(): return lax.ppermute(value, AXES, pairs)  36.8 us
    dot_general x5, matrix products, product(): lax.dot_general(rows[:, :width], head, (((1,), (1,)), ((), ())), preferre...  28.2 us
    dynamic_update_slice x32, local copies, waits for them, and re-layouts, put(): return lax.dynamic_update_slice(into, value, begin)  19.2 us
    all_to_all x1, blocking collectives, local(): lax.all_to_all(jnp.broadcast_to(both[None], (NX,) + both.shape), 'x', 0,...  11.9 us
    ppermute x18, starting transfers between devices, send(): return lax.ppermute(value, AXES, pairs)  11.7 us
    all_to_all x1, waiting for transfers between devices, local(): lax.all_to_all(jnp.broadcast_to(pair[None], (NX * NZ, 2, 512)), ('x', 'z'...  10.5 us
    all_to_all x1, starting transfers between devices, local(): lax.all_to_all(jnp.broadcast_to(pair[None], (NX * NZ, 2, 512)), ('x', 'z'...  6.84 us
    sub x1, other arithmetic, local(): return logits - top[:, None] - jnp.log(total)[:, None]  3.77 us
  transfers between devices with their start and end apart: 19, of which 12 were waited for; matrix products, arithmetic and copies ran while one was open for 34% of the time, Pallas kernels for 0%

profile of v1, /device:TPU:8, one launch (start us, length us, event | category | flops | bytes accessed | tf_op | source)
XLA Modules:
  0.0 164.0 jit_solution(10246509883912983536)
XLA Ops:
  0.0 0.7 convert_element_type.93
  0.7 1.0 fusion.15
  1.8 2.4 %collective-permute-start = (bf16[8,3712]{1,0:T(8,128)(2,1)S(1)}, bf16[8,3712]{1,0:T(8,128)(2,1)S(1)}, u32[]{:S(2)}, u32[]{:S(2)}) collective-permute-start(bf16[8,3712]{1,0:T(8,128)(2,1)S(1)} %pad_maximum_fusion.22), channel_id=1, source_target_pairs={{0,128},{1,129},{2,130},{3,131},{4,132},{5,133},{6,134},{7,135},{8... | collective-permute-start | bytes 178184 | tf_op jit(solution)/shard_map/ppermute | solution.py:23
  4.2 3.4 %collective-permute-done = bf16[8,3712]{1,0:T(8,128)(2,1)S(1)} collective-permute-done((bf16[8,3712]{1,0:T(8,128)(2,1)S(1)}, bf16[8,3712]{1,0:T(8,128)(2,1)S(1)}, u32[]{:S(2)}, u32[]{:S(2)}) %collective-permute-start) | collective-permute-done | bytes 59424 | tf_op jit(solution)/shard_map/ppermute | solution.py:23
  7.7 11.9 %all_to_all.10 = bf16[4,16,3712]{2,1,0:T(8,128)(2,1)S(1)} all-to-all(bf16[4,16,3712]{2,1,0:T(8,128)(2,1)S(1)} %broadcast_in_dim.13), channel_id=1, replica_groups=mesh['yh'=2,'core'=2,'x'=4,'z'=8,'h'=2] {'x'}, dimensions={0} | all-to-all | bytes 950272 | tf_op jit(solution)/shard_map/all_to_all | solution.py:57
  19.6 1.8 %collective-permute-done.1 = bf16[4,16,3712]{2,1,0:T(8,128)(2,1)S(1)} collective-permute-done((bf16[4,16,3712]{2,1,0:T(8,128)(2,1)S(1)}, bf16[4,16,3712]{2,1,0:T(8,128)(2,1)S(1)}, u32[]{:S(2)}, u32[]{:S(2)}) %collective-permute-start.1) | collective-permute-done | bytes 475168 | tf_op jit(solution)/shard_map/ppermute | solution.py:23
  21.6 1.0 copy.134
  22.7 6.6 %fusion.12 = f32[128,1280]{1,0:T(8,128)S(1)} fusion(bf16[1280,3584]{1,0:T(8,128)(2,1)} %param.5, bf16[64,3712]{1,0:T(8,128)(2,1)S(1)} %bitcast.144, bf16[64,3712]{1,0:T(8,128)(2,1)S(1)} %bitcast.146), kind=kOutput, calls=%fused_computation.28 | convolution fusion | flops 1176240128 | bytes 10780672 | tf_op jit(solution)/shard_map/dot_general | solution.py:76
  29.4 2.0 %collective-permute-start.2 = (bf16[128,3712]{1,0:T(8,128)(2,1)}, bf16[128,3712]{1,0:T(8,128)(2,1)}, u32[]{:S(2)}, u32[]{:S(2)}) collective-permute-start(bf16[128,3712]{1,0:T(8,128)(2,1)} %bitcast.8), channel_id=1, source_target_pairs={{0,2},{1,3},{2,4},{3,5},{4,6},{5,7},{6,8},{7,9},{8,10},{9,11},{10,... | collective-permute-start | bytes 2850824 | tf_op jit(solution)/shard_map/ppermute | solution.py:23
  33.2 1.5 dynamic_update_slice.112
  34.9 12.4 %collective-permute-done.2 = bf16[128,3712]{1,0:T(8,128)(2,1)} collective-permute-done((bf16[128,3712]{1,0:T(8,128)(2,1)}, bf16[128,3712]{1,0:T(8,128)(2,1)}, u32[]{:S(2)}, u32[]{:S(2)}) %collective-permute-start.2) | collective-permute-done | bytes 950304 | tf_op jit(solution)/shard_map/ppermute | solution.py:23
  47.4 1.2 broadcast_in_dim.14
  48.5 0.7 constant_dynamic-update-slice_fusion.7
  49.2 1.2 fusion.49
  50.7 6.2 %fusion.8 = f32[256,1280]{1,0:T(8,128)S(1)} fusion(bf16[1280,3584]{1,0:T(8,128)(2,1)} %param.5, bf16[64,3712]{1,0:T(8,128)(2,1)S(1)} %get-tuple-element.27, bf16[64,3712]{1,0:T(8,128)(2,1)S(1)} %get-tuple-element.25, bf16[64,3712]{1,0:T(8,128)(2,1)S(1)} %get-tuple-element.26, bf16[64,3712]{1,0:T(8,128)(2,1)S(1)} %get-tuple-element.24), kind=kOutput, calls=%fused_computation.19 | convolution fusion | flops 2356150272 | bytes 12386304 | tf_op jit(solution)/shard_map/dot_general | solution.py:76
  57.8 6.7 %collective-permute-done.4 = bf16[128,3712]{1,0:T(8,128)(2,1)} collective-permute-done((bf16[128,3712]{1,0:T(8,128)(2,1)}, bf16[128,3712]{1,0:T(8,128)(2,1)}, u32[]{:S(2)}, u32[]{:S(2)}) %collective-permute-start.4) | collective-permute-done | bytes 950304 | tf_op jit(solution)/shard_map/ppermute | solution.py:23
  64.5 2.0 %fusion.47 = (bf16[64,3712]{1,0:T(8,128)(2,1)S(1)}, bf16[64,3712]{1,0:T(8,128)(2,1)}) fusion(bf16[128,3712]{1,0:T(8,128)(2,1)} %collective-permute-done.4), kind=kLoop, calls=%fused_computation.140 | loop fusion | bytes 1900544 | tf_op jit(solution)/shard_map/slice | solution.py:111
  67.1 1.5 dynamic_update_slice.113
  68.6 1.5 dynamic_update_slice.114
  70.1 1.1 fusion.56
  71.2 0.7 constant_dynamic-update-slice_fusion.6
  71.9 0.7 constant_dynamic-update-slice_fusion.5
  72.6 1.2 fusion.48
  73.9 6.2 %fusion.6 = f32[256,1280]{1,0:T(8,128)S(1)} fusion(bf16[1280,3584]{1,0:T(8,128)(2,1)} %param.5, bf16[64,3712]{1,0:T(8,128)(2,1)S(1)} %get-tuple-element.23, bf16[64,3712]{1,0:T(8,128)(2,1)S(1)} %copy-done.3, bf16[64,3712]{1,0:T(8,128)(2,1)S(1)} %get-tuple-element.22, bf16[64,3712]{1,0:T(8,128)(2,1)S(1)} %get-tuple-element.20), kind=kOutput, calls=%fused_computation.14 | convolution fusion | flops 2356150272 | bytes 12386304 | tf_op jit(solution)/shard_map/dot_general | solution.py:76
  80.1 1.0 copy-done.1
  81.5 1.2 multiply_convert_fusion.1
  83.3 1.1 fusion.44
  84.4 1.0 collective-permute-done.6
  85.3 2.4 %constant_dynamic-slice_fusion = (bf16[64,3712]{1,0:T(8,128)(2,1)}, bf16[64,3712]{1,0:T(8,128)(2,1)S(1)}, bf16[64,3712]{1,0:T(8,128)(2,1)}) fusion(bf16[128,3712]{1,0:T(8,128)(2,1)} %collective-permute-done.6, s32[]{:T(128)S(6)} %select_n.150), kind=kLoop, calls=%fused_computation.88 | loop fusion | bytes 2850820 | tf_op jit(solution)/shard_map/dynamic_slice | solution.py:113
  88.8 1.5 dynamic_update_slice.115
  90.3 1.5 dynamic_update_slice.116
  91.7 1.6 collective-permute-done.12
  93.3 1.1 fusion.55
  94.4 0.7 constant_dynamic-update-slice_fusion.4
  95.1 0.7 constant_dynamic-update-slice_fusion.3
  95.8 2.1 %collective-permute-done.8 = bf16[64,3712]{1,0:T(8,128)(2,1)} collective-permute-done((bf16[64,3712]{1,0:T(8,128)(2,1)}, bf16[64,3712]{1,0:T(8,128)(2,1)}, u32[]{:S(2)}, u32[]{:S(2)}) %collective-permute-start.8) | collective-permute-done | bytes 475168 | tf_op jit(solution)/shard_map/ppermute | solution.py:23
  97.9 1.2 fusion.46
  99.3 6.3 %fusion.4 = f32[256,1280]{1,0:T(8,128)S(1)} fusion(bf16[1280,3584]{1,0:T(8,128)(2,1)} %param.5, bf16[64,3712]{1,0:T(8,128)(2,1)S(1)} %get-tuple-element.19, bf16[64,3712]{1,0:T(8,128)(2,1)S(1)} %get-tuple-element.16, bf16[64,3712]{1,0:T(8,128)(2,1)S(1)} %get-tuple-element.18, bf16[64,3712]{1,0:T(8,128)(2,1)S(1)} %copy-done.2), kind=kOutput, calls=%fused_computation.9 | convolution fusion | flops 2356150272 | bytes 12386304 | tf_op jit(solution)/shard_map/dot_general | solution.py:76
  105.8 1.4 broadcast_select_fusion.1
  107.3 3.0 %fusion.10 = f32[128,1280]{1,0:T(8,128)S(1)} fusion(bf16[1280,3584]{1,0:T(8,128)(2,1)S(1)} %bitcast.143, bf16[64,3712]{1,0:T(8,128)(2,1)S(1)} %get-tuple-element.14, bf16[64,3712]{1,0:T(8,128)(2,1)S(1)} %get-tuple-element.13), kind=kOutput, calls=%fused_computation.25 | convolution fusion | flops 1176240128 | bytes 10780672 | tf_op jit(solution)/shard_map/dot_general | solution.py:76
  110.5 0.8 fusion.52
  111.6 2.0 %multiply_convert_fusion = f16[128,1280]{1,0:T(8,128)(2,1)} fusion(f32[256,1280]{1,0:T(8,128)} %copy-done, f32[128]{0:T(128)S(1)} %get-tuple-element.62), kind=kLoop, calls=%fused_computation.31 | loop fusion | flops 491520 | bytes 983552 | tf_op jit(solution)/shard_map/convert_element_type | solution.py:91
  113.6 0.6 collective-permute-start.13
  114.3 1.5 dynamic_update_slice.117
  115.8 1.5 dynamic_update_slice.118
  117.3 1.5 dynamic_update_slice.119
  118.8 1.4 collective-permute-start.15
  120.2 0.6 collective-permute-start.14
  120.9 1.0 constant_dynamic-update-slice_fusion.8
  122.6 3.2 %collective-permute-done.15 = f32[2,2,4,8,8]{4,3,2,1,0:T(8,128)S(1)} collective-permute-done((f32[2,2,4,8,8]{4,3,2,1,0:T(8,128)}, f32[2,2,4,8,8]{4,3,2,1,0:T(8,128)S(1)}, u32[]{:S(2)}, u32[]{:S(2)}) %collective-permute-start.15) | collective-permute-done | bytes 4128 | tf_op jit(solution)/shard_map/ppermute | solution.py:23
  125.8 1.1 fusion.54
  126.8 0.7 constant_dynamic-update-slice_fusion.2
  127.5 0.7 constant_dynamic-update-slice_fusion.1
  128.2 0.6 collective-permute-done.14
  128.8 0.7 constant_dynamic-update-slice_fusion
  129.5 1.9 %fusion.14 = f32[2,4,8,8]{3,2,1,0:T(8,128)S(1)} fusion(f32[2,4,8,8]{3,2,1,0:T(8,128)S(1)} %fusion.24, f32[2,4,8,8,1280]{4,3,2,1,0:T(8,128)S(1)} %constant_dynamic-update-slice_fusion.8, f32[2,4,8,8]{3,2,1,0:T(8,128)S(1)} %get-tuple-element.46, f16[2,4,8,8,1280]{4,3,2,1,0:T(8,128)(2,1)} %constant_dynamic-update-slice_fusion), kind=kLoop, calls=%fused_computation.30 | loop fusion | flops 3931648 | bytes 3938304 | tf_op jit(solution)/shard_map/reduce_max | solution.py:121
  131.6 3.6 %exponential_reduce_fusion = (f32[2,4,8,8]{3,2,1,0:T(8,128)S(1)}, f32[2,4,8,8,1280]{4,3,2,1,0:T(8,128)}) fusion(f32[2,4,8,8]{3,2,1,0:T(8,128)S(1)} %fusion.14, f32[2,4,8,8]{3,2,1,0:T(8,128)S(1)} %fusion.24, f32[2,4,8,8,1280]{4,3,2,1,0:T(8,128)S(1)} %constant_dynamic-update-slice_fusion.8, f32[2,4,8,8]{3,2,1,0:T(8,128)S(1)} %get-tuple-element.46, ...), kind=kLoop, calls=%fused_computation.5 | loop fusion | flops 4587008 | bytes 6561792 | tf_op jit(solution)/shard_map/reduce_sum | solution.py:122
  135.3 2.4 %collective-permute-start.16 = (f32[2,512]{1,0:T(2,128)S(1)}, f32[2,512]{1,0:T(2,128)S(1)}, u32[]{:S(2)}, u32[]{:S(2)}) collective-permute-start(f32[2,512]{1,0:T(2,128)S(1)} %pad_maximum_fusion.32), channel_id=1, source_target_pairs={{0,128},{1,129},{2,130},{3,131},{4,132},{5,133},{6,134},{7,135},{8... | collective-permute-start | bytes 12296 | tf_op jit(solution)/shard_map/ppermute | solution.py:23
  137.7 2.8 %collective-permute-done.16 = f32[2,512]{1,0:T(2,128)S(1)} collective-permute-done((f32[2,512]{1,0:T(2,128)S(1)}, f32[2,512]{1,0:T(2,128)S(1)}, u32[]{:S(2)}, u32[]{:S(2)}) %collective-permute-start.16) | collective-permute-done | bytes 4128 | tf_op jit(solution)/shard_map/ppermute | solution.py:23
  140.7 1.2 collective-permute-done.17
  141.9 0.7 broadcast_in_dim.17
  142.6 6.8 %all-to-all-start.1 = ((f32[32,2,512]{2,1,0:T(2,128)}), f32[32,2,512]{2,1,0:T(2,128)S(1)}, u32[]{:S(2)}, u32[]{:S(2)}) async-start(f32[32,2,512]{2,1,0:T(2,128)} %broadcast_in_dim.17), calls=%async_computation.1 | async-start | bytes 262144 | tf_op jit(solution)/shard_map/all_to_all | solution.py:133
  149.6 10.5 %all-to-all-done.1 = f32[32,2,512]{2,1,0:T(2,128)S(1)} async-done(((f32[32,2,512]{2,1,0:T(2,128)}), f32[32,2,512]{2,1,0:T(2,128)S(1)}, u32[]{:S(2)}, u32[]{:S(2)}) %all-to-all-start.1) | async-done | bytes 131104 | tf_op jit(solution)/shard_map/all_to_all | solution.py:133
  160.2 3.8 %fusion.3 = f32[512,1280]{1,0:T(8,128)} fusion(f32[2,4,8,8,1280]{4,3,2,1,0:T(8,128)} %get-tuple-element.6, f32[2,4,8,8,1280]{4,3,2,1,0:T(8,128)S(1)} %constant_dynamic-update-slice_fusion.8, f32[512]{0:T(512)S(1)} %log.7, f32[512]{0:T(512)S(1)} %get-tuple-element.42, f32[512]{0:T(512)S(1)} %rsqrt.12, f32[512]{0:T(512)S(1)} %add.147), kind=kLoop, calls=%fused_computation.4 | loop fusion | flops 3276800 | bytes 7872512 | tf_op jit(solution)/shard_map/sub | solution.py:135
  (127 shorter events, 8.7 us)
Async XLA Ops:
  1.8 5.8 %collective-permute-start = (bf16[8,3712]{1,0:T(8,128)(2,1)S(1)}, bf16[8,3712]{1,0:T(8,128)(2,1)S(1)}, u32[]{:S(2)}, u32[]{:S(2)}) collective-permute-start(bf16[8,3712]{1,0:T(8,128)(2,1)S(1)} %pad_maximum_fusion.22), channel_id=1, source_target_pairs={{0,128},{1,129},{2,130},{3,131},{4,132},{5,133},{6,134},{7,135},{8... | collective-permute-start | bytes 178184 | tf_op jit(solution)/shard_map/ppermute | solution.py:23
  19.6 1.8 %collective-permute-start.1 = (bf16[4,16,3712]{2,1,0:T(8,128)(2,1)S(1)}, bf16[4,16,3712]{2,1,0:T(8,128)(2,1)S(1)}, u32[]{:S(2)}, u32[]{:S(2)}) collective-permute-start(bf16[4,16,3712]{2,1,0:T(8,128)(2,1)S(1)} %all_to_all.10), channel_id=1, source_target_pairs={{0,64},{1,65},{2,66},{3,67},{4,68},{5,69},{6,70},{7,71},{8,72},{9,... | collective-permute-start | bytes 1425416 | tf_op jit(solution)/shard_map/ppermute | solution.py:23
  29.4 18.0 %collective-permute-start.2 = (bf16[128,3712]{1,0:T(8,128)(2,1)}, bf16[128,3712]{1,0:T(8,128)(2,1)}, u32[]{:S(2)}, u32[]{:S(2)}) collective-permute-start(bf16[128,3712]{1,0:T(8,128)(2,1)} %bitcast.8), channel_id=1, source_target_pairs={{0,2},{1,3},{2,4},{3,5},{4,6},{5,7},{6,8},{7,9},{8,10},{9,11},{10,... | collective-permute-start | bytes 2850824 | tf_op jit(solution)/shard_map/ppermute | solution.py:23
  32.0 15.4 %collective-permute-start.10 = (f16[64,1280]{1,0:T(8,128)(2,1)S(1)}, f16[64,1280]{1,0:T(8,128)(2,1)S(1)}, u32[]{:S(2)}, u32[]{:S(2)}) collective-permute-start(f16[64,1280]{1,0:T(8,128)(2,1)S(1)} %get-tuple-element.35), channel_id=1, source_target_pairs={{0,1},{1,0},{2,3},{3,2},{4,5},{5,4},{6,7},{7,6},{8,9},{9,8},{10,11... | collective-permute-start | bytes 491528 | tf_op jit(solution)/shard_map/ppermute | solution.py:23
  47.4 3.1 %collective-permute-start.3 = (bf16[128,3712]{1,0:T(8,128)(2,1)}, bf16[128,3712]{1,0:T(8,128)(2,1)S(1)}, u32[]{:S(2)}, u32[]{:S(2)}) collective-permute-start(bf16[128,3712]{1,0:T(8,128)(2,1)} %collective-permute-done.2), channel_id=1, source_target_pairs={{0,64},{1,65},{2,66},{3,67},{4,68},{5,69},{6,70},{7,71},{8,72},{9,... | collective-permute-start | bytes 2850824 | tf_op jit(solution)/shard_map/ppermute | solution.py:23
  49.2 15.3 %collective-permute-start.4 = (bf16[128,3712]{1,0:T(8,128)(2,1)}, bf16[128,3712]{1,0:T(8,128)(2,1)}, u32[]{:S(2)}, u32[]{:S(2)}) collective-permute-start(bf16[128,3712]{1,0:T(8,128)(2,1)} %collective-permute-done.2), channel_id=1, source_target_pairs={{0,2},{1,3},{2,4},{3,5},{4,6},{5,7},{6,8},{7,9},{8,10},{9,11},{10,... | collective-permute-start | bytes 2850824 | tf_op jit(solution)/shard_map/ppermute | solution.py:23
  57.1 13.0 %collective-permute-start.11 = (f16[128,1280]{1,0:T(8,128)(2,1)S(1)}, f16[128,1280]{1,0:T(8,128)(2,1)}, u32[]{:S(2)}, u32[]{:S(2)}) collective-permute-start(f16[128,1280]{1,0:T(8,128)(2,1)S(1)} %multiply_convert_fusion.2), channel_id=1, source_target_pairs={{0,1},{1,0},{2,3},{3,2},{4,5},{5,4},{6,7},{7,6},{8,9},{9,8},{10,11... | collective-permute-start | bytes 983048 | tf_op jit(solution)/shard_map/ppermute | solution.py:23
  66.6 6.0 %collective-permute-start.5 = (bf16[128,3712]{1,0:T(8,128)(2,1)}, bf16[128,3712]{1,0:T(8,128)(2,1)}, u32[]{:S(2)}, u32[]{:S(2)}) collective-permute-start(bf16[128,3712]{1,0:T(8,128)(2,1)} %collective-permute-done.4), channel_id=1, source_target_pairs={{0,64},{1,65},{2,66},{3,67},{4,68},{5,69},{6,70},{7,71},{8,72},{9,... | collective-permute-start | bytes 2850824 | tf_op jit(solution)/shard_map/ppermute | solution.py:23
  70.1 3.8 %copy-start.3 = (bf16[64,3712]{1,0:T(8,128)(2,1)S(1)}, bf16[64,3712]{1,0:T(8,128)(2,1)}, u32[]{:S(2)}) copy-start(bf16[64,3712]{1,0:T(8,128)(2,1)} %get-tuple-element.21) | copy-start | bytes 1425412
  70.1 15.3 %collective-permute-start.6 = (bf16[128,3712]{1,0:T(8,128)(2,1)}, bf16[128,3712]{1,0:T(8,128)(2,1)}, u32[]{:S(2)}, u32[]{:S(2)}) collective-permute-start(bf16[128,3712]{1,0:T(8,128)(2,1)} %collective-permute-done.4), channel_id=1, source_target_pairs={{0,2},{1,3},{2,4},{3,5},{4,6},{5,7},{6,8},{7,9},{8,10},{9,11},{10,... | collective-permute-start | bytes 2850824 | tf_op jit(solution)/shard_map/ppermute | solution.py:23
  80.1 1.1 copy-start.1
  82.7 10.6 %collective-permute-start.12 = (f16[128,1280]{1,0:T(8,128)(2,1)S(1)}, f16[128,1280]{1,0:T(8,128)(2,1)}, u32[]{:S(2)}, u32[]{:S(2)}) collective-permute-start(f16[128,1280]{1,0:T(8,128)(2,1)S(1)} %multiply_convert_fusion.1), channel_id=1, source_target_pairs={{0,1},{1,0},{2,3},{3,2},{4,5},{5,4},{6,7},{7,6},{8,9},{9,8},{10,11... | collective-permute-start | bytes 983048 | tf_op jit(solution)/shard_map/ppermute | solution.py:23
  87.7 10.2 %collective-permute-start.8 = (bf16[64,3712]{1,0:T(8,128)(2,1)}, bf16[64,3712]{1,0:T(8,128)(2,1)}, u32[]{:S(2)}, u32[]{:S(2)}) collective-permute-start(bf16[64,3712]{1,0:T(8,128)(2,1)} %get-tuple-element.15), channel_id=1, source_target_pairs={{0,2},{1,3},{2,4},{3,5},{4,6},{5,7},{6,8},{7,9},{8,10},{9,11},{10,... | collective-permute-start | bytes 1425416 | tf_op jit(solution)/shard_map/ppermute | solution.py:23
  87.8 10.1 %collective-permute-start.7 = (bf16[128,3712]{1,0:T(8,128)(2,1)}, bf16[128,3712]{1,0:T(8,128)(2,1)}, u32[]{:S(2)}, u32[]{:S(2)}) collective-permute-start(bf16[128,3712]{1,0:T(8,128)(2,1)} %collective-permute-done.6), channel_id=1, source_target_pairs={{0,64},{1,65},{2,66},{3,67},{4,68},{5,69},{6,70},{7,71},{8,72},{9,... | collective-permute-start | bytes 2850824 | tf_op jit(solution)/shard_map/ppermute | solution.py:23
  91.7 7.4 %copy-start.2 = (bf16[64,3712]{1,0:T(8,128)(2,1)S(1)}, bf16[64,3712]{1,0:T(8,128)(2,1)}, u32[]{:S(2)}) copy-start(bf16[64,3712]{1,0:T(8,128)(2,1)} %get-tuple-element.17) | copy-start | bytes 1425412
  97.9 7.9 %collective-permute-start.9 = (bf16[64,3712]{1,0:T(8,128)(2,1)}, bf16[64,3712]{1,0:T(8,128)(2,1)S(1)}, u32[]{:S(2)}, u32[]{:S(2)}) collective-permute-start(bf16[64,3712]{1,0:T(8,128)(2,1)} %collective-permute-done.8), channel_id=1, source_target_pairs={{0,64},{1,65},{2,66},{3,67},{4,68},{5,69},{6,70},{7,71},{8,72},{9,... | collective-permute-start | bytes 1425416 | tf_op jit(solution)/shard_map/ppermute | solution.py:23
  99.1 8.2 %slice-start = ((s8[9175040]{0:T(1024)(128)(4,1)}), s8[4194304]{0:T(1024)(128)(4,1)S(1)}, s32[]{:S(2)}) async-start(s8[9175040]{0:T(1024)(128)(4,1)} %bitcast.142), calls=%async_computation.2 | async-start | bytes 8388608
  99.2 8.1 %slice-start.1 = ((s8[9175040]{0:T(1024)(128)(4,1)}), s8[4194304]{0:T(1024)(128)(4,1)S(1)}, s32[]{:S(2)}) async-start(s8[9175040]{0:T(1024)(128)(4,1)} %bitcast.142), calls=%async_computation.3 | async-start | bytes 8388608
  99.3 8.1 %slice-start.2 = ((s8[9175040]{0:T(1024)(128)(4,1)}), s8[786432]{0:T(1024)(128)(4,1)S(1)}, s32[]{:S(2)}) async-start(s8[9175040]{0:T(1024)(128)(4,1)} %bitcast.142), calls=%async_computation.4 | async-start | bytes 1572864
  105.6 4.7 %copy-start = (f32[256,1280]{1,0:T(8,128)}, f32[256,1280]{1,0:T(8,128)S(1)}, u32[]{:S(2)}) copy-start(f32[256,1280]{1,0:T(8,128)S(1)} %fusion.4) | copy-start | bytes 3932164
  113.6 12.1 %collective-permute-start.13 = (f16[128,1280]{1,0:T(8,128)(2,1)}, f16[128,1280]{1,0:T(8,128)(2,1)}, u32[]{:S(2)}, u32[]{:S(2)}) collective-permute-start(f16[128,1280]{1,0:T(8,128)(2,1)} %multiply_convert_fusion), channel_id=1, source_target_pairs={{0,1},{1,0},{2,3},{3,2},{4,5},{5,4},{6,7},{7,6},{8,9},{9,8},{10,11... | collective-permute-start | bytes 983048 | tf_op jit(solution)/shard_map/ppermute | solution.py:23
  118.8 6.9 %collective-permute-start.15 = (f32[2,2,4,8,8]{4,3,2,1,0:T(8,128)}, f32[2,2,4,8,8]{4,3,2,1,0:T(8,128)S(1)}, u32[]{:S(2)}, u32[]{:S(2)}) collective-permute-start(f32[2,2,4,8,8]{4,3,2,1,0:T(8,128)} %dynamic_update_slice.119), channel_id=1, source_target_pairs={{0,1},{1,0},{2,3},{3,2},{4,5},{5,4},{6,7},{7,6},{8,9},{9,8},{10,11... | collective-permute-start | bytes 12296 | tf_op jit(solution)/shard_map/ppermute | solution.py:23
  120.2 8.7 %collective-permute-start.14 = (f16[64,1280]{1,0:T(8,128)(2,1)}, f16[64,1280]{1,0:T(8,128)(2,1)S(1)}, u32[]{:S(2)}, u32[]{:S(2)}) collective-permute-start(f16[64,1280]{1,0:T(8,128)(2,1)} %get-tuple-element.33), channel_id=1, source_target_pairs={{0,1},{1,0},{2,3},{3,2},{4,5},{5,4},{6,7},{7,6},{8,9},{9,8},{10,11... | collective-permute-start | bytes 491528 | tf_op jit(solution)/shard_map/ppermute | solution.py:23
  135.3 5.2 %collective-permute-start.16 = (f32[2,512]{1,0:T(2,128)S(1)}, f32[2,512]{1,0:T(2,128)S(1)}, u32[]{:S(2)}, u32[]{:S(2)}) collective-permute-start(f32[2,512]{1,0:T(2,128)S(1)} %pad_maximum_fusion.32), channel_id=1, source_target_pairs={{0,128},{1,129},{2,130},{3,131},{4,132},{5,133},{6,134},{7,135},{8... | collective-permute-start | bytes 12296 | tf_op jit(solution)/shard_map/ppermute | solution.py:23
  140.6 1.3 collective-permute-start.17
  142.6 17.5 %all-to-all-start.1 = ((f32[32,2,512]{2,1,0:T(2,128)}), f32[32,2,512]{2,1,0:T(2,128)S(1)}, u32[]{:S(2)}, u32[]{:S(2)}) async-start(f32[32,2,512]{2,1,0:T(2,128)} %broadcast_in_dim.17), calls=%async_computation.1 | async-start | bytes 262144 | tf_op jit(solution)/shard_map/all_to_all | solution.py:133

commit v2 on v0

v2 whole, which is shorter than its diff:
```python
import functools
import itertools

import jax
import jax.numpy as jnp
from jax import lax
from jax.experimental import pallas as pl
from jax.experimental.pallas import tpu as pltpu
from jax.sharding import Mesh
from jax.sharding import PartitionSpec as P

D = 7168
epsilon = 1e-06
AXES = ("yh", "core", "x", "z", "h")
NY, NC, NX, NZ, NH = SIZES = (2, 2, 4, 8, 2)
HALF = 3584
VOCAB = 1280
ROWS = 512
LANES = 128
TILE = 256
WHOLE = pl.BlockSpec(memory_space=pltpu.VMEM)


def send(value, target):
    pairs = []
    for i, at in enumerate(itertools.product(*[range(n) for n in SIZES])):
        j = 0
        for a, n in zip(target(*at), SIZES):
            j = j * n + a % n
        pairs.append((i, j))
    return lax.ppermute(value, AXES, pairs)


def to_core(value):
    return send(value, lambda y, c, x, z, h: (y, c + 1, x, z, h))


def to_hid(value):
    return send(value, lambda y, c, x, z, h: (y, c, x, z, h + 1))


def along_z(value):
    return send(value, lambda y, c, x, z, h: (y, c, x, z + (1 if c == 0 else -1), h))


def along_x(value):
    return send(value, lambda y, c, x, z, h: (y, c, x + (1 if c == 0 else -1), z, h))


def split3(value):
    parts = []
    for _ in range(3):
        part = lax.reduce_precision(value, 8, 7)
        parts.append(part.astype(jnp.bfloat16))
        value = value - part
    return parts


def product_kernel(n_out, n_stay, *refs):
    outward, stay, (head_ref,) = refs[:n_out], refs[n_out : n_out + n_stay], refs[n_out + n_stay : n_out + n_stay + 1]
    sent_ref, rest = refs[n_out + n_stay + 1], refs[n_out + n_stay + 2 :]
    kept_ref, rows = (rest[0] if n_stay else None), rest[-1]
    at = 0
    for ref in outward + stay:
        n = ref.shape[0]
        rows[at : at + n] = ref[:, :HALF]
        at += n
    m = sent_ref.shape[0]
    centre = None
    for begin in range(0, VOCAB, TILE):
        columns = slice(begin, begin + TILE)
        part = lax.dot_general(
            rows[...], head_ref[columns, :], (((1,), (1,)), ((), ())), preferred_element_type=jnp.float32
        )
        if centre is None:
            centre = jnp.mean(part[:m], axis=1, keepdims=True)
        sent_ref[:, columns] = (part[:m] - centre).astype(jnp.bfloat16)
        if n_stay:
            kept_ref[:, columns] = part[m:]
    high = centre.astype(jnp.bfloat16).astype(jnp.float32)
    middle = (centre - high).astype(jnp.bfloat16).astype(jnp.float32)
    low = centre - high - middle
    at = 0
    for ref in outward:
        n = ref.shape[0]
        part = slice(at, at + n)
        lane = lax.broadcasted_iota(jnp.int32, (n, LANES), 1)
        extra = ref[:, HALF:].astype(jnp.float32)
        extra = jnp.where(lane == 0, high[part], jnp.where(lane == 1, middle[part], jnp.where(lane == 2, low[part], extra)))
        sent_ref[part, VOCAB:] = extra.astype(jnp.bfloat16)
        at += n
    at = 0
    for ref in stay:
        n = ref.shape[0]
        kept_ref[at : at + n, VOCAB:] = ref[:, HALF:].astype(jnp.float32)
        at += n


def product(outward, stay, head):
    m, k = (sum(a.shape[0] for a in arrays) for arrays in (outward, stay))
    shapes = [jax.ShapeDtypeStruct((m, VOCAB + LANES), jnp.bfloat16)]
    if stay:
        shapes.append(jax.ShapeDtypeStruct((k, VOCAB + LANES), jnp.float32))
    return pl.pallas_call(
        functools.partial(product_kernel, len(outward), len(stay)),
        in_specs=[WHOLE] * (len(outward) + len(stay) + 1),
        out_specs=[WHOLE] * len(shapes),
        out_shape=shapes,
        scratch_shapes=[pltpu.VMEM((m + k, HALF), jnp.bfloat16)],
        compiler_params=pltpu.CompilerParams(vmem_limit_bytes=30 * 2**20),
        cost_estimate=pl.CostEstimate(
            flops=2 * max(m + k, 256) * VOCAB * HALF, bytes_accessed=2 * VOCAB * HALF, transcendentals=0
        ),
        name="product",
    )(*outward, *stay, head)


def join_kernel(places, n_got, *refs):
    got, kept, (logits_ref, stats_ref, total) = refs[:n_got], refs[n_got:-3], refs[-3:]
    core, x, z = (lax.axis_index(a) for a in ("core", "x", "z"))
    mine = jnp.where(core == 0, -1, 1)
    for first, refs in ((True, got), (False, kept)):
        for ref, groups in zip(refs, places[0 if first else 1]):
            for begin, blocks in groups:
                count = len(blocks)
                value = ref[begin : begin + 8 * count, :].astype(jnp.float32)
                for i, (c, (dx, sx), (dz, sz)) in enumerate(blocks):
                    x_at = lax.rem(x + dx + sx * mine + 2 * NX, NX)
                    z_at = lax.rem(z + dz + sz * mine + 2 * NZ, NZ)
                    at = pl.ds(pl.multiple_of(((c * NX + x_at) * NZ + z_at) * 8, 8), 8)
                    block = value[8 * i : 8 * i + 8]
                    if first:
                        total[at, :] = block
                    else:
                        total[at, :] = total[at, :] + block
    step = 128
    for begin in range(0, ROWS, step):
        rows = slice(begin, begin + step)
        extra = total[rows, VOCAB:]
        lane = lax.broadcasted_iota(jnp.int32, (step, LANES), 1)
        centre = jnp.sum(jnp.where(lane < 3, extra, 0.0), axis=1, keepdims=True)
        squares = jnp.sum(jnp.where(lane < 3, 0.0, extra), axis=1, keepdims=True)
        inv_rms = lax.rsqrt(squares / D + epsilon)
        logits = (total[rows, :VOCAB] + centre) * inv_rms
        top = jnp.max(logits, axis=1, keepdims=True)
        summed = jnp.sum(jnp.exp(logits - top), axis=1, keepdims=True)
        logits_ref[rows, :] = logits
        pair = jnp.where(lane == 0, top, summed)
        stats_ref[:, rows] = pair.T[:8]


def join(places, got, kept):
    return pl.pallas_call(
        functools.partial(join_kernel, places, len(got)),
        in_specs=[WHOLE] * (len(got) + len(kept)),
        out_specs=[WHOLE] * 2,
        out_shape=[
            jax.ShapeDtypeStruct((ROWS, VOCAB), jnp.float32),
            jax.ShapeDtypeStruct((8, ROWS), jnp.float32),
        ],
        scratch_shapes=[pltpu.VMEM((ROWS, VOCAB + LANES), jnp.float32)],
        compiler_params=pltpu.CompilerParams(vmem_limit_bytes=30 * 2**20),
        name="join",
    )(*got, *kept)


def local(tokens, gain, head):
    yh, core, h = (lax.axis_index(a) for a in ("yh", "core", "h"))
    f32 = tokens.astype(jnp.float32)
    scaled = (f32 * gain.astype(jnp.float32)).astype(jnp.bfloat16)
    squares = jnp.sum(jnp.square(f32), axis=1)
    pieces = jnp.stack(split3(squares), axis=1)
    own = jnp.concatenate([scaled, jnp.pad(pieces, ((0, 0), (3, LANES - 6)))], axis=1)

    first = core == 0

    def cat(*arrays):
        return jnp.concatenate(arrays)

    def by_core(mine, other):
        return jnp.where(first, mine, other), jnp.where(first, other, mine)

    from_y = send(own, lambda y, c, x, z, h: (y + 1, c, x, z, h))
    from_c = to_core(own)
    from_yc = send(own, lambda y, c, x, z, h: (y + 1, c + 1, x, z, h))
    stays = yh == h
    out_mine, out_other = jnp.where(stays, from_y, own), jnp.where(stays, from_yc, from_c)
    stay_mine, stay_other = jnp.where(stays, own, from_y), jnp.where(stays, from_c, from_yc)
    out16 = cat(*by_core(out_mine, out_other))
    stay16 = cat(*by_core(stay_mine, stay_other))

    near = along_x(out16)
    far = send(out_mine, lambda y, c, x, z, h: (y, c, x + 2, z, h))
    ring = [along_z(stay16)]
    side = cat(near, far)
    other_side = to_core(side)
    out64 = cat(out16, *by_core(side[:16], other_side[:16]), *by_core(side[16:], other_side[16:]))
    ring.append(along_z(ring[-1]))
    block = along_z(out64)
    ring.append(along_z(ring[-1]))
    ring.append(along_z(jnp.where(first, ring[-1][:8], ring[-1][8:])))
    ring = cat(*ring)
    other_ring = to_core(ring)
    stay128 = [stay16]
    for step in range(3):
        part = slice(16 * step, 16 * step + 16)
        stay128 += by_core(ring[part], other_ring[part])
    stay128 = cat(*stay128, *by_core(ring[48:], other_ring[48:]))

    side_x = along_x(stay128)
    sides = [(block, to_core(block))]
    block = along_z(block)
    got, kept = [], []

    def work(outward, stay):
        sent, *rest = product(outward, stay, head)
        got.append(to_hid(sent))
        kept.extend(rest)

    work([out64, *sides[0]], [stay128])
    sides.append((block, to_core(block)))
    block = along_z(block)
    work(list(sides[1]), [])
    sides_x = (side_x, to_core(side_x))
    far_x = along_x(jnp.where(first, side_x[:64], side_x[64:]))
    sides.append((block, to_core(block)))
    far_z = along_z(jnp.where(first, block[:32], block[32:]))
    work(list(sides[2]), list(sides_x))
    last_z = cat(*by_core(far_z, to_core(far_z)))
    last_x = cat(*by_core(far_x, to_core(far_x)))
    work([last_z], [last_x])

    def plane(dz, sz):
        return [(c, (dx, 0), (dz, sz)) for dx in (0, -1, 1, 2) for c in range(NC)]

    def column(dx, sx):
        return [(c, (dx, sx), (dz, 0)) for dz in (0, -1, 1, -2, 2, -3, 3, 4) for c in range(NC)]

    places = (
        (
            ((0, plane(0, 0)), (64, plane(0, 1)), (128, plane(0, -1))),
            ((0, plane(0, 2)), (64, plane(0, -2))),
            ((0, plane(0, 3)), (64, plane(0, -3))),
            ((0, plane(4, 0)),),
        ),
        (
            ((0, column(0, 0)),),
            ((0, column(0, 1)), (128, column(0, -1))),
            ((0, column(2, 0)),),
        ),
    )
    logits, stats = join(places, got, kept)

    def merge(pairs):
        best = jnp.max(pairs[:, 0], axis=0)
        return jnp.stack([best, jnp.sum(pairs[:, 1] * jnp.exp(pairs[:, 0] - best), axis=0)])

    pair = stats[:2]
    section = [pair] + [
        send(pair, lambda y, c, x, z, h: (y + dy, c + dc, x, z, h)) for dy, dc in ((0, 1), (1, 0), (1, 1))
    ]
    pair = merge(jnp.stack(section))
    every = lax.all_to_all(jnp.broadcast_to(pair[None], (NX * NZ, 2, ROWS)), ("x", "z"), 0, 0, tiled=True)
    top, total = merge(every)
    return logits - top[:, None] - jnp.log(total)[:, None]


def solution(mesh):
    fine = Mesh(mesh.devices.reshape(SIZES), AXES)
    rows = ("yh", "core", "x", "z")
    return jax.shard_map(
        local,
        mesh=fine,
        in_specs=(P(rows, "h"), P("h"), P(rows, "h")),
        out_specs=P("h", rows),
        check_vma=False,
    )
```

time: 1160 us -> 134 us (0.12)
  blocking collectives: 985 us -> 17.6 us
  waiting for transfers between devices: 130 us -> 70.2 us
  starting transfers between devices: 0.04 us -> 22.7 us
  matrix products: 16.1 us -> 0 us
  Pallas kernels: 0 us -> 14.4 us
  between operations: 14.1 us -> 0.24 us
    psum x2 -> x0, blocking collectives: 331 us -> none  [the longest x1 326 us: local(): lax.psum(jnp.sum(jnp.exp(logits - top[:, None]), axis=1), ('section', 'vo...]
    unnamed x1 -> x0, blocking collectives: 330 us -> none
    pmax x1 -> x0, blocking collectives: 324 us -> none  [local(): top = lax.pmax(jnp.max(logits, axis=1), ('section', 'vocab'))]
    all_gather x1 -> x0, waiting for transfers between devices: 130 us -> none  [local(): lax.all_gather(scaled, ('section', 'vocab'), axis=0, tiled=True)]
    ppermute x0 -> x30, waiting for transfers between devices: none -> 70.2 us  [send(): return lax.ppermute(value, AXES, pairs)]
    ppermute x0 -> x30, starting transfers between devices: none -> 22.7 us  [send(): return lax.ppermute(value, AXES, pairs)]
    all_to_all x0 -> x1, blocking collectives: none -> 17.6 us  [local(): lax.all_to_all(jnp.broadcast_to(pair[None], (NX * NZ, 2, ROWS)), ('x', 'z...]
    dot_general x1 -> x0, matrix products: 16.1 us -> none  [local(): lax.dot_general(lax.all_gather(scaled, ('section', 'vocab'), axis=0, tile...]
  transfers between devices with their start and end apart: 2 -> 30, of which waited for: 1 -> 15; matrix products, arithmetic and copies ran while one was open for 0% -> 1% of each run, Pallas kernels for 0% -> 10%
where the time goes in v2:
time: 134 us
  waiting for transfers between devices  70.2 us (52%)
  starting transfers between devices  22.7 us (17%)
  blocking collectives  17.6 us (13%)
  Pallas kernels  14.4 us (11%)
  other arithmetic  4.76 us (4%)
  local copies, waits for them, and re-layouts  3.74 us (3%)
    ppermute x30, waiting for transfers between devices, send(): return lax.ppermute(value, AXES, pairs)  70.2 us
    ppermute x30, starting transfers between devices, send(): return lax.ppermute(value, AXES, pairs)  22.7 us
    all_to_all x1, blocking collectives, local(): lax.all_to_all(jnp.broadcast_to(pair[None], (NX * NZ, 2, ROWS)), ('x', 'z...  17.6 us
    pallas_call x4, Pallas kernels, product(): pl.pallas_call(functools.partial(product_kernel, len(outward), len(stay))...  12.9 us
    unnamed x4, local copies, waits for them, and re-layouts  3.6 us
  transfers between devices with their start and end apart: 30, of which 15 were waited for; matrix products, arithmetic and copies ran while one was open for 1% of the time, Pallas kernels for 10%

profile of v2, /device:TPU:8, one launch (start us, length us, event | category | flops | bytes accessed | tf_op | source)
XLA Modules:
  0.0 133.6 jit_solution(16291921952718038067)
XLA Ops:
  0.0 0.7 convert_element_type.42
  0.7 1.0 fusion
  1.7 0.1 copy.11
  1.8 0.1 fusion.17
  1.8 0.1 collective-permute-start.2
  1.9 2.4 %collective-permute-start.1 = (bf16[8,3712]{1,0:T(8,128)(2,1)S(1)}, bf16[8,3712]{1,0:T(8,128)(2,1)S(1)}, u32[]{:S(2)}, u32[]{:S(2)}) collective-permute-start(bf16[8,3712]{1,0:T(8,128)(2,1)S(1)} %pad_maximum_fusion.6), channel_id=1, source_target_pairs={{0,192},{1,193},{2,194},{3,195},{4,196},{5,197},{6,198},{7,199},{8... | collective-permute-start | bytes 178184 | tf_op jit(solution)/shard_map/ppermute | solution.py:31
  4.4 1.2 collective-permute-start
  5.6 0.0 collective-permute-done.2
  5.6 1.6 %collective-permute-done.1 = bf16[8,3712]{1,0:T(8,128)(2,1)S(1)} collective-permute-done((bf16[8,3712]{1,0:T(8,128)(2,1)S(1)}, bf16[8,3712]{1,0:T(8,128)(2,1)S(1)}, u32[]{:S(2)}, u32[]{:S(2)}) %collective-permute-start.1) | collective-permute-done | bytes 59424 | tf_op jit(solution)/shard_map/ppermute | solution.py:31
  7.2 2.8 %collective-permute-done = bf16[8,3712]{1,0:T(8,128)(2,1)S(1)} collective-permute-done((bf16[8,3712]{1,0:T(8,128)(2,1)S(1)}, bf16[8,3712]{1,0:T(8,128)(2,1)S(1)}, u32[]{:S(2)}, u32[]{:S(2)}) %collective-permute-start) | collective-permute-done | bytes 59424 | tf_op jit(solution)/shard_map/ppermute | solution.py:31
  10.1 0.1 constant_dynamic-update-slice_fusion.2
  10.2 3.1 %collective-permute-start.4 = (bf16[8,3712]{1,0:T(8,128)(2,1)S(1)}, bf16[8,3712]{1,0:T(8,128)(2,1)S(1)}, u32[]{:S(2)}, u32[]{:S(2)}) collective-permute-start(bf16[8,3712]{1,0:T(8,128)(2,1)S(1)} %get-tuple-element.36), channel_id=1, source_target_pairs={{0,32},{1,33},{2,34},{3,35},{4,36},{5,37},{6,38},{7,39},{8,40},{9,... | collective-permute-start | bytes 178184 | tf_op jit(solution)/shard_map/ppermute | solution.py:31
  13.3 0.7 collective-permute-start.3
  14.0 2.0 %collective-permute-start.8 = (bf16[16,3712]{1,0:T(8,128)(2,1)S(1)}, bf16[16,3712]{1,0:T(8,128)(2,1)S(1)}, u32[]{:S(2)}, u32[]{:S(2)}) collective-permute-start(bf16[16,3712]{1,0:T(8,128)(2,1)S(1)} %pad_maximum_fusion.5), channel_id=1, source_target_pairs={{0,2},{1,3},{2,4},{3,5},{4,6},{5,7},{6,8},{7,9},{8,10},{9,11},{10,... | collective-permute-start | bytes 356360 | tf_op jit(solution)/shard_map/ppermute | solution.py:31
  16.0 0.0 collective-permute-done.4
  16.0 3.4 %collective-permute-done.3 = bf16[16,3712]{1,0:T(8,128)(2,1)S(1)} collective-permute-done((bf16[16,3712]{1,0:T(8,128)(2,1)S(1)}, bf16[16,3712]{1,0:T(8,128)(2,1)S(1)}, u32[]{:S(2)}, u32[]{:S(2)}) %collective-permute-start.3) | collective-permute-done | bytes 118816 | tf_op jit(solution)/shard_map/ppermute | solution.py:31
  19.5 0.1 collective-permute-start.5
  19.6 3.2 %collective-permute-done.8 = bf16[16,3712]{1,0:T(8,128)(2,1)S(1)} collective-permute-done((bf16[16,3712]{1,0:T(8,128)(2,1)S(1)}, bf16[16,3712]{1,0:T(8,128)(2,1)S(1)}, u32[]{:S(2)}, u32[]{:S(2)}) %collective-permute-start.8) | collective-permute-done | bytes 118816 | tf_op jit(solution)/shard_map/ppermute | solution.py:31
  22.8 6.0 %collective-permute-done.9 = bf16[16,3712]{1,0:T(8,128)(2,1)S(1)} collective-permute-done((bf16[16,3712]{1,0:T(8,128)(2,1)S(1)}, bf16[16,3712]{1,0:T(8,128)(2,1)S(1)}, u32[]{:S(2)}, u32[]{:S(2)}) %collective-permute-start.9) | collective-permute-done | bytes 118816 | tf_op jit(solution)/shard_map/ppermute | solution.py:31
  28.8 0.0 collective-permute-start.10
  28.8 0.0 collective-permute-done.5
  28.9 5.9 %collective-permute-done.10 = bf16[16,3712]{1,0:T(8,128)(2,1)S(1)} collective-permute-done((bf16[16,3712]{1,0:T(8,128)(2,1)S(1)}, bf16[16,3712]{1,0:T(8,128)(2,1)S(1)}, u32[]{:S(2)}, u32[]{:S(2)}) %collective-permute-start.10) | collective-permute-done | bytes 118816 | tf_op jit(solution)/shard_map/ppermute | solution.py:31
  34.9 0.1 collective-permute-start.11
  35.0 0.1 collective-permute-start.6
  35.1 5.3 %collective-permute-done.11 = bf16[8,3712]{1,0:T(8,128)(2,1)S(1)} collective-permute-done((bf16[8,3712]{1,0:T(8,128)(2,1)S(1)}, bf16[8,3712]{1,0:T(8,128)(2,1)S(1)}, u32[]{:S(2)}, u32[]{:S(2)}) %collective-permute-start.11) | collective-permute-done | bytes 59424 | tf_op jit(solution)/shard_map/ppermute | solution.py:31
  40.4 0.1 collective-permute-start.12
  40.5 5.0 %collective-permute-done.6.refs_1_ = bf16[64,3712]{1,0:T(8,128)(2,1)S(1)} collective-permute-done((bf16[64,3712]{1,0:T(8,128)(2,1)S(1)}, bf16[64,3712]{1,0:T(8,128)(2,1)S(1)}, u32[]{:S(2)}, u32[]{:S(2)}) %collective-permute-start.6) | collective-permute-done | bytes 475168 | tf_op jit(solution)/shard_map/ppermute | solution.py:31
  45.4 0.0 collective-permute-start.14
  45.5 0.0 collective-permute-done.12
  45.7 9.6 %collective-permute-done.14.refs_0_ = bf16[64,3712]{1,0:T(8,128)(2,1)S(1)} collective-permute-done((bf16[64,3712]{1,0:T(8,128)(2,1)S(1)}, bf16[64,3712]{1,0:T(8,128)(2,1)S(1)}, u32[]{:S(2)}, u32[]{:S(2)}) %collective-permute-start.14) | collective-permute-done | bytes 475168 | tf_op jit(solution)/shard_map/ppermute | solution.py:31
  55.3 0.0 collective-permute-start.17
  55.3 0.1 collective-permute-start.19
  55.4 2.9 %collective-permute-start.15 = (bf16[64,3712]{1,0:T(8,128)(2,1)S(1)}, bf16[64,3712]{1,0:T(8,128)(2,1)S(1)}, u32[]{:S(2)}, u32[]{:S(2)}) collective-permute-start(bf16[64,3712]{1,0:T(8,128)(2,1)S(1)} %collective-permute-done.14.refs_0_), channel_id=1, source_target_pairs={{0,64},{1,65},{2,66},{3,67},{4,68},{5,69},{6,70},{7,71},{8,72},{9,... | collective-permute-start | bytes 1425416 | tf_op jit(solution)/shard_map/ppermute | solution.py:31
  58.3 6.8 %collective-permute-done.17.refs_0_ = bf16[64,3712]{1,0:T(8,128)(2,1)S(1)} collective-permute-done((bf16[64,3712]{1,0:T(8,128)(2,1)S(1)}, bf16[64,3712]{1,0:T(8,128)(2,1)S(1)}, u32[]{:S(2)}, u32[]{:S(2)}) %collective-permute-start.17) | collective-permute-done | bytes 475168 | tf_op jit(solution)/shard_map/ppermute | solution.py:31
  65.2 0.3 collective-permute-start.22
  65.5 0.0 collective-permute-done.7.refs_2_
  65.5 0.0 copy-start
  65.5 3.6 %copy-done = bf16[1280,3584]{1,0:T(8,128)(2,1)S(1)} copy-done((bf16[1280,3584]{1,0:T(8,128)(2,1)S(1)}, bf16[1280,3584]{1,0:T(8,128)(2,1)}, u32[]{:S(2)}) %copy-start) | copy-done | bytes 9175064
  69.1 3.1 %product.4 = (bf16[192,1408]{1,0:T(8,128)(2,1)S(1)}, f32[128,1408]{1,0:T(8,128)S(1)}) custom-call(bf16[64,3712]{1,0:T(8,128)(2,1)S(1)} %select_dynamic-update-slice_fusion.10.refs_0_, bf16[64,3712]{1,0:T(8,128)(2,1)S(1)} %collective-permute-done.6.refs_1_, bf16[64,3712]{1,0:T(8,128)(2,1)S(1)} %collective-permute-done.7.refs_2_, ...), custom_call_target="tpu_custom_call" | custom-call | flops 2936012800 | bytes 9175040 | tf_op jit(solution)/shard_map/product/pallas_call | solution.py:104
  72.3 1.4 %collective-permute-start.13 = (bf16[192,1408]{1,0:T(8,128)(2,1)S(1)}, bf16[192,1408]{1,0:T(8,128)(2,1)S(1)}, u32[]{:S(2)}, u32[]{:S(2)}) collective-permute-start(bf16[192,1408]{1,0:T(8,128)(2,1)S(1)} %get-tuple-element.13), channel_id=1, source_target_pairs={{0,1},{1,0},{2,3},{3,2},{4,5},{5,4},{6,7},{7,6},{8,9},{9,8},{10,11... | collective-permute-start | bytes 1622024 | tf_op jit(solution)/shard_map/ppermute | solution.py:31
  73.7 3.0 %product.5 = bf16[128,1408]{1,0:T(8,128)(2,1)S(1)} custom-call(bf16[64,3712]{1,0:T(8,128)(2,1)S(1)} %collective-permute-done.14.refs_0_, bf16[64,3712]{1,0:T(8,128)(2,1)S(1)} %collective-permute-done.15.refs_1_, bf16[1280,3584]{1,0:T(8,128)(2,1)S(1)} %copy-done.1), custom_call_target="tpu_custom_call" | custom-call | flops 2348810240 | bytes 9175040 | tf_op jit(solution)/shard_map/product/pallas_call | solution.py:104
  76.7 0.8 collective-permute-start.16
  77.5 0.5 collective-permute-start.23
  78.0 0.1 slice_select_fusion
  78.0 0.1 collective-permute-start.24
  78.1 1.5 %collective-permute-done.23 = bf16[32,3712]{1,0:T(8,128)(2,1)S(1)} collective-permute-done((bf16[32,3712]{1,0:T(8,128)(2,1)S(1)}, bf16[32,3712]{1,0:T(8,128)(2,1)S(1)}, u32[]{:S(2)}, u32[]{:S(2)}) %collective-permute-start.23) | collective-permute-done | bytes 237600 | tf_op jit(solution)/shard_map/ppermute | solution.py:31
  79.6 0.8 collective-permute-start.20
  80.5 7.4 %collective-permute-done.24 = bf16[64,3712]{1,0:T(8,128)(2,1)S(1)} collective-permute-done((bf16[64,3712]{1,0:T(8,128)(2,1)S(1)}, bf16[64,3712]{1,0:T(8,128)(2,1)S(1)}, u32[]{:S(2)}, u32[]{:S(2)}) %collective-permute-start.24) | collective-permute-done | bytes 475168 | tf_op jit(solution)/shard_map/ppermute | solution.py:31
  88.0 3.7 %product.6 = (bf16[128,1408]{1,0:T(8,128)(2,1)S(1)}, f32[256,1408]{1,0:T(8,128)S(1)}) custom-call(bf16[64,3712]{1,0:T(8,128)(2,1)S(1)} %collective-permute-done.17.refs_0_, bf16[64,3712]{1,0:T(8,128)(2,1)S(1)} %collective-permute-done.18.refs_1_, bf16[128,3712]{1,0:T(8,128)(2,1)S(1)} %collective-permute-done.19.refs_2_, ...), custom_call_target="tpu_custom_call" | custom-call | flops 3523215360 | bytes 9175040 | tf_op jit(solution)/shard_map/product/pallas_call | solution.py:104
  91.8 1.4 %collective-permute-start.21 = (bf16[128,1408]{1,0:T(8,128)(2,1)S(1)}, bf16[128,1408]{1,0:T(8,128)(2,1)S(1)}, u32[]{:S(2)}, u32[]{:S(2)}) collective-permute-start(bf16[128,1408]{1,0:T(8,128)(2,1)S(1)} %get-tuple-element.14), channel_id=1, source_target_pairs={{0,1},{1,0},{2,3},{3,2},{4,5},{5,4},{6,7},{7,6},{8,9},{9,8},{10,11... | collective-permute-start | bytes 1081352 | tf_op jit(solution)/shard_map/ppermute | solution.py:31
  93.2 0.1 broadcast_select_fusion.1
  93.3 0.1 pad_maximum_fusion.refs_1_
  93.4 3.1 %product.7 = (bf16[64,1408]{1,0:T(8,128)(2,1)S(1)}, f32[128,1408]{1,0:T(8,128)S(1)}) custom-call(bf16[64,3712]{1,0:T(8,128)(2,1)S(1)} %pad_maximum_fusion.1.refs_0_, bf16[128,3712]{1,0:T(8,128)(2,1)S(1)} %pad_maximum_fusion.refs_1_, bf16[1280,3584]{1,0:T(8,128)(2,1)S(1)} %copy-done.1), custom_call_target="tpu_custom_call" | custom-call | flops 2348810240 | bytes 9175040 | tf_op jit(solution)/shard_map/product/pallas_call | solution.py:104
  96.4 1.0 collective-permute-start.26
  97.4 9.1 %collective-permute-done.26.refs_3_ = bf16[64,1408]{1,0:T(8,128)(2,1)S(1)} collective-permute-done((bf16[64,1408]{1,0:T(8,128)(2,1)S(1)}, bf16[64,1408]{1,0:T(8,128)(2,1)S(1)}, u32[]{:S(2)}, u32[]{:S(2)}) %collective-permute-start.26) | collective-permute-done | bytes 180256 | tf_op jit(solution)/shard_map/ppermute | solution.py:31
  106.6 1.5 %join.1 = (f32[512,1280]{1,0:T(8,128)S(1)}, f32[8,512]{1,0:T(8,128)S(1)}) custom-call(bf16[192,1408]{1,0:T(8,128)(2,1)S(1)} %collective-permute-done.13.refs_0_, bf16[128,1408]{1,0:T(8,128)(2,1)S(1)} %collective-permute-done.16.refs_1_, bf16[128,1408]{1,0:T(8,128)(2,1)S(1)} %collective-permute-done.21.refs_2_, ...), custom_call_target="tpu_custom_call" | custom-call | tf_op jit(solution)/shard_map/join/pallas_call | solution.py:153
  108.0 0.7 collective-permute-start.29
  108.7 2.2 %collective-permute-start.28 = (f32[2,512]{1,0:T(2,128)S(1)}, f32[2,512]{1,0:T(2,128)S(1)}, u32[]{:S(2)}, u32[]{:S(2)}) collective-permute-start(f32[2,512]{1,0:T(2,128)S(1)} %get-tuple-element.46), channel_id=1, source_target_pairs={{0,128},{1,129},{2,130},{3,131},{4,132},{5,133},{6,134},{7,135},{8... | collective-permute-start | bytes 12296 | tf_op jit(solution)/shard_map/ppermute | solution.py:31
  111.0 0.5 collective-permute-start.27
  111.5 1.2 collective-permute-done.29
  112.6 1.2 collective-permute-done.28
  114.0 17.6 %all_to_all.5 = f32[32,2,512]{2,1,0:T(2,128)S(1)} all-to-all(f32[32,2,512]{2,1,0:T(2,128)S(1)} %broadcast_in_dim.2), channel_id=1, replica_groups=mesh['yh'=2,'core'=2,'x'=4,'z'=8,'h'=2] {'x','z'}, dimensions={0} | all-to-all | bytes 262144 | tf_op jit(solution)/shard_map/all_to_all | solution.py:263
  131.6 0.1 slice_reduce_fusion.1
  131.8 1.8 %subtract_subtract_fusion = f32[512,1280]{1,0:T(8,128)} fusion(f32[512,1280]{1,0:T(8,128)S(1)} %get-tuple-element.19, f32[512]{0:T(512)S(1)} %log.7, f32[512]{0:T(512)S(1)} %get-tuple-element.37), kind=kLoop, calls=%fused_computation | loop fusion | flops 1310720 | bytes 5246976 | tf_op jit(solution)/shard_map/sub | solution.py:265
  (48 shorter events, 0.9 us)
Async XLA Ops:
  1.8 3.8 %collective-permute-start.2 = (bf16[8,3712]{1,0:T(8,128)(2,1)S(1)}, bf16[8,3712]{1,0:T(8,128)(2,1)S(1)}, u32[]{:S(2)}, u32[]{:S(2)}) collective-permute-start(bf16[8,3712]{1,0:T(8,128)(2,1)S(1)} %pad_maximum_fusion.6), channel_id=1, source_target_pairs={{0,64},{1,65},{2,66},{3,67},{4,68},{5,69},{6,70},{7,71},{8,72},{9,... | collective-permute-start | bytes 178184 | tf_op jit(solution)/shard_map/ppermute | solution.py:31
  1.9 5.3 %collective-permute-start.1 = (bf16[8,3712]{1,0:T(8,128)(2,1)S(1)}, bf16[8,3712]{1,0:T(8,128)(2,1)S(1)}, u32[]{:S(2)}, u32[]{:S(2)}) collective-permute-start(bf16[8,3712]{1,0:T(8,128)(2,1)S(1)} %pad_maximum_fusion.6), channel_id=1, source_target_pairs={{0,192},{1,193},{2,194},{3,195},{4,196},{5,197},{6,198},{7,199},{8... | collective-permute-start | bytes 178184 | tf_op jit(solution)/shard_map/ppermute | solution.py:31
  4.4 5.7 %collective-permute-start = (bf16[8,3712]{1,0:T(8,128)(2,1)S(1)}, bf16[8,3712]{1,0:T(8,128)(2,1)S(1)}, u32[]{:S(2)}, u32[]{:S(2)}) collective-permute-start(bf16[8,3712]{1,0:T(8,128)(2,1)S(1)} %pad_maximum_fusion.6), channel_id=1, source_target_pairs={{0,128},{1,129},{2,130},{3,131},{4,132},{5,133},{6,134},{7,135},{8... | collective-permute-start | bytes 178184 | tf_op jit(solution)/shard_map/ppermute | solution.py:31
  10.2 5.8 %collective-permute-start.4 = (bf16[8,3712]{1,0:T(8,128)(2,1)S(1)}, bf16[8,3712]{1,0:T(8,128)(2,1)S(1)}, u32[]{:S(2)}, u32[]{:S(2)}) collective-permute-start(bf16[8,3712]{1,0:T(8,128)(2,1)S(1)} %get-tuple-element.36), channel_id=1, source_target_pairs={{0,32},{1,33},{2,34},{3,35},{4,36},{5,37},{6,38},{7,39},{8,40},{9,... | collective-permute-start | bytes 178184 | tf_op jit(solution)/shard_map/ppermute | solution.py:31
  13.3 6.1 %collective-permute-start.3 = (bf16[16,3712]{1,0:T(8,128)(2,1)S(1)}, bf16[16,3712]{1,0:T(8,128)(2,1)S(1)}, u32[]{:S(2)}, u32[]{:S(2)}) collective-permute-start(bf16[16,3712]{1,0:T(8,128)(2,1)S(1)} %pad_maximum_fusion.4), channel_id=1, source_target_pairs={{0,16},{1,17},{2,18},{3,19},{4,20},{5,21},{6,22},{7,23},{8,24},{9,... | collective-permute-start | bytes 356360 | tf_op jit(solution)/shard_map/ppermute | solution.py:31
  14.0 8.7 %collective-permute-start.8 = (bf16[16,3712]{1,0:T(8,128)(2,1)S(1)}, bf16[16,3712]{1,0:T(8,128)(2,1)S(1)}, u32[]{:S(2)}, u32[]{:S(2)}) collective-permute-start(bf16[16,3712]{1,0:T(8,128)(2,1)S(1)} %pad_maximum_fusion.5), channel_id=1, source_target_pairs={{0,2},{1,3},{2,4},{3,5},{4,6},{5,7},{6,8},{7,9},{8,10},{9,11},{10,... | collective-permute-start | bytes 356360 | tf_op jit(solution)/shard_map/ppermute | solution.py:31
  19.5 9.3 %collective-permute-start.5 = (bf16[24,3712]{1,0:T(8,128)(2,1)S(1)}, bf16[24,3712]{1,0:T(8,128)(2,1)S(1)}, u32[]{:S(2)}, u32[]{:S(2)}) collective-permute-start(bf16[24,3712]{1,0:T(8,128)(2,1)S(1)} %pad_maximum_fusion.3), channel_id=1, source_target_pairs={{0,64},{1,65},{2,66},{3,67},{4,68},{5,69},{6,70},{7,71},{8,72},{9,... | collective-permute-start | bytes 534536 | tf_op jit(solution)/shard_map/ppermute | solution.py:31
  22.8 6.0 %collective-permute-start.9 = (bf16[16,3712]{1,0:T(8,128)(2,1)S(1)}, bf16[16,3712]{1,0:T(8,128)(2,1)S(1)}, u32[]{:S(2)}, u32[]{:S(2)}) collective-permute-start(bf16[16,3712]{1,0:T(8,128)(2,1)S(1)} %collective-permute-done.8), channel_id=1, source_target_pairs={{0,2},{1,3},{2,4},{3,5},{4,6},{5,7},{6,8},{7,9},{8,10},{9,11},{10,... | collective-permute-start | bytes 356360 | tf_op jit(solution)/shard_map/ppermute | solution.py:31
  28.8 6.0 %collective-permute-start.10 = (bf16[16,3712]{1,0:T(8,128)(2,1)S(1)}, bf16[16,3712]{1,0:T(8,128)(2,1)S(1)}, u32[]{:S(2)}, u32[]{:S(2)}) collective-permute-start(bf16[16,3712]{1,0:T(8,128)(2,1)S(1)} %collective-permute-done.9), channel_id=1, source_target_pairs={{0,2},{1,3},{2,4},{3,5},{4,6},{5,7},{6,8},{7,9},{8,10},{9,11},{10,... | collective-permute-start | bytes 356360 | tf_op jit(solution)/shard_map/ppermute | solution.py:31
  34.9 5.5 %collective-permute-start.11 = (bf16[8,3712]{1,0:T(8,128)(2,1)S(1)}, bf16[8,3712]{1,0:T(8,128)(2,1)S(1)}, u32[]{:S(2)}, u32[]{:S(2)}) collective-permute-start(bf16[8,3712]{1,0:T(8,128)(2,1)S(1)} %slice_select_fusion.2), channel_id=1, source_target_pairs={{0,2},{1,3},{2,4},{3,5},{4,6},{5,7},{6,8},{7,9},{8,10},{9,11},{10,... | collective-permute-start | bytes 178184 | tf_op jit(solution)/shard_map/ppermute | solution.py:31
  35.0 10.5 %collective-permute-start.6 = (bf16[64,3712]{1,0:T(8,128)(2,1)S(1)}, bf16[64,3712]{1,0:T(8,128)(2,1)S(1)}, u32[]{:S(2)}, u32[]{:S(2)}) collective-permute-start(bf16[64,3712]{1,0:T(8,128)(2,1)S(1)} %select_dynamic-update-slice_fusion.10.refs_0_), channel_id=1, source_target_pairs={{0,2},{1,3},{2,4},{3,5},{4,6},{5,7},{6,8},{7,9},{8,10},{9,11},{10,... | collective-permute-start | bytes 1425416 | tf_op jit(solution)/shard_map/ppermute | solution.py:31
  40.4 5.1 %collective-permute-start.12 = (bf16[56,3712]{1,0:T(8,128)(2,1)S(1)}, bf16[56,3712]{1,0:T(8,128)(2,1)S(1)}, u32[]{:S(2)}, u32[]{:S(2)}) collective-permute-start(bf16[56,3712]{1,0:T(8,128)(2,1)S(1)} %pad_maximum_fusion.2), channel_id=1, source_target_pairs={{0,64},{1,65},{2,66},{3,67},{4,68},{5,69},{6,70},{7,71},{8,72},{9,... | collective-permute-start | bytes 1247240 | tf_op jit(solution)/shard_map/ppermute | solution.py:31
  45.4 20.0 %collective-permute-start.7 = (bf16[64,3712]{1,0:T(8,128)(2,1)S(1)}, bf16[64,3712]{1,0:T(8,128)(2,1)S(1)}, u32[]{:S(2)}, u32[]{:S(2)}) collective-permute-start(bf16[64,3712]{1,0:T(8,128)(2,1)S(1)} %collective-permute-done.6.refs_1_), channel_id=1, source_target_pairs={{0,64},{1,65},{2,66},{3,67},{4,68},{5,69},{6,70},{7,71},{8,72},{9,... | collective-permute-start | bytes 1425416 | tf_op jit(solution)/shard_map/ppermute | solution.py:31
  45.4 9.9 %collective-permute-start.14 = (bf16[64,3712]{1,0:T(8,128)(2,1)S(1)}, bf16[64,3712]{1,0:T(8,128)(2,1)S(1)}, u32[]{:S(2)}, u32[]{:S(2)}) collective-permute-start(bf16[64,3712]{1,0:T(8,128)(2,1)S(1)} %collective-permute-done.6.refs_1_), channel_id=1, source_target_pairs={{0,2},{1,3},{2,4},{3,5},{4,6},{5,7},{6,8},{7,9},{8,10},{9,11},{10,... | collective-permute-start | bytes 1425416 | tf_op jit(solution)/shard_map/ppermute | solution.py:31
  55.3 9.9 %collective-permute-start.17 = (bf16[64,3712]{1,0:T(8,128)(2,1)S(1)}, bf16[64,3712]{1,0:T(8,128)(2,1)S(1)}, u32[]{:S(2)}, u32[]{:S(2)}) collective-permute-start(bf16[64,3712]{1,0:T(8,128)(2,1)S(1)} %collective-permute-done.14.refs_0_), channel_id=1, source_target_pairs={{0,2},{1,3},{2,4},{3,5},{4,6},{5,7},{6,8},{7,9},{8,10},{9,11},{10,... | collective-permute-start | bytes 1425416 | tf_op jit(solution)/shard_map/ppermute | solution.py:31
  55.3 22.6 %collective-permute-start.19 = (bf16[128,3712]{1,0:T(8,128)(2,1)S(1)}, bf16[128,3712]{1,0:T(8,128)(2,1)S(1)}, u32[]{:S(2)}, u32[]{:S(2)}) collective-permute-start(bf16[128,3712]{1,0:T(8,128)(2,1)S(1)} %select_dynamic-update-slice_fusion.8.refs_3_), channel_id=1, source_target_pairs={{0,16},{1,17},{2,18},{3,19},{4,20},{5,21},{6,22},{7,23},{8,24},{9,... | collective-permute-start | bytes 2850824 | tf_op jit(solution)/shard_map/ppermute | solution.py:31
  55.4 18.3 %collective-permute-start.15 = (bf16[64,3712]{1,0:T(8,128)(2,1)S(1)}, bf16[64,3712]{1,0:T(8,128)(2,1)S(1)}, u32[]{:S(2)}, u32[]{:S(2)}) collective-permute-start(bf16[64,3712]{1,0:T(8,128)(2,1)S(1)} %collective-permute-done.14.refs_0_), channel_id=1, source_target_pairs={{0,64},{1,65},{2,66},{3,67},{4,68},{5,69},{6,70},{7,71},{8,72},{9,... | collective-permute-start | bytes 1425416 | tf_op jit(solution)/shard_map/ppermute | solution.py:31
  65.2 12.2 %collective-permute-start.22 = (bf16[32,3712]{1,0:T(8,128)(2,1)S(1)}, bf16[32,3712]{1,0:T(8,128)(2,1)S(1)}, u32[]{:S(2)}, u32[]{:S(2)}) collective-permute-start(bf16[32,3712]{1,0:T(8,128)(2,1)S(1)} %slice_select_fusion.1), channel_id=1, source_target_pairs={{0,2},{1,3},{2,4},{3,5},{4,6},{5,7},{6,8},{7,9},{8,10},{9,11},{10,... | collective-permute-start | bytes 712712 | tf_op jit(solution)/shard_map/ppermute | solution.py:31
  65.5 3.6 %copy-start = (bf16[1280,3584]{1,0:T(8,128)(2,1)S(1)}, bf16[1280,3584]{1,0:T(8,128)(2,1)}, u32[]{:S(2)}) copy-start(bf16[1280,3584]{1,0:T(8,128)(2,1)} %refs_2_.3) | copy-start | bytes 27525124
  69.1 4.6 %copy-start.1 = (bf16[1280,3584]{1,0:T(8,128)(2,1)S(1)}, bf16[1280,3584]{1,0:T(8,128)(2,1)}, u32[]{:S(2)}) copy-start(bf16[1280,3584]{1,0:T(8,128)(2,1)} %refs_2_.3) | copy-start | bytes 27525124
  72.3 25.2 %collective-permute-start.13 = (bf16[192,1408]{1,0:T(8,128)(2,1)S(1)}, bf16[192,1408]{1,0:T(8,128)(2,1)S(1)}, u32[]{:S(2)}, u32[]{:S(2)}) collective-permute-start(bf16[192,1408]{1,0:T(8,128)(2,1)S(1)} %get-tuple-element.13), channel_id=1, source_target_pairs={{0,1},{1,0},{2,3},{3,2},{4,5},{5,4},{6,7},{7,6},{8,9},{9,8},{10,11... | collective-permute-start | bytes 1622024 | tf_op jit(solution)/shard_map/ppermute | solution.py:31
  76.7 20.7 %collective-permute-start.16 = (bf16[128,1408]{1,0:T(8,128)(2,1)S(1)}, bf16[128,1408]{1,0:T(8,128)(2,1)S(1)}, u32[]{:S(2)}, u32[]{:S(2)}) collective-permute-start(bf16[128,1408]{1,0:T(8,128)(2,1)S(1)} %product.5), channel_id=1, source_target_pairs={{0,1},{1,0},{2,3},{3,2},{4,5},{5,4},{6,7},{7,6},{8,9},{9,8},{10,11... | collective-permute-start | bytes 1081352 | tf_op jit(solution)/shard_map/ppermute | solution.py:31
  77.5 10.6 %collective-permute-start.18 = (bf16[64,3712]{1,0:T(8,128)(2,1)S(1)}, bf16[64,3712]{1,0:T(8,128)(2,1)S(1)}, u32[]{:S(2)}, u32[]{:S(2)}) collective-permute-start(bf16[64,3712]{1,0:T(8,128)(2,1)S(1)} %collective-permute-done.17.refs_0_), channel_id=1, source_target_pairs={{0,64},{1,65},{2,66},{3,67},{4,68},{5,69},{6,70},{7,71},{8,72},{9,... | collective-permute-start | bytes 1425416 | tf_op jit(solution)/shard_map/ppermute | solution.py:31
  77.5 2.2 %collective-permute-start.23 = (bf16[32,3712]{1,0:T(8,128)(2,1)S(1)}, bf16[32,3712]{1,0:T(8,128)(2,1)S(1)}, u32[]{:S(2)}, u32[]{:S(2)}) collective-permute-start(bf16[32,3712]{1,0:T(8,128)(2,1)S(1)} %collective-permute-done.22), channel_id=1, source_target_pairs={{0,64},{1,65},{2,66},{3,67},{4,68},{5,69},{6,70},{7,71},{8,72},{9,... | collective-permute-start | bytes 712712 | tf_op jit(solution)/shard_map/ppermute | solution.py:31
  78.0 9.9 %collective-permute-start.24 = (bf16[64,3712]{1,0:T(8,128)(2,1)S(1)}, bf16[64,3712]{1,0:T(8,128)(2,1)S(1)}, u32[]{:S(2)}, u32[]{:S(2)}) collective-permute-start(bf16[64,3712]{1,0:T(8,128)(2,1)S(1)} %slice_select_fusion), channel_id=1, source_target_pairs={{0,16},{1,17},{2,18},{3,19},{4,20},{5,21},{6,22},{7,23},{8,24},{9,... | collective-permute-start | bytes 1425416 | tf_op jit(solution)/shard_map/ppermute | solution.py:31
  79.6 8.4 %collective-permute-start.20 = (bf16[128,3712]{1,0:T(8,128)(2,1)S(1)}, bf16[128,3712]{1,0:T(8,128)(2,1)S(1)}, u32[]{:S(2)}, u32[]{:S(2)}) collective-permute-start(bf16[128,3712]{1,0:T(8,128)(2,1)S(1)} %collective-permute-done.19.refs_2_), channel_id=1, source_target_pairs={{0,64},{1,65},{2,66},{3,67},{4,68},{5,69},{6,70},{7,71},{8,72},{9,... | collective-permute-start | bytes 2850824 | tf_op jit(solution)/shard_map/ppermute | solution.py:31
  88.0 5.2 %collective-permute-start.25 = (bf16[64,3712]{1,0:T(8,128)(2,1)S(1)}, bf16[64,3712]{1,0:T(8,128)(2,1)S(1)}, u32[]{:S(2)}, u32[]{:S(2)}) collective-permute-start(bf16[64,3712]{1,0:T(8,128)(2,1)S(1)} %collective-permute-done.24), channel_id=1, source_target_pairs={{0,64},{1,65},{2,66},{3,67},{4,68},{5,69},{6,70},{7,71},{8,72},{9,... | collective-permute-start | bytes 1425416 | tf_op jit(solution)/shard_map/ppermute | solution.py:31
  91.8 14.8 %collective-permute-start.21 = (bf16[128,1408]{1,0:T(8,128)(2,1)S(1)}, bf16[128,1408]{1,0:T(8,128)(2,1)S(1)}, u32[]{:S(2)}, u32[]{:S(2)}) collective-permute-start(bf16[128,1408]{1,0:T(8,128)(2,1)S(1)} %get-tuple-element.14), channel_id=1, source_target_pairs={{0,1},{1,0},{2,3},{3,2},{4,5},{5,4},{6,7},{7,6},{8,9},{9,8},{10,11... | collective-permute-start | bytes 1081352 | tf_op jit(solution)/shard_map/ppermute | solution.py:31
  96.4 10.1 %collective-permute-start.26 = (bf16[64,1408]{1,0:T(8,128)(2,1)S(1)}, bf16[64,1408]{1,0:T(8,128)(2,1)S(1)}, u32[]{:S(2)}, u32[]{:S(2)}) collective-permute-start(bf16[64,1408]{1,0:T(8,128)(2,1)S(1)} %get-tuple-element.15), channel_id=1, source_target_pairs={{0,1},{1,0},{2,3},{3,2},{4,5},{5,4},{6,7},{7,6},{8,9},{9,8},{10,11... | collective-permute-start | bytes 540680 | tf_op jit(solution)/shard_map/ppermute | solution.py:31
  108.0 4.6 %collective-permute-start.29 = (f32[2,512]{1,0:T(2,128)S(1)}, f32[2,512]{1,0:T(2,128)S(1)}, u32[]{:S(2)}, u32[]{:S(2)}) collective-permute-start(f32[2,512]{1,0:T(2,128)S(1)} %get-tuple-element.46), channel_id=1, source_target_pairs={{0,192},{1,193},{2,194},{3,195},{4,196},{5,197},{6,198},{7,199},{8... | collective-permute-start | bytes 12296 | tf_op jit(solution)/shard_map/ppermute | solution.py:31
  108.7 5.1 %collective-permute-start.28 = (f32[2,512]{1,0:T(2,128)S(1)}, f32[2,512]{1,0:T(2,128)S(1)}, u32[]{:S(2)}, u32[]{:S(2)}) collective-permute-start(f32[2,512]{1,0:T(2,128)S(1)} %get-tuple-element.46), channel_id=1, source_target_pairs={{0,128},{1,129},{2,130},{3,131},{4,132},{5,133},{6,134},{7,135},{8... | collective-permute-start | bytes 12296 | tf_op jit(solution)/shard_map/ppermute | solution.py:31
  111.0 2.9 %collective-permute-start.27 = (f32[2,512]{1,0:T(2,128)S(1)}, f32[2,512]{1,0:T(2,128)S(1)}, u32[]{:S(2)}, u32[]{:S(2)}) collective-permute-start(f32[2,512]{1,0:T(2,128)S(1)} %get-tuple-element.46), channel_id=1, source_target_pairs={{0,64},{1,65},{2,66},{3,67},{4,68},{5,69},{6,70},{7,71},{8,72},{9,... | collective-permute-start | bytes 12296 | tf_op jit(solution)/shard_map/ppermute | solution.py:31

commit v3 on v2

v3 whole, which is shorter than its diff:
```python
import functools
import itertools

import jax
import jax.numpy as jnp
from jax import lax
from jax.experimental import pallas as pl
from jax.experimental.pallas import tpu as pltpu
from jax.sharding import Mesh
from jax.sharding import PartitionSpec as P

D = 7168
epsilon = 1e-06
AXES = ("yh", "core", "x", "z", "h")
NY, NC, NX, NZ, NH = SIZES = (2, 2, 4, 8, 2)
HALF = 3584
VOCAB = 1280
ROWS = 512
LANES = 128
REACH = 80.0
TILE = 256
WHOLE = pl.BlockSpec(memory_space=pltpu.VMEM)


def send(value, target):
    pairs = []
    for i, at in enumerate(itertools.product(*[range(n) for n in SIZES])):
        j = 0
        for a, n in zip(target(*at), SIZES):
            j = j * n + a % n
        pairs.append((i, j))
    return lax.ppermute(value, AXES, pairs)


def to_core(value):
    return send(value, lambda y, c, x, z, h: (y, c + 1, x, z, h))


def to_hid(value):
    return send(value, lambda y, c, x, z, h: (y, c, x, z, h + 1))


def along_z(value, hops=1):
    return send(value, lambda y, c, x, z, h: (y, c, x, z + (hops if c == 0 else -hops), h))


def along_x(value):
    return send(value, lambda y, c, x, z, h: (y, c, x + (1 if c == 0 else -1), z, h))


def split3(value):
    parts = []
    for _ in range(3):
        part = lax.reduce_precision(value, 8, 7)
        parts.append(part.astype(jnp.bfloat16))
        value = value - part
    return parts


def split3_in_kernel(value):
    high = value.astype(jnp.bfloat16).astype(jnp.float32)
    middle = (value - high).astype(jnp.bfloat16).astype(jnp.float32)
    return high, middle, value - high - middle


def product_kernel(n_blocks, *refs):
    outward, stay, (head_ref, sent_ref, kept_ref, rows, raw) = refs[:n_blocks], refs[n_blocks:-5], refs[-5:]
    m = sent_ref.shape[0]
    at = 0
    for ref in outward + stay:
        n = ref.shape[0]
        rows[at : at + n] = ref[:, :HALF]
        if at >= m:
            kept_ref[at - m : at - m + n, VOCAB:] = ref[:, HALF:].astype(jnp.float32)
        at += n
    for begin in range(0, VOCAB, TILE):
        columns = slice(begin, begin + TILE)
        part = lax.dot_general(
            rows[...], head_ref[columns, :], (((1,), (1,)), ((), ())), preferred_element_type=jnp.float32
        )
        raw[:, columns] = part[:m]
        kept_ref[:, columns] = part[m:]
    at = 0
    for ref in outward:
        for begin in range(0, ref.shape[0], 32):
            part = slice(at, at + 32)
            value = raw[part, :]
            high = jnp.max(value, axis=1, keepdims=True)
            low = jnp.min(value, axis=1, keepdims=True)
            centre = 0.5 * (high + low)
            unit = jnp.maximum((high - low) * (0.5 / REACH), 1e-30)
            sent_ref[part, :VOCAB] = jnp.exp((value - centre) * (1.0 / unit)).astype(jnp.bfloat16)
            lane = lax.broadcasted_iota(jnp.int32, (32, LANES), 1)
            extra = ref[begin : begin + 32, HALF:].astype(jnp.float32)
            for where, number in ((0, centre), (6, unit)):
                for i, piece in enumerate(split3_in_kernel(number)):
                    extra = jnp.where(lane == where + i, piece, extra)
            sent_ref[part, VOCAB:] = extra.astype(jnp.bfloat16)
            at += 32


def product(outward, stay, head):
    m = sum(a.shape[0] for a in outward)
    return pl.pallas_call(
        functools.partial(product_kernel, len(outward)),
        in_specs=[WHOLE] * (2 * len(outward) + 1),
        out_specs=[WHOLE] * 2,
        out_shape=[
            jax.ShapeDtypeStruct((m, VOCAB + LANES), jnp.bfloat16),
            jax.ShapeDtypeStruct((m, VOCAB + LANES), jnp.float32),
        ],
        scratch_shapes=[pltpu.VMEM((2 * m, HALF), jnp.bfloat16), pltpu.VMEM((m, VOCAB), jnp.float32)],
        compiler_params=pltpu.CompilerParams(vmem_limit_bytes=30 * 2**20),
        cost_estimate=pl.CostEstimate(flops=1, bytes_accessed=1, transcendentals=0),
        name="product",
    )(*outward, *stay, head)


def join_kernel(places, n_got, *refs):
    got, kept, (logits_ref, stats_ref, total) = refs[:n_got], refs[n_got:-3], refs[-3:]
    core, x, z = (lax.axis_index(a) for a in ("core", "x", "z"))
    mine = jnp.where(core == 0, -1, 1)
    for first, refs in ((True, got), (False, kept)):
        for ref, groups in zip(refs, places):
            for begin, blocks in zip(range(0, ref.shape[0], 64), groups):
                value = ref[begin : begin + 64, :VOCAB].astype(jnp.float32)
                extra = ref[begin : begin + 64, VOCAB:].astype(jnp.float32)
                if first:
                    lane = lax.broadcasted_iota(jnp.int32, extra.shape, 1)
                    centre = jnp.sum(jnp.where(lane < 3, extra, 0.0), axis=1, keepdims=True)
                    unit = jnp.sum(jnp.where(lane < 6, 0.0, extra), axis=1, keepdims=True)
                    extra = jnp.where((lane >= 3) & (lane < 6), extra, 0.0)
                    value = jnp.log(value) * unit + centre
                for i, (c, dx, (dz, sz)) in enumerate(blocks):
                    x_at = lax.rem(x + dx + NX, NX)
                    z_at = lax.rem(z + dz + sz * mine + NZ, NZ)
                    at = pl.ds(pl.multiple_of(((c * NX + x_at) * NZ + z_at) * 8, 8), 8)
                    eight = slice(8 * i, 8 * i + 8)
                    if first:
                        total[at, :VOCAB] = value[eight]
                        total[at, VOCAB:] = extra[eight]
                    else:
                        total[at, :VOCAB] += value[eight]
                        total[at, VOCAB:] += extra[eight]
    step = 128
    for begin in range(0, ROWS, step):
        rows = slice(begin, begin + step)
        lane = lax.broadcasted_iota(jnp.int32, (step, LANES), 1)
        squares = jnp.sum(total[rows, VOCAB:], axis=1, keepdims=True)
        inv_rms = lax.rsqrt(squares / D + epsilon)
        logits = total[rows, :VOCAB] * inv_rms
        top = jnp.max(logits, axis=1, keepdims=True)
        summed = jnp.sum(jnp.exp(logits - top), axis=1, keepdims=True)
        logits_ref[rows, :] = logits
        pair = jnp.where(lane == 0, top, summed)
        stats_ref[:, rows] = pair.T[:8]


def join(places, got, kept):
    return pl.pallas_call(
        functools.partial(join_kernel, places, len(got)),
        in_specs=[WHOLE] * (len(got) + len(kept)),
        out_specs=[WHOLE] * 2,
        out_shape=[
            jax.ShapeDtypeStruct((ROWS, VOCAB), jnp.float32),
            jax.ShapeDtypeStruct((8, ROWS), jnp.float32),
        ],
        scratch_shapes=[pltpu.VMEM((ROWS, VOCAB + LANES), jnp.float32)],
        compiler_params=pltpu.CompilerParams(vmem_limit_bytes=30 * 2**20),
        name="join",
    )(*got, *kept)


def touch_kernel(rows_ref, head_ref, out_ref):
    out_ref[...] = rows_ref[...]


def touch(rows, head):
    return pl.pallas_call(
        touch_kernel,
        in_specs=[WHOLE] * 2,
        out_specs=WHOLE,
        out_shape=jax.ShapeDtypeStruct(rows.shape, rows.dtype),
        compiler_params=pltpu.CompilerParams(vmem_limit_bytes=16 * 2**20),
        name="touch",
    )(rows, head)


def local(tokens, gain, head):
    yh, core, h = (lax.axis_index(a) for a in ("yh", "core", "h"))
    f32 = tokens.astype(jnp.float32)
    scaled = (f32 * gain.astype(jnp.float32)).astype(jnp.bfloat16)
    squares = jnp.sum(jnp.square(f32), axis=1)
    pieces = jnp.stack(split3(squares), axis=1)
    own = jnp.concatenate([scaled, jnp.pad(pieces, ((0, 0), (3, LANES - 6)))], axis=1)

    first = core == 0

    def cat(*arrays):
        return jnp.concatenate(arrays)

    def by_core(mine, other):
        return jnp.where(first, mine, other), jnp.where(first, other, mine)

    from_y = send(own, lambda y, c, x, z, h: (y + 1, c, x, z, h))
    from_c = to_core(own)
    from_yc = send(own, lambda y, c, x, z, h: (y + 1, c + 1, x, z, h))
    flag = touch(jnp.full((8, LANES), yh == h, jnp.float32), head)
    stays = flag[:1, :1] > 0.5
    out_mine, out_other = jnp.where(stays, from_y, own), jnp.where(stays, from_yc, from_c)
    stay_mine, stay_other = jnp.where(stays, own, from_y), jnp.where(stays, from_c, from_yc)
    out16 = cat(*by_core(out_mine, out_other))
    stay16 = cat(*by_core(stay_mine, stay_other))

    after = lax.optimization_barrier

    near = along_x(cat(out16, stay16))
    far = send(cat(out_mine, stay_mine), lambda y, c, x, z, h: (y, c, x + 2, z, h))
    side = cat(near, far)
    other_side = to_core(side)
    planes = []
    for own16, near_at, far_at in ((out16, 0, 32), (stay16, 16, 40)):
        parts = [own16]
        for part in (slice(near_at, near_at + 16), slice(far_at, far_at + 8)):
            parts += by_core(side[part], other_side[part])
        planes.append(cat(*parts))

    got, kept = [], []

    def work(outward, stay):
        sent, rest = product(outward, stay, head)
        got.append(to_hid(sent))
        kept.append(rest)
        return sent

    out, stay = (along_z(a) for a in planes)
    sent = work(planes[:1], planes[1:])
    for step in range(1, 4):
        out_later = along_z(out if step < 3 else jnp.where(first, out[:32], out[32:]))
        out_other = to_core(out)
        stay, sent = after((stay, sent))
        if step > 1:
            stay, got[step - 2] = after((stay, got[step - 2]))
        stay_later = along_z(stay if step < 3 else jnp.where(first, stay[:32], stay[32:]))
        sent = work([out, out_other], [stay, to_core(stay)])
        out, stay = out_later, stay_later
    out_other = to_core(out)
    stay, sent, got[2] = after((stay, sent, got[2]))
    work([cat(*by_core(out, out_other))], [cat(*by_core(stay, to_core(stay)))])

    def rows_of(*shifts):
        return [[(c, dx, shift) for dx in (0, -1, 1, 2) for c in range(NC)] for shift in shifts]

    places = [rows_of((0, 0))] + [rows_of((0, step), (0, -step)) for step in range(1, 4)] + [rows_of((4, 0))]
    logits, stats = join(places, got, kept)

    def merge(pairs):
        best = jnp.max(pairs[:, 0], axis=0)
        return jnp.stack([best, jnp.sum(pairs[:, 1] * jnp.exp(pairs[:, 0] - best), axis=0)])

    pair = stats[:2]
    section = [pair] + [
        send(pair, lambda y, c, x, z, h: (y + dy, c + dc, x, z, h)) for dy, dc in ((0, 1), (1, 0), (1, 1))
    ]
    pair = merge(jnp.stack(section))
    every = lax.all_to_all(jnp.broadcast_to(pair[None], (NX * NZ, 2, ROWS)), ("x", "z"), 0, 0, tiled=True)
    top, total = merge(every)
    return logits - top[:, None] - jnp.log(total)[:, None]


def solution(mesh):
    fine = Mesh(mesh.devices.reshape(SIZES), AXES)
    rows = ("yh", "core", "x", "z")
    return jax.shard_map(
        local,
        mesh=fine,
        in_specs=(P(rows, "h"), P("h"), P(rows, "h")),
        out_specs=P("h", rows),
        check_vma=False,
    )
```

time: 134 us -> 113 us (0.84)
  waiting for transfers between devices: 70.2 us -> 41.2 us
  local copies, waits for them, and re-layouts: 3.74 us -> 7.86 us
  starting transfers between devices: 22.7 us -> 25.3 us
  Pallas kernels: 14.4 us -> 16 us
    ppermute x30, waiting for transfers between devices: 70.2 us -> 41.2 us  [send(): return lax.ppermute(value, AXES, pairs)]
    unnamed x4, local copies, waits for them, and re-layouts: 3.6 us -> 7.21 us
    ppermute x30, starting transfers between devices: 22.7 us -> 25.3 us  [send(): return lax.ppermute(value, AXES, pairs)]
    pallas_call x4 -> x6, Pallas kernels: 12.9 us -> 14.4 us  [the longest x5 14.4 us: product(): pl.pallas_call(functools.partial(product_kernel, len(outward)), in_specs=...]
  transfers between devices with their start and end apart: 30 -> 30, of which waited for: 15 -> 15; matrix products, arithmetic and copies ran while one was open for 1% -> 1% of each run, Pallas kernels for 10% -> 13%
where the time goes in v3:
time: 113 us; the launch traced here: 112 us
  waiting for transfers between devices  41.2 us (36%)
  starting transfers between devices  25.3 us (22%)
  blocking collectives  16.3 us (14%)
  Pallas kernels  16 us (14%)
  local copies, waits for them, and re-layouts  7.86 us (7%)
  other arithmetic  4.46 us (4%)
    ppermute x30, waiting for transfers between devices, send(): return lax.ppermute(value, AXES, pairs)  41.2 us
    ppermute x30, starting transfers between devices, send(): return lax.ppermute(value, AXES, pairs)  25.3 us
    all_to_all x1, blocking collectives, local(): lax.all_to_all(jnp.broadcast_to(pair[None], (NX * NZ, 2, ROWS)), ('x', 'z...  16.3 us
    pallas_call x5, Pallas kernels, product(): pl.pallas_call(functools.partial(product_kernel, len(outward)), in_specs=...  14.4 us
    unnamed x4, local copies, waits for them, and re-layouts  7.21 us
  transfers between devices with their start and end apart: 30, of which 15 were waited for; matrix products, arithmetic and copies ran while one was open for 1% of the time, Pallas kernels for 13%

profile of v3, /device:TPU:8, one launch (start us, length us, event | category | flops | bytes accessed | tf_op | source)
XLA Modules:
  0.0 112.0 jit_solution(14388112863057444891)
XLA Ops:
  0.0 0.7 convert_element_type.46
  0.7 1.0 fusion
  1.7 0.1 copy.11
  1.8 0.1 fusion.17
  1.8 0.1 collective-permute-start.1
  1.9 2.4 %collective-permute-start.2 = (bf16[8,3712]{1,0:T(8,128)(2,1)S(1)}, bf16[8,3712]{1,0:T(8,128)(2,1)S(1)}, u32[]{:S(2)}, u32[]{:S(2)}) collective-permute-start(bf16[8,3712]{1,0:T(8,128)(2,1)S(1)} %pad_maximum_fusion.5), channel_id=1, source_target_pairs={{0,192},{1,193},{2,194},{3,195},{4,196},{5,197},{6,198},{7,199},{8... | collective-permute-start | bytes 178184 | tf_op jit(solution)/shard_map/ppermute | solution.py:32
  4.4 1.2 %collective-permute-start = (bf16[8,3712]{1,0:T(8,128)(2,1)S(1)}, bf16[8,3712]{1,0:T(8,128)(2,1)S(1)}, u32[]{:S(2)}, u32[]{:S(2)}) collective-permute-start(bf16[8,3712]{1,0:T(8,128)(2,1)S(1)} %pad_maximum_fusion.5), channel_id=1, source_target_pairs={{0,128},{1,129},{2,130},{3,131},{4,132},{5,133},{6,134},{7,135},{8... | collective-permute-start | bytes 178184 | tf_op jit(solution)/shard_map/ppermute | solution.py:32
  5.6 3.6 %copy-done = bf16[1280,3584]{1,0:T(8,128)(2,1)S(1)} copy-done((bf16[1280,3584]{1,0:T(8,128)(2,1)S(1)}, bf16[1280,3584]{1,0:T(8,128)(2,1)}, u32[]{:S(2)}) %copy-start) | copy-done | bytes 9175064
  9.2 0.5 slice.56
  10.4 0.0 collective-permute-done.2
  10.4 0.0 collective-permute-done
  10.4 0.1 constant_dynamic-update-slice_fusion.3
  10.6 1.6 %collective-permute-start.3 = (bf16[32,3712]{1,0:T(8,128)(2,1)S(1)}, bf16[32,3712]{1,0:T(8,128)(2,1)S(1)}, u32[]{:S(2)}, u32[]{:S(2)}) collective-permute-start(bf16[32,3712]{1,0:T(8,128)(2,1)S(1)} %pad_maximum_fusion.3), channel_id=1, source_target_pairs={{0,16},{1,17},{2,18},{3,19},{4,20},{5,21},{6,22},{7,23},{8,24},{9,... | collective-permute-start | bytes 712712 | tf_op jit(solution)/shard_map/ppermute | solution.py:32
  12.1 2.8 %collective-permute-start.4 = (bf16[16,3712]{1,0:T(8,128)(2,1)S(1)}, bf16[16,3712]{1,0:T(8,128)(2,1)S(1)}, u32[]{:S(2)}, u32[]{:S(2)}) collective-permute-start(bf16[16,3712]{1,0:T(8,128)(2,1)S(1)} %pad_maximum_fusion.4), channel_id=1, source_target_pairs={{0,32},{1,33},{2,34},{3,35},{4,36},{5,37},{6,38},{7,39},{8,40},{9,... | collective-permute-start | bytes 356360 | tf_op jit(solution)/shard_map/ppermute | solution.py:32
  14.9 6.5 %collective-permute-done.4 = bf16[16,3712]{1,0:T(8,128)(2,1)S(1)} collective-permute-done((bf16[16,3712]{1,0:T(8,128)(2,1)S(1)}, bf16[16,3712]{1,0:T(8,128)(2,1)S(1)}, u32[]{:S(2)}, u32[]{:S(2)}) %collective-permute-start.4) | collective-permute-done | bytes 118816 | tf_op jit(solution)/shard_map/ppermute | solution.py:32
  21.5 0.0 collective-permute-done.3
  21.5 0.1 collective-permute-start.5
  21.6 1.7 %collective-permute-done.5 = bf16[48,3712]{1,0:T(8,128)(2,1)S(1)} collective-permute-done((bf16[48,3712]{1,0:T(8,128)(2,1)S(1)}, bf16[48,3712]{1,0:T(8,128)(2,1)S(1)}, u32[]{:S(2)}, u32[]{:S(2)}) %collective-permute-start.5) | collective-permute-done | bytes 356384 | tf_op jit(solution)/shard_map/ppermute | solution.py:32
  23.3 0.1 select_dynamic-update-slice_fusion.1
  23.4 0.1 select_dynamic-update-slice_fusion
  23.5 2.0 %collective-permute-start.8 = (bf16[64,3712]{1,0:T(8,128)(2,1)S(1)}, bf16[64,3712]{1,0:T(8,128)(2,1)S(1)}, u32[]{:S(2)}, u32[]{:S(2)}) collective-permute-start(bf16[64,3712]{1,0:T(8,128)(2,1)S(1)} %get-tuple-element.65.refs_0_), channel_id=1, source_target_pairs={{0,2},{1,3},{2,4},{3,5},{4,6},{5,7},{6,8},{7,9},{8,10},{9,11},{10,... | collective-permute-start | bytes 1425416 | tf_op jit(solution)/shard_map/ppermute | solution.py:32
  25.5 2.0 %collective-permute-start.6 = (bf16[64,3712]{1,0:T(8,128)(2,1)S(1)}, bf16[64,3712]{1,0:T(8,128)(2,1)S(1)}, u32[]{:S(2)}, u32[]{:S(2)}) collective-permute-start(bf16[64,3712]{1,0:T(8,128)(2,1)S(1)} %select_dynamic-update-slice_fusion.6.refs_1_), channel_id=1, source_target_pairs={{0,2},{1,3},{2,4},{3,5},{4,6},{5,7},{6,8},{7,9},{8,10},{9,11},{10,... | collective-permute-start | bytes 1425416 | tf_op jit(solution)/shard_map/ppermute | solution.py:32
  27.5 8.5 %collective-permute-done.8.refs_0_ = bf16[64,3712]{1,0:T(8,128)(2,1)S(1)} collective-permute-done((bf16[64,3712]{1,0:T(8,128)(2,1)S(1)}, bf16[64,3712]{1,0:T(8,128)(2,1)S(1)}, u32[]{:S(2)}, u32[]{:S(2)}) %collective-permute-start.8) | collective-permute-done | bytes 475168 | tf_op jit(solution)/shard_map/ppermute | solution.py:32
  36.1 0.0 collective-permute-start.13
  36.1 3.6 %copy-done.1 = bf16[1280,3584]{1,0:T(8,128)(2,1)S(1)} copy-done((bf16[1280,3584]{1,0:T(8,128)(2,1)S(1)}, bf16[1280,3584]{1,0:T(8,128)(2,1)}, u32[]{:S(2)}) %copy-start.1) | copy-done | bytes 9175064
  39.7 3.1 %product.5 = (bf16[64,1408]{1,0:T(8,128)(2,1)S(1)}, f32[64,1408]{1,0:T(8,128)S(1)}) custom-call(bf16[64,3712]{1,0:T(8,128)(2,1)S(1)} %get-tuple-element.65.refs_0_, bf16[64,3712]{1,0:T(8,128)(2,1)S(1)} %select_dynamic-update-slice_fusion.6.refs_1_, bf16[1280,3584]{1,0:T(8,128)(2,1)S(1)} %copy-done.1), custom_call_target="tpu_custom_call" | custom-call | flops 1 | bytes 1 | tf_op jit(solution)/shard_map/product/pallas_call | solution.py:104
  42.8 0.0 collective-permute-done.6.refs_2_
  42.8 2.0 %collective-permute-start.9 = (bf16[64,3712]{1,0:T(8,128)(2,1)S(1)}, bf16[64,3712]{1,0:T(8,128)(2,1)S(1)}, u32[]{:S(2)}, u32[]{:S(2)}) collective-permute-start(bf16[64,3712]{1,0:T(8,128)(2,1)S(1)} %collective-permute-done.8.refs_0_), channel_id=1, source_target_pairs={{0,64},{1,65},{2,66},{3,67},{4,68},{5,69},{6,70},{7,71},{8,72},{9,... | collective-permute-start | bytes 1425416 | tf_op jit(solution)/shard_map/ppermute | solution.py:32
  44.8 0.1 collective-permute-start.10
  44.9 1.3 %collective-permute-done.13.refs_0_ = bf16[64,3712]{1,0:T(8,128)(2,1)S(1)} collective-permute-done((bf16[64,3712]{1,0:T(8,128)(2,1)S(1)}, bf16[64,3712]{1,0:T(8,128)(2,1)S(1)}, u32[]{:S(2)}, u32[]{:S(2)}) %collective-permute-start.13) | collective-permute-done | bytes 475168 | tf_op jit(solution)/shard_map/ppermute | solution.py:32
  46.2 0.0 collective-permute-start.18
  46.2 1.0 collective-permute-start.11
  47.3 2.7 %product.6 = (bf16[128,1408]{1,0:T(8,128)(2,1)S(1)}, f32[128,1408]{1,0:T(8,128)S(1)}) custom-call(bf16[64,3712]{1,0:T(8,128)(2,1)S(1)} %collective-permute-done.8.refs_0_, bf16[64,3712]{1,0:T(8,128)(2,1)S(1)} %collective-permute-done.9.refs_1_, bf16[64,3712]{1,0:T(8,128)(2,1)S(1)} %collective-permute-done.6.refs_2_, ...), custom_call_target="tpu_custom_call" | custom-call | flops 1 | bytes 1 | tf_op jit(solution)/shard_map/product/pallas_call | solution.py:104
  50.0 1.1 collective-permute-start.16
  51.1 3.7 %collective-permute-done.7.refs_2_ = bf16[64,3712]{1,0:T(8,128)(2,1)S(1)} collective-permute-done((bf16[64,3712]{1,0:T(8,128)(2,1)S(1)}, bf16[64,3712]{1,0:T(8,128)(2,1)S(1)}, u32[]{:S(2)}, u32[]{:S(2)}) %collective-permute-start.7) | collective-permute-done | bytes 475168 | tf_op jit(solution)/shard_map/ppermute | solution.py:32
  54.8 1.1 %collective-permute-start.12 = (bf16[64,3712]{1,0:T(8,128)(2,1)S(1)}, bf16[64,3712]{1,0:T(8,128)(2,1)S(1)}, u32[]{:S(2)}, u32[]{:S(2)}) collective-permute-start(bf16[64,3712]{1,0:T(8,128)(2,1)S(1)} %collective-permute-done.7.refs_2_), channel_id=1, source_target_pairs={{0,2},{1,3},{2,4},{3,5},{4,6},{5,7},{6,8},{7,9},{8,10},{9,11},{10,... | collective-permute-start | bytes 1425416 | tf_op jit(solution)/shard_map/ppermute | solution.py:32
  56.0 3.9 %collective-permute-done.18.refs_0_ = bf16[64,3712]{1,0:T(8,128)(2,1)S(1)} collective-permute-done((bf16[64,3712]{1,0:T(8,128)(2,1)S(1)}, bf16[64,3712]{1,0:T(8,128)(2,1)S(1)}, u32[]{:S(2)}, u32[]{:S(2)}) %collective-permute-start.18) | collective-permute-done | bytes 475168 | tf_op jit(solution)/shard_map/ppermute | solution.py:32
  59.9 0.1 collective-permute-start.23
  60.0 2.7 %product.7 = (bf16[128,1408]{1,0:T(8,128)(2,1)S(1)}, f32[128,1408]{1,0:T(8,128)S(1)}) custom-call(bf16[64,3712]{1,0:T(8,128)(2,1)S(1)} %collective-permute-done.13.refs_0_, bf16[64,3712]{1,0:T(8,128)(2,1)S(1)} %collective-permute-done.14.refs_1_, bf16[64,3712]{1,0:T(8,128)(2,1)S(1)} %collective-permute-done.7.refs_2_, ...), custom_call_target="tpu_custom_call" | custom-call | flops 1 | bytes 1 | tf_op jit(solution)/shard_map/product/pallas_call | solution.py:104
  62.8 1.1 collective-permute-start.21
  63.9 1.1 collective-permute-done.12.refs_2_
  65.0 0.5 collective-permute-start.19
  65.5 0.1 collective-permute-start.17
  65.6 1.9 %collective-permute-done.23 = bf16[32,3712]{1,0:T(8,128)(2,1)S(1)} collective-permute-done((bf16[32,3712]{1,0:T(8,128)(2,1)S(1)}, bf16[32,3712]{1,0:T(8,128)(2,1)S(1)}, u32[]{:S(2)}, u32[]{:S(2)}) %collective-permute-start.23) | collective-permute-done | bytes 237600 | tf_op jit(solution)/shard_map/ppermute | solution.py:32
  67.5 2.7 %product.8 = (bf16[128,1408]{1,0:T(8,128)(2,1)S(1)}, f32[128,1408]{1,0:T(8,128)S(1)}) custom-call(bf16[64,3712]{1,0:T(8,128)(2,1)S(1)} %collective-permute-done.18.refs_0_, bf16[64,3712]{1,0:T(8,128)(2,1)S(1)} %collective-permute-done.19.refs_1_, bf16[64,3712]{1,0:T(8,128)(2,1)S(1)} %collective-permute-done.12.refs_2_, ...), custom_call_target="tpu_custom_call" | custom-call | flops 1 | bytes 1 | tf_op jit(solution)/shard_map/product/pallas_call | solution.py:104
  70.3 1.1 collective-permute-start.22
  71.4 1.5 %collective-permute-done.17 = bf16[32,3712]{1,0:T(8,128)(2,1)S(1)} collective-permute-done((bf16[32,3712]{1,0:T(8,128)(2,1)S(1)}, bf16[32,3712]{1,0:T(8,128)(2,1)S(1)}, u32[]{:S(2)}, u32[]{:S(2)}) %collective-permute-start.17) | collective-permute-done | bytes 237600 | tf_op jit(solution)/shard_map/ppermute | solution.py:32
  72.9 0.6 collective-permute-done.21.refs_2_
  73.5 0.0 collective-permute-start.25
  73.6 1.4 %collective-permute-done.25 = bf16[32,3712]{1,0:T(8,128)(2,1)S(1)} collective-permute-done((bf16[32,3712]{1,0:T(8,128)(2,1)S(1)}, bf16[32,3712]{1,0:T(8,128)(2,1)S(1)}, u32[]{:S(2)}, u32[]{:S(2)}) %collective-permute-start.25) | collective-permute-done | bytes 237600 | tf_op jit(solution)/shard_map/ppermute | solution.py:32
  75.0 0.1 broadcast_select_fusion.1
  75.1 0.1 pad_maximum_fusion
  75.2 3.1 %product.9 = (bf16[64,1408]{1,0:T(8,128)(2,1)S(1)}, f32[64,1408]{1,0:T(8,128)S(1)}) custom-call(bf16[64,3712]{1,0:T(8,128)(2,1)S(1)} %get-tuple-element.85.refs_0_, bf16[64,3712]{1,0:T(8,128)(2,1)S(1)} %get-tuple-element.86.refs_1_, bf16[1280,3584]{1,0:T(8,128)(2,1)S(1)} %copy-done.1), custom_call_target="tpu_custom_call" | custom-call | flops 1 | bytes 1 | tf_op jit(solution)/shard_map/product/pallas_call | solution.py:104
  78.3 1.1 collective-permute-start.26
  79.4 2.0 %collective-permute-done.22.refs_3_ = bf16[128,1408]{1,0:T(8,128)(2,1)S(1)} collective-permute-done((bf16[128,1408]{1,0:T(8,128)(2,1)S(1)}, bf16[128,1408]{1,0:T(8,128)(2,1)S(1)}, u32[]{:S(2)}, u32[]{:S(2)}) %collective-permute-start.22) | collective-permute-done | bytes 360480 | tf_op jit(solution)/shard_map/ppermute | solution.py:32
  81.3 3.8 %collective-permute-done.26.refs_4_ = bf16[64,1408]{1,0:T(8,128)(2,1)S(1)} collective-permute-done((bf16[64,1408]{1,0:T(8,128)(2,1)S(1)}, bf16[64,1408]{1,0:T(8,128)(2,1)S(1)}, u32[]{:S(2)}, u32[]{:S(2)}) %collective-permute-start.26) | collective-permute-done | bytes 180256 | tf_op jit(solution)/shard_map/ppermute | solution.py:32
  85.1 1.5 %join.1 = (f32[512,1280]{1,0:T(8,128)S(1)}, f32[8,512]{1,0:T(8,128)S(1)}) custom-call(bf16[64,1408]{1,0:T(8,128)(2,1)S(1)} %collective-permute-done.11.refs_0_, bf16[128,1408]{1,0:T(8,128)(2,1)S(1)} %collective-permute-done.16.refs_1_, bf16[128,1408]{1,0:T(8,128)(2,1)S(1)} %collective-permute-done.21.refs_2_, ...), custom_call_target="tpu_custom_call" | custom-call | tf_op jit(solution)/shard_map/join/pallas_call | solution.py:160
  86.7 2.4 %collective-permute-start.28 = (f32[2,512]{1,0:T(2,128)S(1)}, f32[2,512]{1,0:T(2,128)S(1)}, u32[]{:S(2)}, u32[]{:S(2)}) collective-permute-start(f32[2,512]{1,0:T(2,128)S(1)} %get-tuple-element.81), channel_id=1, source_target_pairs={{0,128},{1,129},{2,130},{3,131},{4,132},{5,133},{6,134},{7,135},{8... | collective-permute-start | bytes 12296 | tf_op jit(solution)/shard_map/ppermute | solution.py:32
  89.0 1.3 %collective-permute-start.29 = (f32[2,512]{1,0:T(2,128)S(1)}, f32[2,512]{1,0:T(2,128)S(1)}, u32[]{:S(2)}, u32[]{:S(2)}) collective-permute-start(f32[2,512]{1,0:T(2,128)S(1)} %get-tuple-element.81), channel_id=1, source_target_pairs={{0,192},{1,193},{2,194},{3,195},{4,196},{5,197},{6,198},{7,199},{8... | collective-permute-start | bytes 12296 | tf_op jit(solution)/shard_map/ppermute | solution.py:32
  90.4 1.5 %collective-permute-done.28 = f32[2,512]{1,0:T(2,128)S(1)} collective-permute-done((f32[2,512]{1,0:T(2,128)S(1)}, f32[2,512]{1,0:T(2,128)S(1)}, u32[]{:S(2)}, u32[]{:S(2)}) %collective-permute-start.28) | collective-permute-done | bytes 4128 | tf_op jit(solution)/shard_map/ppermute | solution.py:32
  91.8 1.7 %collective-permute-done.29 = f32[2,512]{1,0:T(2,128)S(1)} collective-permute-done((f32[2,512]{1,0:T(2,128)S(1)}, f32[2,512]{1,0:T(2,128)S(1)}, u32[]{:S(2)}, u32[]{:S(2)}) %collective-permute-start.29) | collective-permute-done | bytes 4128 | tf_op jit(solution)/shard_map/ppermute | solution.py:32
  93.7 16.3 %all_to_all.5 = f32[32,2,512]{2,1,0:T(2,128)S(1)} all-to-all(f32[32,2,512]{2,1,0:T(2,128)S(1)} %broadcast_in_dim.35), channel_id=1, replica_groups=mesh['yh'=2,'core'=2,'x'=4,'z'=8,'h'=2] {'x','z'}, dimensions={0} | all-to-all | bytes 262144 | tf_op jit(solution)/shard_map/all_to_all | solution.py:266
  110.0 0.1 slice_reduce_fusion.1
  110.2 1.8 %subtract_subtract_fusion = f32[512,1280]{1,0:T(8,128)} fusion(f32[512,1280]{1,0:T(8,128)S(1)} %get-tuple-element.45, f32[512]{0:T(512)S(1)} %log.7, f32[512]{0:T(512)S(1)} %get-tuple-element.70), kind=kLoop, calls=%fused_computation | loop fusion | flops 1310720 | bytes 5246976 | tf_op jit(solution)/shard_map/sub | solution.py:268
  (41 shorter events, 0.6 us)
Async XLA Ops:
  1.8 8.5 %collective-permute-start.1 = (bf16[8,3712]{1,0:T(8,128)(2,1)S(1)}, bf16[8,3712]{1,0:T(8,128)(2,1)S(1)}, u32[]{:S(2)}, u32[]{:S(2)}) collective-permute-start(bf16[8,3712]{1,0:T(8,128)(2,1)S(1)} %pad_maximum_fusion.5), channel_id=1, source_target_pairs={{0,64},{1,65},{2,66},{3,67},{4,68},{5,69},{6,70},{7,71},{8,72},{9,... | collective-permute-start | bytes 178184 | tf_op jit(solution)/shard_map/ppermute | solution.py:32
  1.9 8.4 %collective-permute-start.2 = (bf16[8,3712]{1,0:T(8,128)(2,1)S(1)}, bf16[8,3712]{1,0:T(8,128)(2,1)S(1)}, u32[]{:S(2)}, u32[]{:S(2)}) collective-permute-start(bf16[8,3712]{1,0:T(8,128)(2,1)S(1)} %pad_maximum_fusion.5), channel_id=1, source_target_pairs={{0,192},{1,193},{2,194},{3,195},{4,196},{5,197},{6,198},{7,199},{8... | collective-permute-start | bytes 178184 | tf_op jit(solution)/shard_map/ppermute | solution.py:32
  4.4 6.0 %collective-permute-start = (bf16[8,3712]{1,0:T(8,128)(2,1)S(1)}, bf16[8,3712]{1,0:T(8,128)(2,1)S(1)}, u32[]{:S(2)}, u32[]{:S(2)}) collective-permute-start(bf16[8,3712]{1,0:T(8,128)(2,1)S(1)} %pad_maximum_fusion.5), channel_id=1, source_target_pairs={{0,128},{1,129},{2,130},{3,131},{4,132},{5,133},{6,134},{7,135},{8... | collective-permute-start | bytes 178184 | tf_op jit(solution)/shard_map/ppermute | solution.py:32
  5.6 3.6 %copy-start = (bf16[1280,3584]{1,0:T(8,128)(2,1)S(1)}, bf16[1280,3584]{1,0:T(8,128)(2,1)}, u32[]{:S(2)}) copy-start(bf16[1280,3584]{1,0:T(8,128)(2,1)} %refs_2_.3) | copy-start | bytes 27525124
  10.6 10.9 %collective-permute-start.3 = (bf16[32,3712]{1,0:T(8,128)(2,1)S(1)}, bf16[32,3712]{1,0:T(8,128)(2,1)S(1)}, u32[]{:S(2)}, u32[]{:S(2)}) collective-permute-start(bf16[32,3712]{1,0:T(8,128)(2,1)S(1)} %pad_maximum_fusion.3), channel_id=1, source_target_pairs={{0,16},{1,17},{2,18},{3,19},{4,20},{5,21},{6,22},{7,23},{8,24},{9,... | collective-permute-start | bytes 712712 | tf_op jit(solution)/shard_map/ppermute | solution.py:32
  12.1 9.3 %collective-permute-start.4 = (bf16[16,3712]{1,0:T(8,128)(2,1)S(1)}, bf16[16,3712]{1,0:T(8,128)(2,1)S(1)}, u32[]{:S(2)}, u32[]{:S(2)}) collective-permute-start(bf16[16,3712]{1,0:T(8,128)(2,1)S(1)} %pad_maximum_fusion.4), channel_id=1, source_target_pairs={{0,32},{1,33},{2,34},{3,35},{4,36},{5,37},{6,38},{7,39},{8,40},{9,... | collective-permute-start | bytes 356360 | tf_op jit(solution)/shard_map/ppermute | solution.py:32
  21.5 1.8 %collective-permute-start.5 = (bf16[48,3712]{1,0:T(8,128)(2,1)S(1)}, bf16[48,3712]{1,0:T(8,128)(2,1)S(1)}, u32[]{:S(2)}, u32[]{:S(2)}) collective-permute-start(bf16[48,3712]{1,0:T(8,128)(2,1)S(1)} %pad_maximum_fusion.2), channel_id=1, source_target_pairs={{0,64},{1,65},{2,66},{3,67},{4,68},{5,69},{6,70},{7,71},{8,72},{9,... | collective-permute-start | bytes 1069064 | tf_op jit(solution)/shard_map/ppermute | solution.py:32
  23.5 12.6 %collective-permute-start.8 = (bf16[64,3712]{1,0:T(8,128)(2,1)S(1)}, bf16[64,3712]{1,0:T(8,128)(2,1)S(1)}, u32[]{:S(2)}, u32[]{:S(2)}) collective-permute-start(bf16[64,3712]{1,0:T(8,128)(2,1)S(1)} %get-tuple-element.65.refs_0_), channel_id=1, source_target_pairs={{0,2},{1,3},{2,4},{3,5},{4,6},{5,7},{6,8},{7,9},{8,10},{9,11},{10,... | collective-permute-start | bytes 1425416 | tf_op jit(solution)/shard_map/ppermute | solution.py:32
  25.5 17.3 %collective-permute-start.6 = (bf16[64,3712]{1,0:T(8,128)(2,1)S(1)}, bf16[64,3712]{1,0:T(8,128)(2,1)S(1)}, u32[]{:S(2)}, u32[]{:S(2)}) collective-permute-start(bf16[64,3712]{1,0:T(8,128)(2,1)S(1)} %select_dynamic-update-slice_fusion.6.refs_1_), channel_id=1, source_target_pairs={{0,2},{1,3},{2,4},{3,5},{4,6},{5,7},{6,8},{7,9},{8,10},{9,11},{10,... | collective-permute-start | bytes 1425416 | tf_op jit(solution)/shard_map/ppermute | solution.py:32
  36.1 10.2 %collective-permute-start.13 = (bf16[64,3712]{1,0:T(8,128)(2,1)S(1)}, bf16[64,3712]{1,0:T(8,128)(2,1)S(1)}, u32[]{:S(2)}, u32[]{:S(2)}) collective-permute-start(bf16[64,3712]{1,0:T(8,128)(2,1)S(1)} %collective-permute-done.8.refs_0_), channel_id=1, source_target_pairs={{0,2},{1,3},{2,4},{3,5},{4,6},{5,7},{6,8},{7,9},{8,10},{9,11},{10,... | collective-permute-start | bytes 1425416 | tf_op jit(solution)/shard_map/ppermute | solution.py:32
  36.1 3.6 %copy-start.1 = (bf16[1280,3584]{1,0:T(8,128)(2,1)S(1)}, bf16[1280,3584]{1,0:T(8,128)(2,1)}, u32[]{:S(2)}) copy-start(bf16[1280,3584]{1,0:T(8,128)(2,1)} %refs_2_.3) | copy-start | bytes 27525124
  42.8 4.4 %collective-permute-start.9 = (bf16[64,3712]{1,0:T(8,128)(2,1)S(1)}, bf16[64,3712]{1,0:T(8,128)(2,1)S(1)}, u32[]{:S(2)}, u32[]{:S(2)}) collective-permute-start(bf16[64,3712]{1,0:T(8,128)(2,1)S(1)} %collective-permute-done.8.refs_0_), channel_id=1, source_target_pairs={{0,64},{1,65},{2,66},{3,67},{4,68},{5,69},{6,70},{7,71},{8,72},{9,... | collective-permute-start | bytes 1425416 | tf_op jit(solution)/shard_map/ppermute | solution.py:32
  44.8 2.4 %collective-permute-start.10 = (bf16[64,3712]{1,0:T(8,128)(2,1)S(1)}, bf16[64,3712]{1,0:T(8,128)(2,1)S(1)}, u32[]{:S(2)}, u32[]{:S(2)}) collective-permute-start(bf16[64,3712]{1,0:T(8,128)(2,1)S(1)} %collective-permute-done.6.refs_2_), channel_id=1, source_target_pairs={{0,64},{1,65},{2,66},{3,67},{4,68},{5,69},{6,70},{7,71},{8,72},{9,... | collective-permute-start | bytes 1425416 | tf_op jit(solution)/shard_map/ppermute | solution.py:32
  44.9 9.9 %collective-permute-start.7 = (bf16[64,3712]{1,0:T(8,128)(2,1)S(1)}, bf16[64,3712]{1,0:T(8,128)(2,1)S(1)}, u32[]{:S(2)}, u32[]{:S(2)}) collective-permute-start(bf16[64,3712]{1,0:T(8,128)(2,1)S(1)} %collective-permute-done.6.refs_2_), channel_id=1, source_target_pairs={{0,2},{1,3},{2,4},{3,5},{4,6},{5,7},{6,8},{7,9},{8,10},{9,11},{10,... | collective-permute-start | bytes 1425416 | tf_op jit(solution)/shard_map/ppermute | solution.py:32
  46.2 13.6 %collective-permute-start.18 = (bf16[64,3712]{1,0:T(8,128)(2,1)S(1)}, bf16[64,3712]{1,0:T(8,128)(2,1)S(1)}, u32[]{:S(2)}, u32[]{:S(2)}) collective-permute-start(bf16[64,3712]{1,0:T(8,128)(2,1)S(1)} %collective-permute-done.13.refs_0_), channel_id=1, source_target_pairs={{0,2},{1,3},{2,4},{3,5},{4,6},{5,7},{6,8},{7,9},{8,10},{9,11},{10,... | collective-permute-start | bytes 1425416 | tf_op jit(solution)/shard_map/ppermute | solution.py:32
  46.2 8.5 %collective-permute-start.11 = (bf16[64,1408]{1,0:T(8,128)(2,1)S(1)}, bf16[64,1408]{1,0:T(8,128)(2,1)S(1)}, u32[]{:S(2)}, u32[]{:S(2)}) collective-permute-start(bf16[64,1408]{1,0:T(8,128)(2,1)S(1)} %get-tuple-element.26), channel_id=1, source_target_pairs={{0,1},{1,0},{2,3},{3,2},{4,5},{5,4},{6,7},{7,6},{8,9},{9,8},{10,11... | collective-permute-start | bytes 540680 | tf_op jit(solution)/shard_map/ppermute | solution.py:32
  50.0 15.0 %collective-permute-start.16 = (bf16[128,1408]{1,0:T(8,128)(2,1)S(1)}, bf16[128,1408]{1,0:T(8,128)(2,1)S(1)}, u32[]{:S(2)}, u32[]{:S(2)}) collective-permute-start(bf16[128,1408]{1,0:T(8,128)(2,1)S(1)} %get-tuple-element.28), channel_id=1, source_target_pairs={{0,1},{1,0},{2,3},{3,2},{4,5},{5,4},{6,7},{7,6},{8,9},{9,8},{10,11... | collective-permute-start | bytes 1081352 | tf_op jit(solution)/shard_map/ppermute | solution.py:32
  54.8 5.2 %collective-permute-start.15 = (bf16[64,3712]{1,0:T(8,128)(2,1)S(1)}, bf16[64,3712]{1,0:T(8,128)(2,1)S(1)}, u32[]{:S(2)}, u32[]{:S(2)}) collective-permute-start(bf16[64,3712]{1,0:T(8,128)(2,1)S(1)} %collective-permute-done.7.refs_2_), channel_id=1, source_target_pairs={{0,64},{1,65},{2,66},{3,67},{4,68},{5,69},{6,70},{7,71},{8,72},{9,... | collective-permute-start | bytes 1425416 | tf_op jit(solution)/shard_map/ppermute | solution.py:32
  54.8 10.2 %collective-permute-start.12 = (bf16[64,3712]{1,0:T(8,128)(2,1)S(1)}, bf16[64,3712]{1,0:T(8,128)(2,1)S(1)}, u32[]{:S(2)}, u32[]{:S(2)}) collective-permute-start(bf16[64,3712]{1,0:T(8,128)(2,1)S(1)} %collective-permute-done.7.refs_2_), channel_id=1, source_target_pairs={{0,2},{1,3},{2,4},{3,5},{4,6},{5,7},{6,8},{7,9},{8,10},{9,11},{10,... | collective-permute-start | bytes 1425416 | tf_op jit(solution)/shard_map/ppermute | solution.py:32
  56.0 4.1 %collective-permute-start.14 = (bf16[64,3712]{1,0:T(8,128)(2,1)S(1)}, bf16[64,3712]{1,0:T(8,128)(2,1)S(1)}, u32[]{:S(2)}, u32[]{:S(2)}) collective-permute-start(bf16[64,3712]{1,0:T(8,128)(2,1)S(1)} %collective-permute-done.13.refs_0_), channel_id=1, source_target_pairs={{0,64},{1,65},{2,66},{3,67},{4,68},{5,69},{6,70},{7,71},{8,72},{9,... | collective-permute-start | bytes 1425416 | tf_op jit(solution)/shard_map/ppermute | solution.py:32
  59.9 7.6 %collective-permute-start.23 = (bf16[32,3712]{1,0:T(8,128)(2,1)S(1)}, bf16[32,3712]{1,0:T(8,128)(2,1)S(1)}, u32[]{:S(2)}, u32[]{:S(2)}) collective-permute-start(bf16[32,3712]{1,0:T(8,128)(2,1)S(1)} %slice_select_fusion), channel_id=1, source_target_pairs={{0,2},{1,3},{2,4},{3,5},{4,6},{5,7},{6,8},{7,9},{8,10},{9,11},{10,... | collective-permute-start | bytes 712712 | tf_op jit(solution)/shard_map/ppermute | solution.py:32
  62.8 10.7 %collective-permute-start.21 = (bf16[128,1408]{1,0:T(8,128)(2,1)S(1)}, bf16[128,1408]{1,0:T(8,128)(2,1)S(1)}, u32[]{:S(2)}, u32[]{:S(2)}) collective-permute-start(bf16[128,1408]{1,0:T(8,128)(2,1)S(1)} %get-tuple-element.32), channel_id=1, source_target_pairs={{0,1},{1,0},{2,3},{3,2},{4,5},{5,4},{6,7},{7,6},{8,9},{9,8},{10,11... | collective-permute-start | bytes 1081352 | tf_op jit(solution)/shard_map/ppermute | solution.py:32
  65.0 2.6 %collective-permute-start.20 = (bf16[64,3712]{1,0:T(8,128)(2,1)S(1)}, bf16[64,3712]{1,0:T(8,128)(2,1)S(1)}, u32[]{:S(2)}, u32[]{:S(2)}) collective-permute-start(bf16[64,3712]{1,0:T(8,128)(2,1)S(1)} %collective-permute-done.12.refs_2_), channel_id=1, source_target_pairs={{0,64},{1,65},{2,66},{3,67},{4,68},{5,69},{6,70},{7,71},{8,72},{9,... | collective-permute-start | bytes 1425416 | tf_op jit(solution)/shard_map/ppermute | solution.py:32
  65.0 2.5 %collective-permute-start.19 = (bf16[64,3712]{1,0:T(8,128)(2,1)S(1)}, bf16[64,3712]{1,0:T(8,128)(2,1)S(1)}, u32[]{:S(2)}, u32[]{:S(2)}) collective-permute-start(bf16[64,3712]{1,0:T(8,128)(2,1)S(1)} %collective-permute-done.18.refs_0_), channel_id=1, source_target_pairs={{0,64},{1,65},{2,66},{3,67},{4,68},{5,69},{6,70},{7,71},{8,72},{9,... | collective-permute-start | bytes 1425416 | tf_op jit(solution)/shard_map/ppermute | solution.py:32
  65.5 7.4 %collective-permute-start.17 = (bf16[32,3712]{1,0:T(8,128)(2,1)S(1)}, bf16[32,3712]{1,0:T(8,128)(2,1)S(1)}, u32[]{:S(2)}, u32[]{:S(2)}) collective-permute-start(bf16[32,3712]{1,0:T(8,128)(2,1)S(1)} %slice_select_fusion.1), channel_id=1, source_target_pairs={{0,2},{1,3},{2,4},{3,5},{4,6},{5,7},{6,8},{7,9},{8,10},{9,11},{10,... | collective-permute-start | bytes 712712 | tf_op jit(solution)/shard_map/ppermute | solution.py:32
  67.5 6.0 %collective-permute-start.24 = (bf16[32,3712]{1,0:T(8,128)(2,1)S(1)}, bf16[32,3712]{1,0:T(8,128)(2,1)S(1)}, u32[]{:S(2)}, u32[]{:S(2)}) collective-permute-start(bf16[32,3712]{1,0:T(8,128)(2,1)S(1)} %collective-permute-done.23), channel_id=1, source_target_pairs={{0,64},{1,65},{2,66},{3,67},{4,68},{5,69},{6,70},{7,71},{8,72},{9,... | collective-permute-start | bytes 712712 | tf_op jit(solution)/shard_map/ppermute | solution.py:32
  70.3 11.0 %collective-permute-start.22 = (bf16[128,1408]{1,0:T(8,128)(2,1)S(1)}, bf16[128,1408]{1,0:T(8,128)(2,1)S(1)}, u32[]{:S(2)}, u32[]{:S(2)}) collective-permute-start(bf16[128,1408]{1,0:T(8,128)(2,1)S(1)} %get-tuple-element.36), channel_id=1, source_target_pairs={{0,1},{1,0},{2,3},{3,2},{4,5},{5,4},{6,7},{7,6},{8,9},{9,8},{10,11... | collective-permute-start | bytes 1081352 | tf_op jit(solution)/shard_map/ppermute | solution.py:32
  73.5 1.5 %collective-permute-start.25 = (bf16[32,3712]{1,0:T(8,128)(2,1)S(1)}, bf16[32,3712]{1,0:T(8,128)(2,1)S(1)}, u32[]{:S(2)}, u32[]{:S(2)}) collective-permute-start(bf16[32,3712]{1,0:T(8,128)(2,1)S(1)} %collective-permute-done.17), channel_id=1, source_target_pairs={{0,64},{1,65},{2,66},{3,67},{4,68},{5,69},{6,70},{7,71},{8,72},{9,... | collective-permute-start | bytes 712712 | tf_op jit(solution)/shard_map/ppermute | solution.py:32
  78.3 6.8 %collective-permute-start.26 = (bf16[64,1408]{1,0:T(8,128)(2,1)S(1)}, bf16[64,1408]{1,0:T(8,128)(2,1)S(1)}, u32[]{:S(2)}, u32[]{:S(2)}) collective-permute-start(bf16[64,1408]{1,0:T(8,128)(2,1)S(1)} %get-tuple-element.39), channel_id=1, source_target_pairs={{0,1},{1,0},{2,3},{3,2},{4,5},{5,4},{6,7},{7,6},{8,9},{9,8},{10,11... | collective-permute-start | bytes 540680 | tf_op jit(solution)/shard_map/ppermute | solution.py:32
  86.7 5.2 %collective-permute-start.28 = (f32[2,512]{1,0:T(2,128)S(1)}, f32[2,512]{1,0:T(2,128)S(1)}, u32[]{:S(2)}, u32[]{:S(2)}) collective-permute-start(f32[2,512]{1,0:T(2,128)S(1)} %get-tuple-element.81), channel_id=1, source_target_pairs={{0,128},{1,129},{2,130},{3,131},{4,132},{5,133},{6,134},{7,135},{8... | collective-permute-start | bytes 12296 | tf_op jit(solution)/shard_map/ppermute | solution.py:32
  89.0 2.8 %collective-permute-start.27 = (f32[2,512]{1,0:T(2,128)S(1)}, f32[2,512]{1,0:T(2,128)S(1)}, u32[]{:S(2)}, u32[]{:S(2)}) collective-permute-start(f32[2,512]{1,0:T(2,128)S(1)} %get-tuple-element.81), channel_id=1, source_target_pairs={{0,64},{1,65},{2,66},{3,67},{4,68},{5,69},{6,70},{7,71},{8,72},{9,... | collective-permute-start | bytes 12296 | tf_op jit(solution)/shard_map/ppermute | solution.py:32
  89.0 4.5 %collective-permute-start.29 = (f32[2,512]{1,0:T(2,128)S(1)}, f32[2,512]{1,0:T(2,128)S(1)}, u32[]{:S(2)}, u32[]{:S(2)}) collective-permute-start(f32[2,512]{1,0:T(2,128)S(1)} %get-tuple-element.81), channel_id=1, source_target_pairs={{0,192},{1,193},{2,194},{3,195},{4,196},{5,197},{6,198},{7,199},{8... | collective-permute-start | bytes 12296 | tf_op jit(solution)/shard_map/ppermute | solution.py:32

commit v4 on v3

--- a/solution.py
+++ b/solution.py
@@ -153,7 +153,10 @@
         summed = jnp.sum(jnp.exp(logits - top), axis=1, keepdims=True)
         logits_ref[rows, :] = logits
         pair = jnp.where(lane == 0, top, summed)
-        stats_ref[:, rows] = pair.T[:8]
+        pair = pair.T
+        at = begin // step
+        stats_ref[at : at + 1, :] = pair[:1]
+        stats_ref[4 + at : 5 + at, :] = pair[1:2]
 
 
 def join(places, got, kept):
@@ -163,27 +166,12 @@
         out_specs=[WHOLE] * 2,
         out_shape=[
             jax.ShapeDtypeStruct((ROWS, VOCAB), jnp.float32),
-            jax.ShapeDtypeStruct((8, ROWS), jnp.float32),
+            jax.ShapeDtypeStruct((8, LANES), jnp.float32),
         ],
         scratch_shapes=[pltpu.VMEM((ROWS, VOCAB + LANES), jnp.float32)],
         compiler_params=pltpu.CompilerParams(vmem_limit_bytes=30 * 2**20),
         name="join",
     )(*got, *kept)
-
-
-def touch_kernel(rows_ref, head_ref, out_ref):
-    out_ref[...] = rows_ref[...]
-
-
-def touch(rows, head):
-    return pl.pallas_call(
-        touch_kernel,
-        in_specs=[WHOLE] * 2,
-        out_specs=WHOLE,
-        out_shape=jax.ShapeDtypeStruct(rows.shape, rows.dtype),
-        compiler_params=pltpu.CompilerParams(vmem_limit_bytes=16 * 2**20),
-        name="touch",
-    )(rows, head)
 
 
 def local(tokens, gain, head):
@@ -205,8 +193,7 @@
     from_y = send(own, lambda y, c, x, z, h: (y + 1, c, x, z, h))
     from_c = to_core(own)
     from_yc = send(own, lambda y, c, x, z, h: (y + 1, c + 1, x, z, h))
-    flag = touch(jnp.full((8, LANES), yh == h, jnp.float32), head)
-    stays = flag[:1, :1] > 0.5
+    stays = yh == h
     out_mine, out_other = jnp.where(stays, from_y, own), jnp.where(stays, from_yc, from_c)
     stay_mine, stay_other = jnp.where(stays, own, from_y), jnp.where(stays, from_c, from_yc)
     out16 = cat(*by_core(out_mine, out_other))
@@ -214,16 +201,12 @@
 
     after = lax.optimization_barrier
 
-    near = along_x(cat(out16, stay16))
-    far = send(cat(out_mine, stay_mine), lambda y, c, x, z, h: (y, c, x + 2, z, h))
-    side = cat(near, far)
-    other_side = to_core(side)
     planes = []
-    for own16, near_at, far_at in ((out16, 0, 32), (stay16, 16, 40)):
-        parts = [own16]
-        for part in (slice(near_at, near_at + 16), slice(far_at, far_at + 8)):
-            parts += by_core(side[part], other_side[part])
-        planes.append(cat(*parts))
+    for own16, own8 in ((out16, out_mine), (stay16, stay_mine)):
+        side = cat(along_x(own16), send(own8, lambda y, c, x, z, h: (y, c, x + 2, z, h)))
+        other_side = to_core(side)
+        parts = by_core(side[:16], other_side[:16]) + by_core(side[16:], other_side[16:])
+        planes.append(cat(own16, *parts))
 
     got, kept = [], []
 
@@ -235,6 +218,7 @@
 
     out, stay = (along_z(a) for a in planes)
     sent = work(planes[:1], planes[1:])
+    out, sent = after((out, sent))
     for step in range(1, 4):
         out_later = along_z(out if step < 3 else jnp.where(first, out[:32], out[32:]))
         out_other = to_core(out)
@@ -255,17 +239,17 @@
     logits, stats = join(places, got, kept)
 
     def merge(pairs):
-        best = jnp.max(pairs[:, 0], axis=0)
-        return jnp.stack([best, jnp.sum(pairs[:, 1] * jnp.exp(pairs[:, 0] - best), axis=0)])
-
-    pair = stats[:2]
-    section = [pair] + [
-        send(pair, lambda y, c, x, z, h: (y + dy, c + dc, x, z, h)) for dy, dc in ((0, 1), (1, 0), (1, 1))
+        best = jnp.max(pairs[:, :4], axis=0)
+        return jnp.concatenate([best, jnp.sum(pairs[:, 4:] * jnp.exp(pairs[:, :4] - best), axis=0)])
+
+    section = [stats] + [
+        send(stats, lambda y, c, x, z, h: (y + dy, c + dc, x, z, h)) for dy, dc in ((0, 1), (1, 0), (1, 1))
     ]
-    pair = merge(jnp.stack(section))
-    every = lax.all_to_all(jnp.broadcast_to(pair[None], (NX * NZ, 2, ROWS)), ("x", "z"), 0, 0, tiled=True)
-    top, total = merge(every)
-    return logits - top[:, None] - jnp.log(total)[:, None]
+    stats = merge(jnp.stack(section))
+    every = lax.all_to_all(jnp.broadcast_to(stats[None], (NX * NZ, 8, LANES)), ("x", "z"), 0, 0, tiled=True)
+    stats = merge(every)
+    top, total = stats[:4].reshape(ROWS, 1), stats[4:].reshape(ROWS, 1)
+    return logits - top - jnp.log(total)
 
 
 def solution(mesh):

time: 113 us -> 109 us (0.965)
  starting transfers between devices: 25.3 us -> 31 us
  waiting for transfers between devices: 41.2 us -> 36.6 us
  local copies, waits for them, and re-layouts: 7.86 us -> 3.71 us
    ppermute x30 -> x33, starting transfers between devices: 25.3 us -> 31 us  [send(): return lax.ppermute(value, AXES, pairs)]
    ppermute x30 -> x33, waiting for transfers between devices: 41.2 us -> 36.6 us  [send(): return lax.ppermute(value, AXES, pairs)]
    unnamed x4, local copies, waits for them, and re-layouts: 7.21 us -> 3.61 us
  transfers between devices with their start and end apart: 30 -> 33, of which waited for: 15 -> 20; matrix products, arithmetic and copies ran while one was open for 1% -> 1% of each run, Pallas kernels for 13% -> 13%
where the time goes in v4:
time: 109 us
  waiting for transfers between devices  36.6 us (34%)
  starting transfers between devices  31 us (28%)
  blocking collectives  17.1 us (16%)
  Pallas kernels  16 us (15%)
  other arithmetic  4.36 us (4%)
  local copies, waits for them, and re-layouts  3.71 us (3%)
    ppermute x33, waiting for transfers between devices, send(): return lax.ppermute(value, AXES, pairs)  36.6 us
    ppermute x33, starting transfers between devices, send(): return lax.ppermute(value, AXES, pairs)  31 us
    all_to_all x1, blocking collectives, local(): lax.all_to_all(jnp.broadcast_to(stats[None], (NX * NZ, 8, LANES)), ('x',...  17.1 us
    pallas_call x5, Pallas kernels, product(): pl.pallas_call(functools.partial(product_kernel, len(outward)), in_specs=...  14.4 us
    unnamed x4, local copies, waits for them, and re-layouts  3.61 us
  transfers between devices with their start and end apart: 33, of which 20 were waited for; matrix products, arithmetic and copies ran while one was open for 1% of the time, Pallas kernels for 13%

profile of v4, /device:TPU:8, one launch (start us, length us, event | category | flops | bytes accessed | tf_op | source)
XLA Modules:
  0.0 109.0 jit_solution(13273864104402289449)
XLA Ops:
  0.0 0.7 convert_element_type.42
  0.7 1.0 fusion
  1.7 0.1 copy.8
  1.8 0.1 fusion.11
  1.8 0.1 collective-permute-start.1
  1.9 2.4 %collective-permute-start.2 = (bf16[8,3712]{1,0:T(8,128)(2,1)S(1)}, bf16[8,3712]{1,0:T(8,128)(2,1)S(1)}, u32[]{:S(2)}, u32[]{:S(2)}) collective-permute-start(bf16[8,3712]{1,0:T(8,128)(2,1)S(1)} %pad_maximum_fusion.6), channel_id=1, source_target_pairs={{0,192},{1,193},{2,194},{3,195},{4,196},{5,197},{6,198},{7,199},{8... | collective-permute-start | bytes 178184 | tf_op jit(solution)/shard_map/ppermute | solution.py:32
  4.4 1.2 %collective-permute-start = (bf16[8,3712]{1,0:T(8,128)(2,1)S(1)}, bf16[8,3712]{1,0:T(8,128)(2,1)S(1)}, u32[]{:S(2)}, u32[]{:S(2)}) collective-permute-start(bf16[8,3712]{1,0:T(8,128)(2,1)S(1)} %pad_maximum_fusion.6), channel_id=1, source_target_pairs={{0,128},{1,129},{2,130},{3,131},{4,132},{5,133},{6,134},{7,135},{8... | collective-permute-start | bytes 178184 | tf_op jit(solution)/shard_map/ppermute | solution.py:32
  5.6 1.6 %collective-permute-done.2 = bf16[8,3712]{1,0:T(8,128)(2,1)S(1)} collective-permute-done((bf16[8,3712]{1,0:T(8,128)(2,1)S(1)}, bf16[8,3712]{1,0:T(8,128)(2,1)S(1)}, u32[]{:S(2)}, u32[]{:S(2)}) %collective-permute-start.2) | collective-permute-done | bytes 59424 | tf_op jit(solution)/shard_map/ppermute | solution.py:32
  7.2 2.8 %collective-permute-done = bf16[8,3712]{1,0:T(8,128)(2,1)S(1)} collective-permute-done((bf16[8,3712]{1,0:T(8,128)(2,1)S(1)}, bf16[8,3712]{1,0:T(8,128)(2,1)S(1)}, u32[]{:S(2)}, u32[]{:S(2)}) %collective-permute-start) | collective-permute-done | bytes 59424 | tf_op jit(solution)/shard_map/ppermute | solution.py:32
  10.1 0.1 constant_dynamic-update-slice_fusion.3
  10.1 3.1 %collective-permute-start.9 = (bf16[8,3712]{1,0:T(8,128)(2,1)S(1)}, bf16[8,3712]{1,0:T(8,128)(2,1)S(1)}, u32[]{:S(2)}, u32[]{:S(2)}) collective-permute-start(bf16[8,3712]{1,0:T(8,128)(2,1)S(1)} %get-tuple-element.51), channel_id=1, source_target_pairs={{0,32},{1,33},{2,34},{3,35},{4,36},{5,37},{6,38},{7,39},{8,40},{9,... | collective-permute-start | bytes 178184 | tf_op jit(solution)/shard_map/ppermute | solution.py:32
  13.2 0.5 collective-permute-start.4
  13.8 1.6 %collective-permute-start.8 = (bf16[16,3712]{1,0:T(8,128)(2,1)S(1)}, bf16[16,3712]{1,0:T(8,128)(2,1)S(1)}, u32[]{:S(2)}, u32[]{:S(2)}) collective-permute-start(bf16[16,3712]{1,0:T(8,128)(2,1)S(1)} %pad_maximum_fusion.5), channel_id=1, source_target_pairs={{0,16},{1,17},{2,18},{3,19},{4,20},{5,21},{6,22},{7,23},{8,24},{9,... | collective-permute-start | bytes 356360 | tf_op jit(solution)/shard_map/ppermute | solution.py:32
  15.4 1.6 %collective-permute-start.3 = (bf16[16,3712]{1,0:T(8,128)(2,1)S(1)}, bf16[16,3712]{1,0:T(8,128)(2,1)S(1)}, u32[]{:S(2)}, u32[]{:S(2)}) collective-permute-start(bf16[16,3712]{1,0:T(8,128)(2,1)S(1)} %pad_maximum_fusion.4), channel_id=1, source_target_pairs={{0,16},{1,17},{2,18},{3,19},{4,20},{5,21},{6,22},{7,23},{8,24},{9,... | collective-permute-start | bytes 356360 | tf_op jit(solution)/shard_map/ppermute | solution.py:32
  17.0 3.3 %collective-permute-done.8 = bf16[16,3712]{1,0:T(8,128)(2,1)S(1)} collective-permute-done((bf16[16,3712]{1,0:T(8,128)(2,1)S(1)}, bf16[16,3712]{1,0:T(8,128)(2,1)S(1)}, u32[]{:S(2)}, u32[]{:S(2)}) %collective-permute-start.8) | collective-permute-done | bytes 118816 | tf_op jit(solution)/shard_map/ppermute | solution.py:32
  20.2 0.1 collective-permute-start.10
  20.3 1.2 %collective-permute-done.3 = bf16[16,3712]{1,0:T(8,128)(2,1)S(1)} collective-permute-done((bf16[16,3712]{1,0:T(8,128)(2,1)S(1)}, bf16[16,3712]{1,0:T(8,128)(2,1)S(1)}, u32[]{:S(2)}, u32[]{:S(2)}) %collective-permute-start.3) | collective-permute-done | bytes 118816 | tf_op jit(solution)/shard_map/ppermute | solution.py:32
  21.5 0.1 collective-permute-start.5
  21.6 0.1 collective-permute-done.10
  21.9 2.0 %collective-permute-start.11 = (bf16[64,3712]{1,0:T(8,128)(2,1)S(1)}, bf16[64,3712]{1,0:T(8,128)(2,1)S(1)}, u32[]{:S(2)}, u32[]{:S(2)}) collective-permute-start(bf16[64,3712]{1,0:T(8,128)(2,1)S(1)} %select_dynamic-update-slice_fusion.4.refs_0_), channel_id=1, source_target_pairs={{0,2},{1,3},{2,4},{3,5},{4,6},{5,7},{6,8},{7,9},{8,10},{9,11},{10,... | collective-permute-start | bytes 1425416 | tf_op jit(solution)/shard_map/ppermute | solution.py:32
  24.0 2.0 %collective-permute-start.6 = (bf16[64,3712]{1,0:T(8,128)(2,1)S(1)}, bf16[64,3712]{1,0:T(8,128)(2,1)S(1)}, u32[]{:S(2)}, u32[]{:S(2)}) collective-permute-start(bf16[64,3712]{1,0:T(8,128)(2,1)S(1)} %select_dynamic-update-slice_fusion.6.refs_1_), channel_id=1, source_target_pairs={{0,2},{1,3},{2,4},{3,5},{4,6},{5,7},{6,8},{7,9},{8,10},{9,11},{10,... | collective-permute-start | bytes 1425416 | tf_op jit(solution)/shard_map/ppermute | solution.py:32
  26.0 3.6 %copy-done = bf16[1280,3584]{1,0:T(8,128)(2,1)S(1)} copy-done((bf16[1280,3584]{1,0:T(8,128)(2,1)S(1)}, bf16[1280,3584]{1,0:T(8,128)(2,1)}, u32[]{:S(2)}) %copy-start) | copy-done | bytes 9175064
  29.6 3.1 %product.5 = (bf16[64,1408]{1,0:T(8,128)(2,1)S(1)}, f32[64,1408]{1,0:T(8,128)S(1)}) custom-call(bf16[64,3712]{1,0:T(8,128)(2,1)S(1)} %select_dynamic-update-slice_fusion.4.refs_0_, bf16[64,3712]{1,0:T(8,128)(2,1)S(1)} %select_dynamic-update-slice_fusion.6.refs_1_, bf16[1280,3584]{1,0:T(8,128)(2,1)S(1)} %copy-done), custom_call_target="tpu_custom_call" | custom-call | flops 1 | bytes 1 | tf_op jit(solution)/shard_map/product/pallas_call | solution.py:104
  32.7 1.7 %collective-permute-done.11.refs_0_ = bf16[64,3712]{1,0:T(8,128)(2,1)S(1)} collective-permute-done((bf16[64,3712]{1,0:T(8,128)(2,1)S(1)}, bf16[64,3712]{1,0:T(8,128)(2,1)S(1)}, u32[]{:S(2)}, u32[]{:S(2)}) %collective-permute-start.11) | collective-permute-done | bytes 475168 | tf_op jit(solution)/shard_map/ppermute | solution.py:32
  34.4 0.3 collective-permute-start.16
  34.7 4.8 %collective-permute-done.6.refs_2_ = bf16[64,3712]{1,0:T(8,128)(2,1)S(1)} collective-permute-done((bf16[64,3712]{1,0:T(8,128)(2,1)S(1)}, bf16[64,3712]{1,0:T(8,128)(2,1)S(1)}, u32[]{:S(2)}, u32[]{:S(2)}) %collective-permute-start.6) | collective-permute-done | bytes 475168 | tf_op jit(solution)/shard_map/ppermute | solution.py:32
  39.5 0.5 collective-permute-start.12
  40.0 4.6 %collective-permute-done.16.refs_0_ = bf16[64,3712]{1,0:T(8,128)(2,1)S(1)} collective-permute-done((bf16[64,3712]{1,0:T(8,128)(2,1)S(1)}, bf16[64,3712]{1,0:T(8,128)(2,1)S(1)}, u32[]{:S(2)}, u32[]{:S(2)}) %collective-permute-start.16) | collective-permute-done | bytes 475168 | tf_op jit(solution)/shard_map/ppermute | solution.py:32
  44.6 0.0 collective-permute-start.21
  44.6 1.3 %collective-permute-start.14 = (bf16[64,1408]{1,0:T(8,128)(2,1)S(1)}, bf16[64,1408]{1,0:T(8,128)(2,1)S(1)}, u32[]{:S(2)}, u32[]{:S(2)}) collective-permute-start(bf16[64,1408]{1,0:T(8,128)(2,1)S(1)} %get-tuple-element.26), channel_id=1, source_target_pairs={{0,1},{1,0},{2,3},{3,2},{4,5},{5,4},{6,7},{7,6},{8,9},{9,8},{10,11... | collective-permute-start | bytes 540680 | tf_op jit(solution)/shard_map/ppermute | solution.py:32
  46.0 2.7 %product.6 = (bf16[128,1408]{1,0:T(8,128)(2,1)S(1)}, f32[128,1408]{1,0:T(8,128)S(1)}) custom-call(bf16[64,3712]{1,0:T(8,128)(2,1)S(1)} %collective-permute-done.11.refs_0_, bf16[64,3712]{1,0:T(8,128)(2,1)S(1)} %collective-permute-done.12.refs_1_, bf16[64,3712]{1,0:T(8,128)(2,1)S(1)} %collective-permute-done.6.refs_2_, ...), custom_call_target="tpu_custom_call" | custom-call | flops 1 | bytes 1 | tf_op jit(solution)/shard_map/product/pallas_call | solution.py:104
  48.7 0.8 collective-permute-start.19
  49.5 0.4 collective-permute-done.7.refs_2_
  49.9 0.9 collective-permute-done.14.refs_0_
  50.8 1.4 %collective-permute-start.18 = (bf16[64,3712]{1,0:T(8,128)(2,1)S(1)}, bf16[64,3712]{1,0:T(8,128)(2,1)S(1)}, u32[]{:S(2)}, u32[]{:S(2)}) collective-permute-start(bf16[64,3712]{1,0:T(8,128)(2,1)S(1)} %collective-permute-done.7.refs_2_), channel_id=1, source_target_pairs={{0,64},{1,65},{2,66},{3,67},{4,68},{5,69},{6,70},{7,71},{8,72},{9,... | collective-permute-start | bytes 1425416 | tf_op jit(solution)/shard_map/ppermute | solution.py:32
  52.2 1.6 %collective-permute-start.17 = (bf16[64,3712]{1,0:T(8,128)(2,1)S(1)}, bf16[64,3712]{1,0:T(8,128)(2,1)S(1)}, u32[]{:S(2)}, u32[]{:S(2)}) collective-permute-start(bf16[64,3712]{1,0:T(8,128)(2,1)S(1)} %collective-permute-done.16.refs_0_), channel_id=1, source_target_pairs={{0,64},{1,65},{2,66},{3,67},{4,68},{5,69},{6,70},{7,71},{8,72},{9,... | collective-permute-start | bytes 1425416 | tf_op jit(solution)/shard_map/ppermute | solution.py:32
  53.8 1.2 %collective-permute-done.21.refs_0_ = bf16[64,3712]{1,0:T(8,128)(2,1)S(1)} collective-permute-done((bf16[64,3712]{1,0:T(8,128)(2,1)S(1)}, bf16[64,3712]{1,0:T(8,128)(2,1)S(1)}, u32[]{:S(2)}, u32[]{:S(2)}) %collective-permute-start.21) | collective-permute-done | bytes 475168 | tf_op jit(solution)/shard_map/ppermute | solution.py:32
  55.0 0.1 collective-permute-start.26
  55.1 0.1 collective-permute-done.17.refs_1_
  55.3 2.7 %product.7 = (bf16[128,1408]{1,0:T(8,128)(2,1)S(1)}, f32[128,1408]{1,0:T(8,128)S(1)}) custom-call(bf16[64,3712]{1,0:T(8,128)(2,1)S(1)} %collective-permute-done.16.refs_0_, bf16[64,3712]{1,0:T(8,128)(2,1)S(1)} %collective-permute-done.17.refs_1_, bf16[64,3712]{1,0:T(8,128)(2,1)S(1)} %collective-permute-done.7.refs_2_, ...), custom_call_target="tpu_custom_call" | custom-call | flops 1 | bytes 1 | tf_op jit(solution)/shard_map/product/pallas_call | solution.py:104
  58.0 2.0 %collective-permute-start.24 = (bf16[128,1408]{1,0:T(8,128)(2,1)S(1)}, bf16[128,1408]{1,0:T(8,128)(2,1)S(1)}, u32[]{:S(2)}, u32[]{:S(2)}) collective-permute-start(bf16[128,1408]{1,0:T(8,128)(2,1)S(1)} %get-tuple-element.32), channel_id=1, source_target_pairs={{0,1},{1,0},{2,3},{3,2},{4,5},{5,4},{6,7},{7,6},{8,9},{9,8},{10,11... | collective-permute-start | bytes 1081352 | tf_op jit(solution)/shard_map/ppermute | solution.py:32
  60.0 2.0 %collective-permute-done.15.refs_2_ = bf16[64,3712]{1,0:T(8,128)(2,1)S(1)} collective-permute-done((bf16[64,3712]{1,0:T(8,128)(2,1)S(1)}, bf16[64,3712]{1,0:T(8,128)(2,1)S(1)}, u32[]{:S(2)}, u32[]{:S(2)}) %collective-permute-start.15) | collective-permute-done | bytes 475168 | tf_op jit(solution)/shard_map/ppermute | solution.py:32
  62.0 0.5 collective-permute-start.22
  62.6 0.7 collective-permute-start.20
  63.3 1.3 %collective-permute-done.26 = bf16[32,3712]{1,0:T(8,128)(2,1)S(1)} collective-permute-done((bf16[32,3712]{1,0:T(8,128)(2,1)S(1)}, bf16[32,3712]{1,0:T(8,128)(2,1)S(1)}, u32[]{:S(2)}, u32[]{:S(2)}) %collective-permute-start.26) | collective-permute-done | bytes 237600 | tf_op jit(solution)/shard_map/ppermute | solution.py:32
  64.6 2.7 %product.8 = (bf16[128,1408]{1,0:T(8,128)(2,1)S(1)}, f32[128,1408]{1,0:T(8,128)S(1)}) custom-call(bf16[64,3712]{1,0:T(8,128)(2,1)S(1)} %collective-permute-done.21.refs_0_, bf16[64,3712]{1,0:T(8,128)(2,1)S(1)} %collective-permute-done.22.refs_1_, bf16[64,3712]{1,0:T(8,128)(2,1)S(1)} %collective-permute-done.15.refs_2_, ...), custom_call_target="tpu_custom_call" | custom-call | flops 1 | bytes 1 | tf_op jit(solution)/shard_map/product/pallas_call | solution.py:104
  67.3 1.9 %collective-permute-start.25 = (bf16[128,1408]{1,0:T(8,128)(2,1)S(1)}, bf16[128,1408]{1,0:T(8,128)(2,1)S(1)}, u32[]{:S(2)}, u32[]{:S(2)}) collective-permute-start(bf16[128,1408]{1,0:T(8,128)(2,1)S(1)} %get-tuple-element.36), channel_id=1, source_target_pairs={{0,1},{1,0},{2,3},{3,2},{4,5},{5,4},{6,7},{7,6},{8,9},{9,8},{10,11... | collective-permute-start | bytes 1081352 | tf_op jit(solution)/shard_map/ppermute | solution.py:32
  69.3 0.7 collective-permute-done.20
  70.0 0.1 broadcast_select_fusion.3
  70.0 1.4 %collective-permute-done.28 = bf16[32,3712]{1,0:T(8,128)(2,1)S(1)} collective-permute-done((bf16[32,3712]{1,0:T(8,128)(2,1)S(1)}, bf16[32,3712]{1,0:T(8,128)(2,1)S(1)}, u32[]{:S(2)}, u32[]{:S(2)}) %collective-permute-start.28) | collective-permute-done | bytes 237600 | tf_op jit(solution)/shard_map/ppermute | solution.py:32
  71.5 0.1 pad_maximum_fusion
  71.6 3.1 %product.9 = (bf16[64,1408]{1,0:T(8,128)(2,1)S(1)}, f32[64,1408]{1,0:T(8,128)S(1)}) custom-call(bf16[64,3712]{1,0:T(8,128)(2,1)S(1)} %get-tuple-element.71.refs_0_, bf16[64,3712]{1,0:T(8,128)(2,1)S(1)} %get-tuple-element.72.refs_1_, bf16[1280,3584]{1,0:T(8,128)(2,1)S(1)} %copy-done.1), custom_call_target="tpu_custom_call" | custom-call | flops 1 | bytes 1 | tf_op jit(solution)/shard_map/product/pallas_call | solution.py:104
  74.7 1.7 %collective-permute-start.29 = (bf16[64,1408]{1,0:T(8,128)(2,1)S(1)}, bf16[64,1408]{1,0:T(8,128)(2,1)S(1)}, u32[]{:S(2)}, u32[]{:S(2)}) collective-permute-start(bf16[64,1408]{1,0:T(8,128)(2,1)S(1)} %get-tuple-element.39), channel_id=1, source_target_pairs={{0,1},{1,0},{2,3},{3,2},{4,5},{5,4},{6,7},{7,6},{8,9},{9,8},{10,11... | collective-permute-start | bytes 540680 | tf_op jit(solution)/shard_map/ppermute | solution.py:32
  76.4 2.4 %collective-permute-done.25.refs_3_ = bf16[128,1408]{1,0:T(8,128)(2,1)S(1)} collective-permute-done((bf16[128,1408]{1,0:T(8,128)(2,1)S(1)}, bf16[128,1408]{1,0:T(8,128)(2,1)S(1)}, u32[]{:S(2)}, u32[]{:S(2)}) %collective-permute-start.25) | collective-permute-done | bytes 360480 | tf_op jit(solution)/shard_map/ppermute | solution.py:32
  78.8 3.5 %collective-permute-done.29.refs_4_ = bf16[64,1408]{1,0:T(8,128)(2,1)S(1)} collective-permute-done((bf16[64,1408]{1,0:T(8,128)(2,1)S(1)}, bf16[64,1408]{1,0:T(8,128)(2,1)S(1)}, u32[]{:S(2)}, u32[]{:S(2)}) %collective-permute-start.29) | collective-permute-done | bytes 180256 | tf_op jit(solution)/shard_map/ppermute | solution.py:32
  82.3 1.5 %join.1 = (f32[512,1280]{1,0:T(8,128)S(1)}, f32[8,128]{1,0:T(8,128)S(1)}) custom-call(bf16[64,1408]{1,0:T(8,128)(2,1)S(1)} %collective-permute-done.14.refs_0_, bf16[128,1408]{1,0:T(8,128)(2,1)S(1)} %collective-permute-done.19.refs_1_, bf16[128,1408]{1,0:T(8,128)(2,1)S(1)} %collective-permute-done.24.refs_2_, ...), custom_call_target="tpu_custom_call" | custom-call | tf_op jit(solution)/shard_map/join/pallas_call | solution.py:163
  83.9 0.9 collective-permute-start.32
  84.8 2.0 %collective-permute-start.31 = (f32[8,128]{1,0:T(8,128)S(1)}, f32[8,128]{1,0:T(8,128)S(1)}, u32[]{:S(2)}, u32[]{:S(2)}) collective-permute-start(f32[8,128]{1,0:T(8,128)S(1)} %get-tuple-element.46), channel_id=1, source_target_pairs={{0,128},{1,129},{2,130},{3,131},{4,132},{5,133},{6,134},{7,135},{8... | collective-permute-start | bytes 12296 | tf_op jit(solution)/shard_map/ppermute | solution.py:32
  86.8 0.5 collective-permute-start.30
  87.3 1.2 %collective-permute-done.32 = f32[8,128]{1,0:T(8,128)S(1)} collective-permute-done((f32[8,128]{1,0:T(8,128)S(1)}, f32[8,128]{1,0:T(8,128)S(1)}, u32[]{:S(2)}, u32[]{:S(2)}) %collective-permute-start.32) | collective-permute-done | bytes 4128 | tf_op jit(solution)/shard_map/ppermute | solution.py:32
  88.5 1.4 %collective-permute-done.31 = f32[8,128]{1,0:T(8,128)S(1)} collective-permute-done((f32[8,128]{1,0:T(8,128)S(1)}, f32[8,128]{1,0:T(8,128)S(1)}, u32[]{:S(2)}, u32[]{:S(2)}) %collective-permute-start.31) | collective-permute-done | bytes 4128 | tf_op jit(solution)/shard_map/ppermute | solution.py:32
  90.0 17.1 %all_to_all.5 = f32[32,8,128]{2,1,0:T(8,128)S(1)} all-to-all(f32[32,8,128]{2,1,0:T(8,128)S(1)} %broadcast_in_dim.2), channel_id=1, replica_groups=mesh['yh'=2,'core'=2,'x'=4,'z'=8,'h'=2] {'x','z'}, dimensions={0} | all-to-all | bytes 262144 | tf_op jit(solution)/shard_map/all_to_all | solution.py:249
  107.1 0.1 fusion.2
  107.2 1.8 %subtract_subtract_fusion = f32[512,1280]{1,0:T(8,128)} fusion(f32[512,1280]{1,0:T(8,128)S(1)} %get-tuple-element.45, f32[512]{0:T(512)S(1)} %log_bitcast_fusion, f32[512]{0:T(512)S(1)} %bitcast.9), kind=kLoop, calls=%fused_computation | loop fusion | flops 1310720 | bytes 5246976 | tf_op jit(solution)/shard_map/sub | solution.py:252
  (47 shorter events, 0.7 us)
Async XLA Ops:
  1.8 3.8 %collective-permute-start.1 = (bf16[8,3712]{1,0:T(8,128)(2,1)S(1)}, bf16[8,3712]{1,0:T(8,128)(2,1)S(1)}, u32[]{:S(2)}, u32[]{:S(2)}) collective-permute-start(bf16[8,3712]{1,0:T(8,128)(2,1)S(1)} %pad_maximum_fusion.6), channel_id=1, source_target_pairs={{0,64},{1,65},{2,66},{3,67},{4,68},{5,69},{6,70},{7,71},{8,72},{9,... | collective-permute-start | bytes 178184 | tf_op jit(solution)/shard_map/ppermute | solution.py:32
  1.9 5.3 %collective-permute-start.2 = (bf16[8,3712]{1,0:T(8,128)(2,1)S(1)}, bf16[8,3712]{1,0:T(8,128)(2,1)S(1)}, u32[]{:S(2)}, u32[]{:S(2)}) collective-permute-start(bf16[8,3712]{1,0:T(8,128)(2,1)S(1)} %pad_maximum_fusion.6), channel_id=1, source_target_pairs={{0,192},{1,193},{2,194},{3,195},{4,196},{5,197},{6,198},{7,199},{8... | collective-permute-start | bytes 178184 | tf_op jit(solution)/shard_map/ppermute | solution.py:32
  4.4 5.7 %collective-permute-start = (bf16[8,3712]{1,0:T(8,128)(2,1)S(1)}, bf16[8,3712]{1,0:T(8,128)(2,1)S(1)}, u32[]{:S(2)}, u32[]{:S(2)}) collective-permute-start(bf16[8,3712]{1,0:T(8,128)(2,1)S(1)} %pad_maximum_fusion.6), channel_id=1, source_target_pairs={{0,128},{1,129},{2,130},{3,131},{4,132},{5,133},{6,134},{7,135},{8... | collective-permute-start | bytes 178184 | tf_op jit(solution)/shard_map/ppermute | solution.py:32
  10.1 6.8 %collective-permute-start.9 = (bf16[8,3712]{1,0:T(8,128)(2,1)S(1)}, bf16[8,3712]{1,0:T(8,128)(2,1)S(1)}, u32[]{:S(2)}, u32[]{:S(2)}) collective-permute-start(bf16[8,3712]{1,0:T(8,128)(2,1)S(1)} %get-tuple-element.51), channel_id=1, source_target_pairs={{0,32},{1,33},{2,34},{3,35},{4,36},{5,37},{6,38},{7,39},{8,40},{9,... | collective-permute-start | bytes 178184 | tf_op jit(solution)/shard_map/ppermute | solution.py:32
  13.2 7.1 %collective-permute-start.4 = (bf16[8,3712]{1,0:T(8,128)(2,1)S(1)}, bf16[8,3712]{1,0:T(8,128)(2,1)S(1)}, u32[]{:S(2)}, u32[]{:S(2)}) collective-permute-start(bf16[8,3712]{1,0:T(8,128)(2,1)S(1)} %get-tuple-element.63), channel_id=1, source_target_pairs={{0,32},{1,33},{2,34},{3,35},{4,36},{5,37},{6,38},{7,39},{8,40},{9,... | collective-permute-start | bytes 178184 | tf_op jit(solution)/shard_map/ppermute | solution.py:32
  13.8 6.4 %collective-permute-start.8 = (bf16[16,3712]{1,0:T(8,128)(2,1)S(1)}, bf16[16,3712]{1,0:T(8,128)(2,1)S(1)}, u32[]{:S(2)}, u32[]{:S(2)}) collective-permute-start(bf16[16,3712]{1,0:T(8,128)(2,1)S(1)} %pad_maximum_fusion.5), channel_id=1, source_target_pairs={{0,16},{1,17},{2,18},{3,19},{4,20},{5,21},{6,22},{7,23},{8,24},{9,... | collective-permute-start | bytes 356360 | tf_op jit(solution)/shard_map/ppermute | solution.py:32
  15.4 6.1 %collective-permute-start.3 = (bf16[16,3712]{1,0:T(8,128)(2,1)S(1)}, bf16[16,3712]{1,0:T(8,128)(2,1)S(1)}, u32[]{:S(2)}, u32[]{:S(2)}) collective-permute-start(bf16[16,3712]{1,0:T(8,128)(2,1)S(1)} %pad_maximum_fusion.4), channel_id=1, source_target_pairs={{0,16},{1,17},{2,18},{3,19},{4,20},{5,21},{6,22},{7,23},{8,24},{9,... | collective-permute-start | bytes 356360 | tf_op jit(solution)/shard_map/ppermute | solution.py:32
  20.2 1.5 %collective-permute-start.10 = (bf16[24,3712]{1,0:T(8,128)(2,1)S(1)}, bf16[24,3712]{1,0:T(8,128)(2,1)S(1)}, u32[]{:S(2)}, u32[]{:S(2)}) collective-permute-start(bf16[24,3712]{1,0:T(8,128)(2,1)S(1)} %pad_maximum_fusion.3), channel_id=1, source_target_pairs={{0,64},{1,65},{2,66},{3,67},{4,68},{5,69},{6,70},{7,71},{8,72},{9,... | collective-permute-start | bytes 534536 | tf_op jit(solution)/shard_map/ppermute | solution.py:32
  21.5 2.3 %collective-permute-start.5 = (bf16[24,3712]{1,0:T(8,128)(2,1)S(1)}, bf16[24,3712]{1,0:T(8,128)(2,1)S(1)}, u32[]{:S(2)}, u32[]{:S(2)}) collective-permute-start(bf16[24,3712]{1,0:T(8,128)(2,1)S(1)} %pad_maximum_fusion.2), channel_id=1, source_target_pairs={{0,64},{1,65},{2,66},{3,67},{4,68},{5,69},{6,70},{7,71},{8,72},{9,... | collective-permute-start | bytes 534536 | tf_op jit(solution)/shard_map/ppermute | solution.py:32
  21.9 12.6 %collective-permute-start.11 = (bf16[64,3712]{1,0:T(8,128)(2,1)S(1)}, bf16[64,3712]{1,0:T(8,128)(2,1)S(1)}, u32[]{:S(2)}, u32[]{:S(2)}) collective-permute-start(bf16[64,3712]{1,0:T(8,128)(2,1)S(1)} %select_dynamic-update-slice_fusion.4.refs_0_), channel_id=1, source_target_pairs={{0,2},{1,3},{2,4},{3,5},{4,6},{5,7},{6,8},{7,9},{8,10},{9,11},{10,... | collective-permute-start | bytes 1425416 | tf_op jit(solution)/shard_map/ppermute | solution.py:32
  24.0 15.5 %collective-permute-start.6 = (bf16[64,3712]{1,0:T(8,128)(2,1)S(1)}, bf16[64,3712]{1,0:T(8,128)(2,1)S(1)}, u32[]{:S(2)}, u32[]{:S(2)}) collective-permute-start(bf16[64,3712]{1,0:T(8,128)(2,1)S(1)} %select_dynamic-update-slice_fusion.6.refs_1_), channel_id=1, source_target_pairs={{0,2},{1,3},{2,4},{3,5},{4,6},{5,7},{6,8},{7,9},{8,10},{9,11},{10,... | collective-permute-start | bytes 1425416 | tf_op jit(solution)/shard_map/ppermute | solution.py:32
  26.0 3.6 %copy-start = (bf16[1280,3584]{1,0:T(8,128)(2,1)S(1)}, bf16[1280,3584]{1,0:T(8,128)(2,1)}, u32[]{:S(2)}) copy-start(bf16[1280,3584]{1,0:T(8,128)(2,1)} %refs_2_.3) | copy-start | bytes 27525124
  29.6 16.4 %copy-start.1 = (bf16[1280,3584]{1,0:T(8,128)(2,1)S(1)}, bf16[1280,3584]{1,0:T(8,128)(2,1)}, u32[]{:S(2)}) copy-start(bf16[1280,3584]{1,0:T(8,128)(2,1)} %refs_2_.3) | copy-start | bytes 27525124
  34.4 10.2 %collective-permute-start.16 = (bf16[64,3712]{1,0:T(8,128)(2,1)S(1)}, bf16[64,3712]{1,0:T(8,128)(2,1)S(1)}, u32[]{:S(2)}, u32[]{:S(2)}) collective-permute-start(bf16[64,3712]{1,0:T(8,128)(2,1)S(1)} %collective-permute-done.11.refs_0_), channel_id=1, source_target_pairs={{0,2},{1,3},{2,4},{3,5},{4,6},{5,7},{6,8},{7,9},{8,10},{9,11},{10,... | collective-permute-start | bytes 1425416 | tf_op jit(solution)/shard_map/ppermute | solution.py:32
  39.5 6.4 %collective-permute-start.13 = (bf16[64,3712]{1,0:T(8,128)(2,1)S(1)}, bf16[64,3712]{1,0:T(8,128)(2,1)S(1)}, u32[]{:S(2)}, u32[]{:S(2)}) collective-permute-start(bf16[64,3712]{1,0:T(8,128)(2,1)S(1)} %collective-permute-done.6.refs_2_), channel_id=1, source_target_pairs={{0,64},{1,65},{2,66},{3,67},{4,68},{5,69},{6,70},{7,71},{8,72},{9,... | collective-permute-start | bytes 1425416 | tf_op jit(solution)/shard_map/ppermute | solution.py:32
  39.5 6.4 %collective-permute-start.12 = (bf16[64,3712]{1,0:T(8,128)(2,1)S(1)}, bf16[64,3712]{1,0:T(8,128)(2,1)S(1)}, u32[]{:S(2)}, u32[]{:S(2)}) collective-permute-start(bf16[64,3712]{1,0:T(8,128)(2,1)S(1)} %collective-permute-done.11.refs_0_), channel_id=1, source_target_pairs={{0,64},{1,65},{2,66},{3,67},{4,68},{5,69},{6,70},{7,71},{8,72},{9,... | collective-permute-start | bytes 1425416 | tf_op jit(solution)/shard_map/ppermute | solution.py:32
  40.0 9.9 %collective-permute-start.7 = (bf16[64,3712]{1,0:T(8,128)(2,1)S(1)}, bf16[64,3712]{1,0:T(8,128)(2,1)S(1)}, u32[]{:S(2)}, u32[]{:S(2)}) collective-permute-start(bf16[64,3712]{1,0:T(8,128)(2,1)S(1)} %collective-permute-done.6.refs_2_), channel_id=1, source_target_pairs={{0,2},{1,3},{2,4},{3,5},{4,6},{5,7},{6,8},{7,9},{8,10},{9,11},{10,... | collective-permute-start | bytes 1425416 | tf_op jit(solution)/shard_map/ppermute | solution.py:32
  44.6 10.4 %collective-permute-start.21 = (bf16[64,3712]{1,0:T(8,128)(2,1)S(1)}, bf16[64,3712]{1,0:T(8,128)(2,1)S(1)}, u32[]{:S(2)}, u32[]{:S(2)}) collective-permute-start(bf16[64,3712]{1,0:T(8,128)(2,1)S(1)} %collective-permute-done.16.refs_0_), channel_id=1, source_target_pairs={{0,2},{1,3},{2,4},{3,5},{4,6},{5,7},{6,8},{7,9},{8,10},{9,11},{10,... | collective-permute-start | bytes 1425416 | tf_op jit(solution)/shard_map/ppermute | solution.py:32
  44.6 6.2 %collective-permute-start.14 = (bf16[64,1408]{1,0:T(8,128)(2,1)S(1)}, bf16[64,1408]{1,0:T(8,128)(2,1)S(1)}, u32[]{:S(2)}, u32[]{:S(2)}) collective-permute-start(bf16[64,1408]{1,0:T(8,128)(2,1)S(1)} %get-tuple-element.26), channel_id=1, source_target_pairs={{0,1},{1,0},{2,3},{3,2},{4,5},{5,4},{6,7},{7,6},{8,9},{9,8},{10,11... | collective-permute-start | bytes 540680 | tf_op jit(solution)/shard_map/ppermute | solution.py:32
  48.7 13.3 %collective-permute-start.19 = (bf16[128,1408]{1,0:T(8,128)(2,1)S(1)}, bf16[128,1408]{1,0:T(8,128)(2,1)S(1)}, u32[]{:S(2)}, u32[]{:S(2)}) collective-permute-start(bf16[128,1408]{1,0:T(8,128)(2,1)S(1)} %get-tuple-element.28), channel_id=1, source_target_pairs={{0,1},{1,0},{2,3},{3,2},{4,5},{5,4},{6,7},{7,6},{8,9},{9,8},{10,11... | collective-permute-start | bytes 1081352 | tf_op jit(solution)/shard_map/ppermute | solution.py:32
  50.8 4.5 %collective-permute-start.18 = (bf16[64,3712]{1,0:T(8,128)(2,1)S(1)}, bf16[64,3712]{1,0:T(8,128)(2,1)S(1)}, u32[]{:S(2)}, u32[]{:S(2)}) collective-permute-start(bf16[64,3712]{1,0:T(8,128)(2,1)S(1)} %collective-permute-done.7.refs_2_), channel_id=1, source_target_pairs={{0,64},{1,65},{2,66},{3,67},{4,68},{5,69},{6,70},{7,71},{8,72},{9,... | collective-permute-start | bytes 1425416 | tf_op jit(solution)/shard_map/ppermute | solution.py:32
  52.2 9.9 %collective-permute-start.15 = (bf16[64,3712]{1,0:T(8,128)(2,1)S(1)}, bf16[64,3712]{1,0:T(8,128)(2,1)S(1)}, u32[]{:S(2)}, u32[]{:S(2)}) collective-permute-start(bf16[64,3712]{1,0:T(8,128)(2,1)S(1)} %collective-permute-done.7.refs_2_), channel_id=1, source_target_pairs={{0,2},{1,3},{2,4},{3,5},{4,6},{5,7},{6,8},{7,9},{8,10},{9,11},{10,... | collective-permute-start | bytes 1425416 | tf_op jit(solution)/shard_map/ppermute | solution.py:32
  52.2 3.1 %collective-permute-start.17 = (bf16[64,3712]{1,0:T(8,128)(2,1)S(1)}, bf16[64,3712]{1,0:T(8,128)(2,1)S(1)}, u32[]{:S(2)}, u32[]{:S(2)}) collective-permute-start(bf16[64,3712]{1,0:T(8,128)(2,1)S(1)} %collective-permute-done.16.refs_0_), channel_id=1, source_target_pairs={{0,64},{1,65},{2,66},{3,67},{4,68},{5,69},{6,70},{7,71},{8,72},{9,... | collective-permute-start | bytes 1425416 | tf_op jit(solution)/shard_map/ppermute | solution.py:32
  55.0 9.5 %collective-permute-start.26 = (bf16[32,3712]{1,0:T(8,128)(2,1)S(1)}, bf16[32,3712]{1,0:T(8,128)(2,1)S(1)}, u32[]{:S(2)}, u32[]{:S(2)}) collective-permute-start(bf16[32,3712]{1,0:T(8,128)(2,1)S(1)} %slice_select_fusion), channel_id=1, source_target_pairs={{0,2},{1,3},{2,4},{3,5},{4,6},{5,7},{6,8},{7,9},{8,10},{9,11},{10,... | collective-permute-start | bytes 712712 | tf_op jit(solution)/shard_map/ppermute | solution.py:32
  58.0 12.0 %collective-permute-start.24 = (bf16[128,1408]{1,0:T(8,128)(2,1)S(1)}, bf16[128,1408]{1,0:T(8,128)(2,1)S(1)}, u32[]{:S(2)}, u32[]{:S(2)}) collective-permute-start(bf16[128,1408]{1,0:T(8,128)(2,1)S(1)} %get-tuple-element.32), channel_id=1, source_target_pairs={{0,1},{1,0},{2,3},{3,2},{4,5},{5,4},{6,7},{7,6},{8,9},{9,8},{10,11... | collective-permute-start | bytes 1081352 | tf_op jit(solution)/shard_map/ppermute | solution.py:32
  62.0 2.6 %collective-permute-start.23 = (bf16[64,3712]{1,0:T(8,128)(2,1)S(1)}, bf16[64,3712]{1,0:T(8,128)(2,1)S(1)}, u32[]{:S(2)}, u32[]{:S(2)}) collective-permute-start(bf16[64,3712]{1,0:T(8,128)(2,1)S(1)} %collective-permute-done.15.refs_2_), channel_id=1, source_target_pairs={{0,64},{1,65},{2,66},{3,67},{4,68},{5,69},{6,70},{7,71},{8,72},{9,... | collective-permute-start | bytes 1425416 | tf_op jit(solution)/shard_map/ppermute | solution.py:32
  62.0 2.5 %collective-permute-start.22 = (bf16[64,3712]{1,0:T(8,128)(2,1)S(1)}, bf16[64,3712]{1,0:T(8,128)(2,1)S(1)}, u32[]{:S(2)}, u32[]{:S(2)}) collective-permute-start(bf16[64,3712]{1,0:T(8,128)(2,1)S(1)} %collective-permute-done.21.refs_0_), channel_id=1, source_target_pairs={{0,64},{1,65},{2,66},{3,67},{4,68},{5,69},{6,70},{7,71},{8,72},{9,... | collective-permute-start | bytes 1425416 | tf_op jit(solution)/shard_map/ppermute | solution.py:32
  62.6 7.4 %collective-permute-start.20 = (bf16[32,3712]{1,0:T(8,128)(2,1)S(1)}, bf16[32,3712]{1,0:T(8,128)(2,1)S(1)}, u32[]{:S(2)}, u32[]{:S(2)}) collective-permute-start(bf16[32,3712]{1,0:T(8,128)(2,1)S(1)} %slice_select_fusion.1), channel_id=1, source_target_pairs={{0,2},{1,3},{2,4},{3,5},{4,6},{5,7},{6,8},{7,9},{8,10},{9,11},{10,... | collective-permute-start | bytes 712712 | tf_op jit(solution)/shard_map/ppermute | solution.py:32
  64.6 5.4 %collective-permute-start.27 = (bf16[32,3712]{1,0:T(8,128)(2,1)S(1)}, bf16[32,3712]{1,0:T(8,128)(2,1)S(1)}, u32[]{:S(2)}, u32[]{:S(2)}) collective-permute-start(bf16[32,3712]{1,0:T(8,128)(2,1)S(1)} %collective-permute-done.26), channel_id=1, source_target_pairs={{0,64},{1,65},{2,66},{3,67},{4,68},{5,69},{6,70},{7,71},{8,72},{9,... | collective-permute-start | bytes 712712 | tf_op jit(solution)/shard_map/ppermute | solution.py:32
  67.3 11.5 %collective-permute-start.25 = (bf16[128,1408]{1,0:T(8,128)(2,1)S(1)}, bf16[128,1408]{1,0:T(8,128)(2,1)S(1)}, u32[]{:S(2)}, u32[]{:S(2)}) collective-permute-start(bf16[128,1408]{1,0:T(8,128)(2,1)S(1)} %get-tuple-element.36), channel_id=1, source_target_pairs={{0,1},{1,0},{2,3},{3,2},{4,5},{5,4},{6,7},{7,6},{8,9},{9,8},{10,11... | collective-permute-start | bytes 1081352 | tf_op jit(solution)/shard_map/ppermute | solution.py:32
  70.0 1.5 %collective-permute-start.28 = (bf16[32,3712]{1,0:T(8,128)(2,1)S(1)}, bf16[32,3712]{1,0:T(8,128)(2,1)S(1)}, u32[]{:S(2)}, u32[]{:S(2)}) collective-permute-start(bf16[32,3712]{1,0:T(8,128)(2,1)S(1)} %collective-permute-done.20), channel_id=1, source_target_pairs={{0,64},{1,65},{2,66},{3,67},{4,68},{5,69},{6,70},{7,71},{8,72},{9,... | collective-permute-start | bytes 712712 | tf_op jit(solution)/shard_map/ppermute | solution.py:32
  74.7 7.6 %collective-permute-start.29 = (bf16[64,1408]{1,0:T(8,128)(2,1)S(1)}, bf16[64,1408]{1,0:T(8,128)(2,1)S(1)}, u32[]{:S(2)}, u32[]{:S(2)}) collective-permute-start(bf16[64,1408]{1,0:T(8,128)(2,1)S(1)} %get-tuple-element.39), channel_id=1, source_target_pairs={{0,1},{1,0},{2,3},{3,2},{4,5},{5,4},{6,7},{7,6},{8,9},{9,8},{10,11... | collective-permute-start | bytes 540680 | tf_op jit(solution)/shard_map/ppermute | solution.py:32
  83.9 4.6 %collective-permute-start.32 = (f32[8,128]{1,0:T(8,128)S(1)}, f32[8,128]{1,0:T(8,128)S(1)}, u32[]{:S(2)}, u32[]{:S(2)}) collective-permute-start(f32[8,128]{1,0:T(8,128)S(1)} %get-tuple-element.46), channel_id=1, source_target_pairs={{0,192},{1,193},{2,194},{3,195},{4,196},{5,197},{6,198},{7,199},{8... | collective-permute-start | bytes 12296 | tf_op jit(solution)/shard_map/ppermute | solution.py:32
  84.8 5.1 %collective-permute-start.31 = (f32[8,128]{1,0:T(8,128)S(1)}, f32[8,128]{1,0:T(8,128)S(1)}, u32[]{:S(2)}, u32[]{:S(2)}) collective-permute-start(f32[8,128]{1,0:T(8,128)S(1)} %get-tuple-element.46), channel_id=1, source_target_pairs={{0,128},{1,129},{2,130},{3,131},{4,132},{5,133},{6,134},{7,135},{8... | collective-permute-start | bytes 12296 | tf_op jit(solution)/shard_map/ppermute | solution.py:32
  86.8 3.1 %collective-permute-start.30 = (f32[8,128]{1,0:T(8,128)S(1)}, f32[8,128]{1,0:T(8,128)S(1)}, u32[]{:S(2)}, u32[]{:S(2)}) collective-permute-start(f32[8,128]{1,0:T(8,128)S(1)} %get-tuple-element.46), channel_id=1, source_target_pairs={{0,64},{1,65},{2,66},{3,67},{4,68},{5,69},{6,70},{7,71},{8,72},{9,... | collective-permute-start | bytes 12296 | tf_op jit(solution)/shard_map/ppermute | solution.py:32

commit v5 on v4

--- a/solution.py
+++ b/solution.py
@@ -177,7 +177,8 @@
 def local(tokens, gain, head):
     yh, core, h = (lax.axis_index(a) for a in ("yh", "core", "h"))
     f32 = tokens.astype(jnp.float32)
-    scaled = (f32 * gain.astype(jnp.float32)).astype(jnp.bfloat16)
+    wide = lax.optimization_barrier(jnp.broadcast_to(gain, tokens.shape))
+    scaled = (f32 * wide.astype(jnp.float32)).astype(jnp.bfloat16)
     squares = jnp.sum(jnp.square(f32), axis=1)
     pieces = jnp.stack(split3(squares), axis=1)
     own = jnp.concatenate([scaled, jnp.pad(pieces, ((0, 0), (3, LANES - 6)))], axis=1)

time: 109 us -> 109 us (level)
  no operation moved by 1% of the time
where the time goes in v5:
time: 109 us
  waiting for transfers between devices  36.6 us (34%)
  starting transfers between devices  31 us (28%)
  blocking collectives  17.1 us (16%)
  Pallas kernels  16 us (15%)
  local copies, waits for them, and re-layouts  4.42 us (4%)
  other arithmetic  3.66 us (3%)
    ppermute x33, waiting for transfers between devices, send(): return lax.ppermute(value, AXES, pairs)  36.6 us
    ppermute x33, starting transfers between devices, send(): return lax.ppermute(value, AXES, pairs)  31 us
    all_to_all x1, blocking collectives, local(): lax.all_to_all(jnp.broadcast_to(stats[None], (NX * NZ, 8, LANES)), ('x',...  17.1 us
    pallas_call x5, Pallas kernels, product(): pl.pallas_call(functools.partial(product_kernel, len(outward)), in_specs=...  14.4 us
    unnamed x4, local copies, waits for them, and re-layouts  3.61 us
  transfers between devices with their start and end apart: 33, of which 20 were waited for; matrix products, arithmetic and copies ran while one was open for 1% of the time, Pallas kernels for 13%

profile of v5, /device:TPU:8, one launch (start us, length us, event | category | flops | bytes accessed | tf_op | source)
XLA Modules:
  0.0 109.0 jit_solution(6088631350055929487)
XLA Ops:
  0.0 0.7 broadcast_in_dim.4
  0.7 1.0 fusion
  1.7 0.1 copy.8
  1.8 0.1 fusion.11
  1.9 0.1 collective-permute-start.1
  2.0 2.4 %collective-permute-start.2 = (bf16[8,3712]{1,0:T(8,128)(2,1)S(1)}, bf16[8,3712]{1,0:T(8,128)(2,1)S(1)}, u32[]{:S(2)}, u32[]{:S(2)}) collective-permute-start(bf16[8,3712]{1,0:T(8,128)(2,1)S(1)} %pad_maximum_fusion.6), channel_id=1, source_target_pairs={{0,192},{1,193},{2,194},{3,195},{4,196},{5,197},{6,198},{7,199},{8... | collective-permute-start | bytes 178184 | tf_op jit(solution)/shard_map/ppermute | solution.py:32
  4.4 1.2 %collective-permute-start = (bf16[8,3712]{1,0:T(8,128)(2,1)S(1)}, bf16[8,3712]{1,0:T(8,128)(2,1)S(1)}, u32[]{:S(2)}, u32[]{:S(2)}) collective-permute-start(bf16[8,3712]{1,0:T(8,128)(2,1)S(1)} %pad_maximum_fusion.6), channel_id=1, source_target_pairs={{0,128},{1,129},{2,130},{3,131},{4,132},{5,133},{6,134},{7,135},{8... | collective-permute-start | bytes 178184 | tf_op jit(solution)/shard_map/ppermute | solution.py:32
  5.6 1.6 %collective-permute-done.2 = bf16[8,3712]{1,0:T(8,128)(2,1)S(1)} collective-permute-done((bf16[8,3712]{1,0:T(8,128)(2,1)S(1)}, bf16[8,3712]{1,0:T(8,128)(2,1)S(1)}, u32[]{:S(2)}, u32[]{:S(2)}) %collective-permute-start.2) | collective-permute-done | bytes 59424 | tf_op jit(solution)/shard_map/ppermute | solution.py:32
  7.3 2.8 %collective-permute-done = bf16[8,3712]{1,0:T(8,128)(2,1)S(1)} collective-permute-done((bf16[8,3712]{1,0:T(8,128)(2,1)S(1)}, bf16[8,3712]{1,0:T(8,128)(2,1)S(1)}, u32[]{:S(2)}, u32[]{:S(2)}) %collective-permute-start) | collective-permute-done | bytes 59424 | tf_op jit(solution)/shard_map/ppermute | solution.py:32
  10.1 0.1 constant_dynamic-update-slice_fusion.3
  10.1 3.1 %collective-permute-start.9 = (bf16[8,3712]{1,0:T(8,128)(2,1)S(1)}, bf16[8,3712]{1,0:T(8,128)(2,1)S(1)}, u32[]{:S(2)}, u32[]{:S(2)}) collective-permute-start(bf16[8,3712]{1,0:T(8,128)(2,1)S(1)} %get-tuple-element.51), channel_id=1, source_target_pairs={{0,32},{1,33},{2,34},{3,35},{4,36},{5,37},{6,38},{7,39},{8,40},{9,... | collective-permute-start | bytes 178184 | tf_op jit(solution)/shard_map/ppermute | solution.py:32
  13.2 0.5 collective-permute-start.4
  13.8 1.6 %collective-permute-start.8 = (bf16[16,3712]{1,0:T(8,128)(2,1)S(1)}, bf16[16,3712]{1,0:T(8,128)(2,1)S(1)}, u32[]{:S(2)}, u32[]{:S(2)}) collective-permute-start(bf16[16,3712]{1,0:T(8,128)(2,1)S(1)} %pad_maximum_fusion.5), channel_id=1, source_target_pairs={{0,16},{1,17},{2,18},{3,19},{4,20},{5,21},{6,22},{7,23},{8,24},{9,... | collective-permute-start | bytes 356360 | tf_op jit(solution)/shard_map/ppermute | solution.py:32
  15.4 1.6 %collective-permute-start.3 = (bf16[16,3712]{1,0:T(8,128)(2,1)S(1)}, bf16[16,3712]{1,0:T(8,128)(2,1)S(1)}, u32[]{:S(2)}, u32[]{:S(2)}) collective-permute-start(bf16[16,3712]{1,0:T(8,128)(2,1)S(1)} %pad_maximum_fusion.4), channel_id=1, source_target_pairs={{0,16},{1,17},{2,18},{3,19},{4,20},{5,21},{6,22},{7,23},{8,24},{9,... | collective-permute-start | bytes 356360 | tf_op jit(solution)/shard_map/ppermute | solution.py:32
  17.0 3.3 %collective-permute-done.8 = bf16[16,3712]{1,0:T(8,128)(2,1)S(1)} collective-permute-done((bf16[16,3712]{1,0:T(8,128)(2,1)S(1)}, bf16[16,3712]{1,0:T(8,128)(2,1)S(1)}, u32[]{:S(2)}, u32[]{:S(2)}) %collective-permute-start.8) | collective-permute-done | bytes 118816 | tf_op jit(solution)/shard_map/ppermute | solution.py:32
  20.2 0.1 collective-permute-start.10
  20.3 1.2 %collective-permute-done.3 = bf16[16,3712]{1,0:T(8,128)(2,1)S(1)} collective-permute-done((bf16[16,3712]{1,0:T(8,128)(2,1)S(1)}, bf16[16,3712]{1,0:T(8,128)(2,1)S(1)}, u32[]{:S(2)}, u32[]{:S(2)}) %collective-permute-start.3) | collective-permute-done | bytes 118816 | tf_op jit(solution)/shard_map/ppermute | solution.py:32
  21.5 0.1 collective-permute-start.5
  21.6 0.1 collective-permute-done.10
  21.9 2.0 %collective-permute-start.11 = (bf16[64,3712]{1,0:T(8,128)(2,1)S(1)}, bf16[64,3712]{1,0:T(8,128)(2,1)S(1)}, u32[]{:S(2)}, u32[]{:S(2)}) collective-permute-start(bf16[64,3712]{1,0:T(8,128)(2,1)S(1)} %select_dynamic-update-slice_fusion.4.refs_0_), channel_id=1, source_target_pairs={{0,2},{1,3},{2,4},{3,5},{4,6},{5,7},{6,8},{7,9},{8,10},{9,11},{10,... | collective-permute-start | bytes 1425416 | tf_op jit(solution)/shard_map/ppermute | solution.py:32
  24.0 2.0 %collective-permute-start.6 = (bf16[64,3712]{1,0:T(8,128)(2,1)S(1)}, bf16[64,3712]{1,0:T(8,128)(2,1)S(1)}, u32[]{:S(2)}, u32[]{:S(2)}) collective-permute-start(bf16[64,3712]{1,0:T(8,128)(2,1)S(1)} %select_dynamic-update-slice_fusion.6.refs_1_), channel_id=1, source_target_pairs={{0,2},{1,3},{2,4},{3,5},{4,6},{5,7},{6,8},{7,9},{8,10},{9,11},{10,... | collective-permute-start | bytes 1425416 | tf_op jit(solution)/shard_map/ppermute | solution.py:32
  26.0 3.6 %copy-done = bf16[1280,3584]{1,0:T(8,128)(2,1)S(1)} copy-done((bf16[1280,3584]{1,0:T(8,128)(2,1)S(1)}, bf16[1280,3584]{1,0:T(8,128)(2,1)}, u32[]{:S(2)}) %copy-start) | copy-done | bytes 9175064
  29.6 3.1 %product.5 = (bf16[64,1408]{1,0:T(8,128)(2,1)S(1)}, f32[64,1408]{1,0:T(8,128)S(1)}) custom-call(bf16[64,3712]{1,0:T(8,128)(2,1)S(1)} %select_dynamic-update-slice_fusion.4.refs_0_, bf16[64,3712]{1,0:T(8,128)(2,1)S(1)} %select_dynamic-update-slice_fusion.6.refs_1_, bf16[1280,3584]{1,0:T(8,128)(2,1)S(1)} %copy-done), custom_call_target="tpu_custom_call" | custom-call | flops 1 | bytes 1 | tf_op jit(solution)/shard_map/product/pallas_call | solution.py:104
  32.7 1.7 %collective-permute-done.11.refs_0_ = bf16[64,3712]{1,0:T(8,128)(2,1)S(1)} collective-permute-done((bf16[64,3712]{1,0:T(8,128)(2,1)S(1)}, bf16[64,3712]{1,0:T(8,128)(2,1)S(1)}, u32[]{:S(2)}, u32[]{:S(2)}) %collective-permute-start.11) | collective-permute-done | bytes 475168 | tf_op jit(solution)/shard_map/ppermute | solution.py:32
  34.4 0.3 collective-permute-start.16
  34.8 4.8 %collective-permute-done.6.refs_2_ = bf16[64,3712]{1,0:T(8,128)(2,1)S(1)} collective-permute-done((bf16[64,3712]{1,0:T(8,128)(2,1)S(1)}, bf16[64,3712]{1,0:T(8,128)(2,1)S(1)}, u32[]{:S(2)}, u32[]{:S(2)}) %collective-permute-start.6) | collective-permute-done | bytes 475168 | tf_op jit(solution)/shard_map/ppermute | solution.py:32
  39.5 0.5 collective-permute-start.12
  40.1 4.6 %collective-permute-done.16.refs_0_ = bf16[64,3712]{1,0:T(8,128)(2,1)S(1)} collective-permute-done((bf16[64,3712]{1,0:T(8,128)(2,1)S(1)}, bf16[64,3712]{1,0:T(8,128)(2,1)S(1)}, u32[]{:S(2)}, u32[]{:S(2)}) %collective-permute-start.16) | collective-permute-done | bytes 475168 | tf_op jit(solution)/shard_map/ppermute | solution.py:32
  44.6 0.0 collective-permute-start.21
  44.6 1.3 %collective-permute-start.14 = (bf16[64,1408]{1,0:T(8,128)(2,1)S(1)}, bf16[64,1408]{1,0:T(8,128)(2,1)S(1)}, u32[]{:S(2)}, u32[]{:S(2)}) collective-permute-start(bf16[64,1408]{1,0:T(8,128)(2,1)S(1)} %get-tuple-element.26), channel_id=1, source_target_pairs={{0,1},{1,0},{2,3},{3,2},{4,5},{5,4},{6,7},{7,6},{8,9},{9,8},{10,11... | collective-permute-start | bytes 540680 | tf_op jit(solution)/shard_map/ppermute | solution.py:32
  46.0 2.7 %product.6 = (bf16[128,1408]{1,0:T(8,128)(2,1)S(1)}, f32[128,1408]{1,0:T(8,128)S(1)}) custom-call(bf16[64,3712]{1,0:T(8,128)(2,1)S(1)} %collective-permute-done.11.refs_0_, bf16[64,3712]{1,0:T(8,128)(2,1)S(1)} %collective-permute-done.12.refs_1_, bf16[64,3712]{1,0:T(8,128)(2,1)S(1)} %collective-permute-done.6.refs_2_, ...), custom_call_target="tpu_custom_call" | custom-call | flops 1 | bytes 1 | tf_op jit(solution)/shard_map/product/pallas_call | solution.py:104
  48.7 0.8 collective-permute-start.19
  49.5 0.4 collective-permute-done.7.refs_2_
  49.9 0.9 collective-permute-done.14.refs_0_
  50.8 1.4 %collective-permute-start.18 = (bf16[64,3712]{1,0:T(8,128)(2,1)S(1)}, bf16[64,3712]{1,0:T(8,128)(2,1)S(1)}, u32[]{:S(2)}, u32[]{:S(2)}) collective-permute-start(bf16[64,3712]{1,0:T(8,128)(2,1)S(1)} %collective-permute-done.7.refs_2_), channel_id=1, source_target_pairs={{0,64},{1,65},{2,66},{3,67},{4,68},{5,69},{6,70},{7,71},{8,72},{9,... | collective-permute-start | bytes 1425416 | tf_op jit(solution)/shard_map/ppermute | solution.py:32
  52.2 1.6 %collective-permute-start.17 = (bf16[64,3712]{1,0:T(8,128)(2,1)S(1)}, bf16[64,3712]{1,0:T(8,128)(2,1)S(1)}, u32[]{:S(2)}, u32[]{:S(2)}) collective-permute-start(bf16[64,3712]{1,0:T(8,128)(2,1)S(1)} %collective-permute-done.16.refs_0_), channel_id=1, source_target_pairs={{0,64},{1,65},{2,66},{3,67},{4,68},{5,69},{6,70},{7,71},{8,72},{9,... | collective-permute-start | bytes 1425416 | tf_op jit(solution)/shard_map/ppermute | solution.py:32
  53.8 1.2 %collective-permute-done.21.refs_0_ = bf16[64,3712]{1,0:T(8,128)(2,1)S(1)} collective-permute-done((bf16[64,3712]{1,0:T(8,128)(2,1)S(1)}, bf16[64,3712]{1,0:T(8,128)(2,1)S(1)}, u32[]{:S(2)}, u32[]{:S(2)}) %collective-permute-start.21) | collective-permute-done | bytes 475168 | tf_op jit(solution)/shard_map/ppermute | solution.py:32
  55.0 0.1 collective-permute-start.26
  55.1 0.1 collective-permute-done.17.refs_1_
  55.3 2.7 %product.7 = (bf16[128,1408]{1,0:T(8,128)(2,1)S(1)}, f32[128,1408]{1,0:T(8,128)S(1)}) custom-call(bf16[64,3712]{1,0:T(8,128)(2,1)S(1)} %collective-permute-done.16.refs_0_, bf16[64,3712]{1,0:T(8,128)(2,1)S(1)} %collective-permute-done.17.refs_1_, bf16[64,3712]{1,0:T(8,128)(2,1)S(1)} %collective-permute-done.7.refs_2_, ...), custom_call_target="tpu_custom_call" | custom-call | flops 1 | bytes 1 | tf_op jit(solution)/shard_map/product/pallas_call | solution.py:104
  58.0 2.0 %collective-permute-start.24 = (bf16[128,1408]{1,0:T(8,128)(2,1)S(1)}, bf16[128,1408]{1,0:T(8,128)(2,1)S(1)}, u32[]{:S(2)}, u32[]{:S(2)}) collective-permute-start(bf16[128,1408]{1,0:T(8,128)(2,1)S(1)} %get-tuple-element.32), channel_id=1, source_target_pairs={{0,1},{1,0},{2,3},{3,2},{4,5},{5,4},{6,7},{7,6},{8,9},{9,8},{10,11... | collective-permute-start | bytes 1081352 | tf_op jit(solution)/shard_map/ppermute | solution.py:32
  60.0 2.0 %collective-permute-done.15.refs_2_ = bf16[64,3712]{1,0:T(8,128)(2,1)S(1)} collective-permute-done((bf16[64,3712]{1,0:T(8,128)(2,1)S(1)}, bf16[64,3712]{1,0:T(8,128)(2,1)S(1)}, u32[]{:S(2)}, u32[]{:S(2)}) %collective-permute-start.15) | collective-permute-done | bytes 475168 | tf_op jit(solution)/shard_map/ppermute | solution.py:32
  62.0 0.5 collective-permute-start.22
  62.6 0.7 collective-permute-start.20
  63.3 1.3 %collective-permute-done.26 = bf16[32,3712]{1,0:T(8,128)(2,1)S(1)} collective-permute-done((bf16[32,3712]{1,0:T(8,128)(2,1)S(1)}, bf16[32,3712]{1,0:T(8,128)(2,1)S(1)}, u32[]{:S(2)}, u32[]{:S(2)}) %collective-permute-start.26) | collective-permute-done | bytes 237600 | tf_op jit(solution)/shard_map/ppermute | solution.py:32
  64.6 2.7 %product.8 = (bf16[128,1408]{1,0:T(8,128)(2,1)S(1)}, f32[128,1408]{1,0:T(8,128)S(1)}) custom-call(bf16[64,3712]{1,0:T(8,128)(2,1)S(1)} %collective-permute-done.21.refs_0_, bf16[64,3712]{1,0:T(8,128)(2,1)S(1)} %collective-permute-done.22.refs_1_, bf16[64,3712]{1,0:T(8,128)(2,1)S(1)} %collective-permute-done.15.refs_2_, ...), custom_call_target="tpu_custom_call" | custom-call | flops 1 | bytes 1 | tf_op jit(solution)/shard_map/product/pallas_call | solution.py:104
  67.3 1.9 %collective-permute-start.25 = (bf16[128,1408]{1,0:T(8,128)(2,1)S(1)}, bf16[128,1408]{1,0:T(8,128)(2,1)S(1)}, u32[]{:S(2)}, u32[]{:S(2)}) collective-permute-start(bf16[128,1408]{1,0:T(8,128)(2,1)S(1)} %get-tuple-element.36), channel_id=1, source_target_pairs={{0,1},{1,0},{2,3},{3,2},{4,5},{5,4},{6,7},{7,6},{8,9},{9,8},{10,11... | collective-permute-start | bytes 1081352 | tf_op jit(solution)/shard_map/ppermute | solution.py:32
  69.3 0.7 collective-permute-done.20
  70.0 0.1 broadcast_select_fusion.3
  70.1 1.4 %collective-permute-done.28 = bf16[32,3712]{1,0:T(8,128)(2,1)S(1)} collective-permute-done((bf16[32,3712]{1,0:T(8,128)(2,1)S(1)}, bf16[32,3712]{1,0:T(8,128)(2,1)S(1)}, u32[]{:S(2)}, u32[]{:S(2)}) %collective-permute-start.28) | collective-permute-done | bytes 237600 | tf_op jit(solution)/shard_map/ppermute | solution.py:32
  71.5 0.1 pad_maximum_fusion
  71.6 3.1 %product.9 = (bf16[64,1408]{1,0:T(8,128)(2,1)S(1)}, f32[64,1408]{1,0:T(8,128)S(1)}) custom-call(bf16[64,3712]{1,0:T(8,128)(2,1)S(1)} %get-tuple-element.71.refs_0_, bf16[64,3712]{1,0:T(8,128)(2,1)S(1)} %get-tuple-element.72.refs_1_, bf16[1280,3584]{1,0:T(8,128)(2,1)S(1)} %copy-done.1), custom_call_target="tpu_custom_call" | custom-call | flops 1 | bytes 1 | tf_op jit(solution)/shard_map/product/pallas_call | solution.py:104
  74.7 1.7 %collective-permute-start.29 = (bf16[64,1408]{1,0:T(8,128)(2,1)S(1)}, bf16[64,1408]{1,0:T(8,128)(2,1)S(1)}, u32[]{:S(2)}, u32[]{:S(2)}) collective-permute-start(bf16[64,1408]{1,0:T(8,128)(2,1)S(1)} %get-tuple-element.39), channel_id=1, source_target_pairs={{0,1},{1,0},{2,3},{3,2},{4,5},{5,4},{6,7},{7,6},{8,9},{9,8},{10,11... | collective-permute-start | bytes 540680 | tf_op jit(solution)/shard_map/ppermute | solution.py:32
  76.5 2.4 %collective-permute-done.25.refs_3_ = bf16[128,1408]{1,0:T(8,128)(2,1)S(1)} collective-permute-done((bf16[128,1408]{1,0:T(8,128)(2,1)S(1)}, bf16[128,1408]{1,0:T(8,128)(2,1)S(1)}, u32[]{:S(2)}, u32[]{:S(2)}) %collective-permute-start.25) | collective-permute-done | bytes 360480 | tf_op jit(solution)/shard_map/ppermute | solution.py:32
  78.9 3.5 %collective-permute-done.29.refs_4_ = bf16[64,1408]{1,0:T(8,128)(2,1)S(1)} collective-permute-done((bf16[64,1408]{1,0:T(8,128)(2,1)S(1)}, bf16[64,1408]{1,0:T(8,128)(2,1)S(1)}, u32[]{:S(2)}, u32[]{:S(2)}) %collective-permute-start.29) | collective-permute-done | bytes 180256 | tf_op jit(solution)/shard_map/ppermute | solution.py:32
  82.3 1.5 %join.1 = (f32[512,1280]{1,0:T(8,128)S(1)}, f32[8,128]{1,0:T(8,128)S(1)}) custom-call(bf16[64,1408]{1,0:T(8,128)(2,1)S(1)} %collective-permute-done.14.refs_0_, bf16[128,1408]{1,0:T(8,128)(2,1)S(1)} %collective-permute-done.19.refs_1_, bf16[128,1408]{1,0:T(8,128)(2,1)S(1)} %collective-permute-done.24.refs_2_, ...), custom_call_target="tpu_custom_call" | custom-call | tf_op jit(solution)/shard_map/join/pallas_call | solution.py:163
  83.9 0.9 collective-permute-start.32
  84.8 2.0 %collective-permute-start.31 = (f32[8,128]{1,0:T(8,128)S(1)}, f32[8,128]{1,0:T(8,128)S(1)}, u32[]{:S(2)}, u32[]{:S(2)}) collective-permute-start(f32[8,128]{1,0:T(8,128)S(1)} %get-tuple-element.46), channel_id=1, source_target_pairs={{0,128},{1,129},{2,130},{3,131},{4,132},{5,133},{6,134},{7,135},{8... | collective-permute-start | bytes 12296 | tf_op jit(solution)/shard_map/ppermute | solution.py:32
  86.8 0.5 collective-permute-start.30
  87.3 1.2 %collective-permute-done.32 = f32[8,128]{1,0:T(8,128)S(1)} collective-permute-done((f32[8,128]{1,0:T(8,128)S(1)}, f32[8,128]{1,0:T(8,128)S(1)}, u32[]{:S(2)}, u32[]{:S(2)}) %collective-permute-start.32) | collective-permute-done | bytes 4128 | tf_op jit(solution)/shard_map/ppermute | solution.py:32
  88.5 1.4 %collective-permute-done.31 = f32[8,128]{1,0:T(8,128)S(1)} collective-permute-done((f32[8,128]{1,0:T(8,128)S(1)}, f32[8,128]{1,0:T(8,128)S(1)}, u32[]{:S(2)}, u32[]{:S(2)}) %collective-permute-start.31) | collective-permute-done | bytes 4128 | tf_op jit(solution)/shard_map/ppermute | solution.py:32
  90.0 17.1 %all_to_all.5 = f32[32,8,128]{2,1,0:T(8,128)S(1)} all-to-all(f32[32,8,128]{2,1,0:T(8,128)S(1)} %broadcast_in_dim.5), channel_id=1, replica_groups=mesh['yh'=2,'core'=2,'x'=4,'z'=8,'h'=2] {'x','z'}, dimensions={0} | all-to-all | bytes 262144 | tf_op jit(solution)/shard_map/all_to_all | solution.py:250
  107.1 0.1 fusion.2
  107.2 1.8 %subtract_subtract_fusion = f32[512,1280]{1,0:T(8,128)} fusion(f32[512,1280]{1,0:T(8,128)S(1)} %get-tuple-element.45, f32[512]{0:T(512)S(1)} %log_bitcast_fusion, f32[512]{0:T(512)S(1)} %bitcast.9), kind=kLoop, calls=%fused_computation | loop fusion | flops 1310720 | bytes 5246976 | tf_op jit(solution)/shard_map/sub | solution.py:253
  (47 shorter events, 0.7 us)
Async XLA Ops:
  1.9 3.8 %collective-permute-start.1 = (bf16[8,3712]{1,0:T(8,128)(2,1)S(1)}, bf16[8,3712]{1,0:T(8,128)(2,1)S(1)}, u32[]{:S(2)}, u32[]{:S(2)}) collective-permute-start(bf16[8,3712]{1,0:T(8,128)(2,1)S(1)} %pad_maximum_fusion.6), channel_id=1, source_target_pairs={{0,64},{1,65},{2,66},{3,67},{4,68},{5,69},{6,70},{7,71},{8,72},{9,... | collective-permute-start | bytes 178184 | tf_op jit(solution)/shard_map/ppermute | solution.py:32
  2.0 5.3 %collective-permute-start.2 = (bf16[8,3712]{1,0:T(8,128)(2,1)S(1)}, bf16[8,3712]{1,0:T(8,128)(2,1)S(1)}, u32[]{:S(2)}, u32[]{:S(2)}) collective-permute-start(bf16[8,3712]{1,0:T(8,128)(2,1)S(1)} %pad_maximum_fusion.6), channel_id=1, source_target_pairs={{0,192},{1,193},{2,194},{3,195},{4,196},{5,197},{6,198},{7,199},{8... | collective-permute-start | bytes 178184 | tf_op jit(solution)/shard_map/ppermute | solution.py:32
  4.4 5.7 %collective-permute-start = (bf16[8,3712]{1,0:T(8,128)(2,1)S(1)}, bf16[8,3712]{1,0:T(8,128)(2,1)S(1)}, u32[]{:S(2)}, u32[]{:S(2)}) collective-permute-start(bf16[8,3712]{1,0:T(8,128)(2,1)S(1)} %pad_maximum_fusion.6), channel_id=1, source_target_pairs={{0,128},{1,129},{2,130},{3,131},{4,132},{5,133},{6,134},{7,135},{8... | collective-permute-start | bytes 178184 | tf_op jit(solution)/shard_map/ppermute | solution.py:32
  10.1 6.8 %collective-permute-start.9 = (bf16[8,3712]{1,0:T(8,128)(2,1)S(1)}, bf16[8,3712]{1,0:T(8,128)(2,1)S(1)}, u32[]{:S(2)}, u32[]{:S(2)}) collective-permute-start(bf16[8,3712]{1,0:T(8,128)(2,1)S(1)} %get-tuple-element.51), channel_id=1, source_target_pairs={{0,32},{1,33},{2,34},{3,35},{4,36},{5,37},{6,38},{7,39},{8,40},{9,... | collective-permute-start | bytes 178184 | tf_op jit(solution)/shard_map/ppermute | solution.py:32
  13.2 7.1 %collective-permute-start.4 = (bf16[8,3712]{1,0:T(8,128)(2,1)S(1)}, bf16[8,3712]{1,0:T(8,128)(2,1)S(1)}, u32[]{:S(2)}, u32[]{:S(2)}) collective-permute-start(bf16[8,3712]{1,0:T(8,128)(2,1)S(1)} %get-tuple-element.63), channel_id=1, source_target_pairs={{0,32},{1,33},{2,34},{3,35},{4,36},{5,37},{6,38},{7,39},{8,40},{9,... | collective-permute-start | bytes 178184 | tf_op jit(solution)/shard_map/ppermute | solution.py:32
  13.8 6.4 %collective-permute-start.8 = (bf16[16,3712]{1,0:T(8,128)(2,1)S(1)}, bf16[16,3712]{1,0:T(8,128)(2,1)S(1)}, u32[]{:S(2)}, u32[]{:S(2)}) collective-permute-start(bf16[16,3712]{1,0:T(8,128)(2,1)S(1)} %pad_maximum_fusion.5), channel_id=1, source_target_pairs={{0,16},{1,17},{2,18},{3,19},{4,20},{5,21},{6,22},{7,23},{8,24},{9,... | collective-permute-start | bytes 356360 | tf_op jit(solution)/shard_map/ppermute | solution.py:32
  15.4 6.1 %collective-permute-start.3 = (bf16[16,3712]{1,0:T(8,128)(2,1)S(1)}, bf16[16,3712]{1,0:T(8,128)(2,1)S(1)}, u32[]{:S(2)}, u32[]{:S(2)}) collective-permute-start(bf16[16,3712]{1,0:T(8,128)(2,1)S(1)} %pad_maximum_fusion.4), channel_id=1, source_target_pairs={{0,16},{1,17},{2,18},{3,19},{4,20},{5,21},{6,22},{7,23},{8,24},{9,... | collective-permute-start | bytes 356360 | tf_op jit(solution)/shard_map/ppermute | solution.py:32
  20.2 1.5 %collective-permute-start.10 = (bf16[24,3712]{1,0:T(8,128)(2,1)S(1)}, bf16[24,3712]{1,0:T(8,128)(2,1)S(1)}, u32[]{:S(2)}, u32[]{:S(2)}) collective-permute-start(bf16[24,3712]{1,0:T(8,128)(2,1)S(1)} %pad_maximum_fusion.3), channel_id=1, source_target_pairs={{0,64},{1,65},{2,66},{3,67},{4,68},{5,69},{6,70},{7,71},{8,72},{9,... | collective-permute-start | bytes 534536 | tf_op jit(solution)/shard_map/ppermute | solution.py:32
  21.5 2.3 %collective-permute-start.5 = (bf16[24,3712]{1,0:T(8,128)(2,1)S(1)}, bf16[24,3712]{1,0:T(8,128)(2,1)S(1)}, u32[]{:S(2)}, u32[]{:S(2)}) collective-permute-start(bf16[24,3712]{1,0:T(8,128)(2,1)S(1)} %pad_maximum_fusion.2), channel_id=1, source_target_pairs={{0,64},{1,65},{2,66},{3,67},{4,68},{5,69},{6,70},{7,71},{8,72},{9,... | collective-permute-start | bytes 534536 | tf_op jit(solution)/shard_map/ppermute | solution.py:32
  21.9 12.6 %collective-permute-start.11 = (bf16[64,3712]{1,0:T(8,128)(2,1)S(1)}, bf16[64,3712]{1,0:T(8,128)(2,1)S(1)}, u32[]{:S(2)}, u32[]{:S(2)}) collective-permute-start(bf16[64,3712]{1,0:T(8,128)(2,1)S(1)} %select_dynamic-update-slice_fusion.4.refs_0_), channel_id=1, source_target_pairs={{0,2},{1,3},{2,4},{3,5},{4,6},{5,7},{6,8},{7,9},{8,10},{9,11},{10,... | collective-permute-start | bytes 1425416 | tf_op jit(solution)/shard_map/ppermute | solution.py:32
  24.0 15.5 %collective-permute-start.6 = (bf16[64,3712]{1,0:T(8,128)(2,1)S(1)}, bf16[64,3712]{1,0:T(8,128)(2,1)S(1)}, u32[]{:S(2)}, u32[]{:S(2)}) collective-permute-start(bf16[64,3712]{1,0:T(8,128)(2,1)S(1)} %select_dynamic-update-slice_fusion.6.refs_1_), channel_id=1, source_target_pairs={{0,2},{1,3},{2,4},{3,5},{4,6},{5,7},{6,8},{7,9},{8,10},{9,11},{10,... | collective-permute-start | bytes 1425416 | tf_op jit(solution)/shard_map/ppermute | solution.py:32
  26.0 3.6 %copy-start = (bf16[1280,3584]{1,0:T(8,128)(2,1)S(1)}, bf16[1280,3584]{1,0:T(8,128)(2,1)}, u32[]{:S(2)}) copy-start(bf16[1280,3584]{1,0:T(8,128)(2,1)} %refs_2_.3) | copy-start | bytes 27525124
  29.6 16.4 %copy-start.1 = (bf16[1280,3584]{1,0:T(8,128)(2,1)S(1)}, bf16[1280,3584]{1,0:T(8,128)(2,1)}, u32[]{:S(2)}) copy-start(bf16[1280,3584]{1,0:T(8,128)(2,1)} %refs_2_.3) | copy-start | bytes 27525124
  34.4 10.2 %collective-permute-start.16 = (bf16[64,3712]{1,0:T(8,128)(2,1)S(1)}, bf16[64,3712]{1,0:T(8,128)(2,1)S(1)}, u32[]{:S(2)}, u32[]{:S(2)}) collective-permute-start(bf16[64,3712]{1,0:T(8,128)(2,1)S(1)} %collective-permute-done.11.refs_0_), channel_id=1, source_target_pairs={{0,2},{1,3},{2,4},{3,5},{4,6},{5,7},{6,8},{7,9},{8,10},{9,11},{10,... | collective-permute-start | bytes 1425416 | tf_op jit(solution)/shard_map/ppermute | solution.py:32
  39.5 6.4 %collective-permute-start.13 = (bf16[64,3712]{1,0:T(8,128)(2,1)S(1)}, bf16[64,3712]{1,0:T(8,128)(2,1)S(1)}, u32[]{:S(2)}, u32[]{:S(2)}) collective-permute-start(bf16[64,3712]{1,0:T(8,128)(2,1)S(1)} %collective-permute-done.6.refs_2_), channel_id=1, source_target_pairs={{0,64},{1,65},{2,66},{3,67},{4,68},{5,69},{6,70},{7,71},{8,72},{9,... | collective-permute-start | bytes 1425416 | tf_op jit(solution)/shard_map/ppermute | solution.py:32
  39.5 6.4 %collective-permute-start.12 = (bf16[64,3712]{1,0:T(8,128)(2,1)S(1)}, bf16[64,3712]{1,0:T(8,128)(2,1)S(1)}, u32[]{:S(2)}, u32[]{:S(2)}) collective-permute-start(bf16[64,3712]{1,0:T(8,128)(2,1)S(1)} %collective-permute-done.11.refs_0_), channel_id=1, source_target_pairs={{0,64},{1,65},{2,66},{3,67},{4,68},{5,69},{6,70},{7,71},{8,72},{9,... | collective-permute-start | bytes 1425416 | tf_op jit(solution)/shard_map/ppermute | solution.py:32
  40.0 9.9 %collective-permute-start.7 = (bf16[64,3712]{1,0:T(8,128)(2,1)S(1)}, bf16[64,3712]{1,0:T(8,128)(2,1)S(1)}, u32[]{:S(2)}, u32[]{:S(2)}) collective-permute-start(bf16[64,3712]{1,0:T(8,128)(2,1)S(1)} %collective-permute-done.6.refs_2_), channel_id=1, source_target_pairs={{0,2},{1,3},{2,4},{3,5},{4,6},{5,7},{6,8},{7,9},{8,10},{9,11},{10,... | collective-permute-start | bytes 1425416 | tf_op jit(solution)/shard_map/ppermute | solution.py:32
  44.6 10.4 %collective-permute-start.21 = (bf16[64,3712]{1,0:T(8,128)(2,1)S(1)}, bf16[64,3712]{1,0:T(8,128)(2,1)S(1)}, u32[]{:S(2)}, u32[]{:S(2)}) collective-permute-start(bf16[64,3712]{1,0:T(8,128)(2,1)S(1)} %collective-permute-done.16.refs_0_), channel_id=1, source_target_pairs={{0,2},{1,3},{2,4},{3,5},{4,6},{5,7},{6,8},{7,9},{8,10},{9,11},{10,... | collective-permute-start | bytes 1425416 | tf_op jit(solution)/shard_map/ppermute | solution.py:32
  44.6 6.2 %collective-permute-start.14 = (bf16[64,1408]{1,0:T(8,128)(2,1)S(1)}, bf16[64,1408]{1,0:T(8,128)(2,1)S(1)}, u32[]{:S(2)}, u32[]{:S(2)}) collective-permute-start(bf16[64,1408]{1,0:T(8,128)(2,1)S(1)} %get-tuple-element.26), channel_id=1, source_target_pairs={{0,1},{1,0},{2,3},{3,2},{4,5},{5,4},{6,7},{7,6},{8,9},{9,8},{10,11... | collective-permute-start | bytes 540680 | tf_op jit(solution)/shard_map/ppermute | solution.py:32
  48.7 13.3 %collective-permute-start.19 = (bf16[128,1408]{1,0:T(8,128)(2,1)S(1)}, bf16[128,1408]{1,0:T(8,128)(2,1)S(1)}, u32[]{:S(2)}, u32[]{:S(2)}) collective-permute-start(bf16[128,1408]{1,0:T(8,128)(2,1)S(1)} %get-tuple-element.28), channel_id=1, source_target_pairs={{0,1},{1,0},{2,3},{3,2},{4,5},{5,4},{6,7},{7,6},{8,9},{9,8},{10,11... | collective-permute-start | bytes 1081352 | tf_op jit(solution)/shard_map/ppermute | solution.py:32
  50.8 4.5 %collective-permute-start.18 = (bf16[64,3712]{1,0:T(8,128)(2,1)S(1)}, bf16[64,3712]{1,0:T(8,128)(2,1)S(1)}, u32[]{:S(2)}, u32[]{:S(2)}) collective-permute-start(bf16[64,3712]{1,0:T(8,128)(2,1)S(1)} %collective-permute-done.7.refs_2_), channel_id=1, source_target_pairs={{0,64},{1,65},{2,66},{3,67},{4,68},{5,69},{6,70},{7,71},{8,72},{9,... | collective-permute-start | bytes 1425416 | tf_op jit(solution)/shard_map/ppermute | solution.py:32
  52.2 9.9 %collective-permute-start.15 = (bf16[64,3712]{1,0:T(8,128)(2,1)S(1)}, bf16[64,3712]{1,0:T(8,128)(2,1)S(1)}, u32[]{:S(2)}, u32[]{:S(2)}) collective-permute-start(bf16[64,3712]{1,0:T(8,128)(2,1)S(1)} %collective-permute-done.7.refs_2_), channel_id=1, source_target_pairs={{0,2},{1,3},{2,4},{3,5},{4,6},{5,7},{6,8},{7,9},{8,10},{9,11},{10,... | collective-permute-start | bytes 1425416 | tf_op jit(solution)/shard_map/ppermute | solution.py:32
  52.2 3.1 %collective-permute-start.17 = (bf16[64,3712]{1,0:T(8,128)(2,1)S(1)}, bf16[64,3712]{1,0:T(8,128)(2,1)S(1)}, u32[]{:S(2)}, u32[]{:S(2)}) collective-permute-start(bf16[64,3712]{1,0:T(8,128)(2,1)S(1)} %collective-permute-done.16.refs_0_), channel_id=1, source_target_pairs={{0,64},{1,65},{2,66},{3,67},{4,68},{5,69},{6,70},{7,71},{8,72},{9,... | collective-permute-start | bytes 1425416 | tf_op jit(solution)/shard_map/ppermute | solution.py:32
  55.0 9.5 %collective-permute-start.26 = (bf16[32,3712]{1,0:T(8,128)(2,1)S(1)}, bf16[32,3712]{1,0:T(8,128)(2,1)S(1)}, u32[]{:S(2)}, u32[]{:S(2)}) collective-permute-start(bf16[32,3712]{1,0:T(8,128)(2,1)S(1)} %slice_select_fusion), channel_id=1, source_target_pairs={{0,2},{1,3},{2,4},{3,5},{4,6},{5,7},{6,8},{7,9},{8,10},{9,11},{10,... | collective-permute-start | bytes 712712 | tf_op jit(solution)/shard_map/ppermute | solution.py:32
  58.0 12.0 %collective-permute-start.24 = (bf16[128,1408]{1,0:T(8,128)(2,1)S(1)}, bf16[128,1408]{1,0:T(8,128)(2,1)S(1)}, u32[]{:S(2)}, u32[]{:S(2)}) collective-permute-start(bf16[128,1408]{1,0:T(8,128)(2,1)S(1)} %get-tuple-element.32), channel_id=1, source_target_pairs={{0,1},{1,0},{2,3},{3,2},{4,5},{5,4},{6,7},{7,6},{8,9},{9,8},{10,11... | collective-permute-start | bytes 1081352 | tf_op jit(solution)/shard_map/ppermute | solution.py:32
  62.0 2.6 %collective-permute-start.23 = (bf16[64,3712]{1,0:T(8,128)(2,1)S(1)}, bf16[64,3712]{1,0:T(8,128)(2,1)S(1)}, u32[]{:S(2)}, u32[]{:S(2)}) collective-permute-start(bf16[64,3712]{1,0:T(8,128)(2,1)S(1)} %collective-permute-done.15.refs_2_), channel_id=1, source_target_pairs={{0,64},{1,65},{2,66},{3,67},{4,68},{5,69},{6,70},{7,71},{8,72},{9,... | collective-permute-start | bytes 1425416 | tf_op jit(solution)/shard_map/ppermute | solution.py:32
  62.0 2.5 %collective-permute-start.22 = (bf16[64,3712]{1,0:T(8,128)(2,1)S(1)}, bf16[64,3712]{1,0:T(8,128)(2,1)S(1)}, u32[]{:S(2)}, u32[]{:S(2)}) collective-permute-start(bf16[64,3712]{1,0:T(8,128)(2,1)S(1)} %collective-permute-done.21.refs_0_), channel_id=1, source_target_pairs={{0,64},{1,65},{2,66},{3,67},{4,68},{5,69},{6,70},{7,71},{8,72},{9,... | collective-permute-start | bytes 1425416 | tf_op jit(solution)/shard_map/ppermute | solution.py:32
  62.6 7.4 %collective-permute-start.20 = (bf16[32,3712]{1,0:T(8,128)(2,1)S(1)}, bf16[32,3712]{1,0:T(8,128)(2,1)S(1)}, u32[]{:S(2)}, u32[]{:S(2)}) collective-permute-start(bf16[32,3712]{1,0:T(8,128)(2,1)S(1)} %slice_select_fusion.1), channel_id=1, source_target_pairs={{0,2},{1,3},{2,4},{3,5},{4,6},{5,7},{6,8},{7,9},{8,10},{9,11},{10,... | collective-permute-start | bytes 712712 | tf_op jit(solution)/shard_map/ppermute | solution.py:32
  64.6 5.4 %collective-permute-start.27 = (bf16[32,3712]{1,0:T(8,128)(2,1)S(1)}, bf16[32,3712]{1,0:T(8,128)(2,1)S(1)}, u32[]{:S(2)}, u32[]{:S(2)}) collective-permute-start(bf16[32,3712]{1,0:T(8,128)(2,1)S(1)} %collective-permute-done.26), channel_id=1, source_target_pairs={{0,64},{1,65},{2,66},{3,67},{4,68},{5,69},{6,70},{7,71},{8,72},{9,... | collective-permute-start | bytes 712712 | tf_op jit(solution)/shard_map/ppermute | solution.py:32
  67.3 11.5 %collective-permute-start.25 = (bf16[128,1408]{1,0:T(8,128)(2,1)S(1)}, bf16[128,1408]{1,0:T(8,128)(2,1)S(1)}, u32[]{:S(2)}, u32[]{:S(2)}) collective-permute-start(bf16[128,1408]{1,0:T(8,128)(2,1)S(1)} %get-tuple-element.36), channel_id=1, source_target_pairs={{0,1},{1,0},{2,3},{3,2},{4,5},{5,4},{6,7},{7,6},{8,9},{9,8},{10,11... | collective-permute-start | bytes 1081352 | tf_op jit(solution)/shard_map/ppermute | solution.py:32
  70.0 1.5 %collective-permute-start.28 = (bf16[32,3712]{1,0:T(8,128)(2,1)S(1)}, bf16[32,3712]{1,0:T(8,128)(2,1)S(1)}, u32[]{:S(2)}, u32[]{:S(2)}) collective-permute-start(bf16[32,3712]{1,0:T(8,128)(2,1)S(1)} %collective-permute-done.20), channel_id=1, source_target_pairs={{0,64},{1,65},{2,66},{3,67},{4,68},{5,69},{6,70},{7,71},{8,72},{9,... | collective-permute-start | bytes 712712 | tf_op jit(solution)/shard_map/ppermute | solution.py:32
  74.7 7.6 %collective-permute-start.29 = (bf16[64,1408]{1,0:T(8,128)(2,1)S(1)}, bf16[64,1408]{1,0:T(8,128)(2,1)S(1)}, u32[]{:S(2)}, u32[]{:S(2)}) collective-permute-start(bf16[64,1408]{1,0:T(8,128)(2,1)S(1)} %get-tuple-element.39), channel_id=1, source_target_pairs={{0,1},{1,0},{2,3},{3,2},{4,5},{5,4},{6,7},{7,6},{8,9},{9,8},{10,11... | collective-permute-start | bytes 540680 | tf_op jit(solution)/shard_map/ppermute | solution.py:32
  83.9 4.6 %collective-permute-start.32 = (f32[8,128]{1,0:T(8,128)S(1)}, f32[8,128]{1,0:T(8,128)S(1)}, u32[]{:S(2)}, u32[]{:S(2)}) collective-permute-start(f32[8,128]{1,0:T(8,128)S(1)} %get-tuple-element.46), channel_id=1, source_target_pairs={{0,192},{1,193},{2,194},{3,195},{4,196},{5,197},{6,198},{7,199},{8... | collective-permute-start | bytes 12296 | tf_op jit(solution)/shard_map/ppermute | solution.py:32
  84.8 5.1 %collective-permute-start.31 = (f32[8,128]{1,0:T(8,128)S(1)}, f32[8,128]{1,0:T(8,128)S(1)}, u32[]{:S(2)}, u32[]{:S(2)}) collective-permute-start(f32[8,128]{1,0:T(8,128)S(1)} %get-tuple-element.46), channel_id=1, source_target_pairs={{0,128},{1,129},{2,130},{3,131},{4,132},{5,133},{6,134},{7,135},{8... | collective-permute-start | bytes 12296 | tf_op jit(solution)/shard_map/ppermute | solution.py:32
  86.8 3.1 %collective-permute-start.30 = (f32[8,128]{1,0:T(8,128)S(1)}, f32[8,128]{1,0:T(8,128)S(1)}, u32[]{:S(2)}, u32[]{:S(2)}) collective-permute-start(f32[8,128]{1,0:T(8,128)S(1)} %get-tuple-element.46), channel_id=1, source_target_pairs={{0,64},{1,65},{2,66},{3,67},{4,68},{5,69},{6,70},{7,71},{8,72},{9,... | collective-permute-start | bytes 12296 | tf_op jit(solution)/shard_map/ppermute | solution.py:32
